TPU v7x, 32 devices: a whole 2x2x4 slice. The times are simulated.
32 devices in a mesh: gx: 4 (over y, x), gy: 8 (over z, core).
Axes of the slice: x: 2, y: 2, z: 4, core: 2. Of those that a mesh axis runs over, the one named last changes fastest.
Arguments:
- velocity: float32 [3, 32, 256, 128], P(None, 'gx', 'gy'), may hold values from -6 to 6
- stress: float32 [6, 32, 256, 128], P(None, 'gx', 'gy'), may hold values from -6 to 6
- density: float32 [32, 256, 128], P('gx', 'gy'), may hold values from 1 to 3
- lame_lambda: float32 [32, 256, 128], P('gx', 'gy'), may hold values from 0.2 to 1
- lame_mu: float32 [32, 256, 128], P('gx', 'gy'), may hold values from 0.1 to 1
Outputs:
- new_velocity: float32 [3, 32, 256, 128], P(None, 'gx', 'gy')
- new_stress: float32 [6, 32, 256, 128], P(None, 'gx', 'gy')
All inputs are finite; a program needn't handle non-finite values.
Results may differ from a plain program's by a relative error of at most 0.00002.
Values sent between devices are 32-bit elements; how exact they have to be, the bound alone decides.
No kernel may reach another device: no remote copies, remote signals or barrier semaphores. Data moves between devices by JAX's collectives and lax.ppermute only.
A program may use at most 64 MiB of HBM per device.

v0:
```python
import jax
import jax.numpy as jnp
from jax import lax
from jax.sharding import PartitionSpec as P

first_coef = 9.0 / 8.0
second_coef = -1.0 / 24.0
time_step = 0.25


def from_behind(block, axis, distance):
    devices = range(lax.axis_size(axis))
    route = [(i - distance, i) for i in devices if i - distance in devices]
    return lax.ppermute(block, axis, route)


def padded_2(block, sides, width):
    for axis, dim in sides:
        count = lax.axis_size(axis)
        forward = [(i, i + 1) for i in range(count - 1)]
        backward = [(target, source) for source, target in forward]
        low = lax.ppermute(
            lax.slice_in_dim(block, block.shape[dim] - width, None, axis=dim), axis, forward
        )
        high = lax.ppermute(lax.slice_in_dim(block, 0, width, axis=dim), axis, backward)
        block = jnp.concatenate([low, block, high], axis=dim)
    return block


def take(field, axis, start):
    count = field.shape[axis] - 4
    index = []
    for dim in range(3):
        if dim == axis:
            index.append(slice(start, start + count))
        else:
            index.append(slice(2, field.shape[dim] - 2))
    return field[tuple(index)]


def forward(field, axis):
    return first_coef * (take(field, axis, 3) - take(field, axis, 2)) + second_coef * (
        take(field, axis, 4) - take(field, axis, 1)
    )


def backward(field, axis):
    return first_coef * (take(field, axis, 2) - take(field, axis, 1)) + second_coef * (
        take(field, axis, 3) - take(field, axis, 0)
    )


def safe_total(total):
    return jnp.where(total > 0.0, total, 1.0)


def coefficients(recips, lam, shear):
    size_x, size_y, size_z = lam.shape
    buoy = recips[0]
    comp = recips[1]

    def part(field, dx, dy, dz):
        return field[dx : dx + size_x, dy : dy + size_y, dz : dz + size_z]

    base_b = part(buoy, 0, 0, 0)
    buoy_x = 0.5 * (base_b + part(buoy, 1, 0, 0))
    buoy_y = 0.5 * (base_b + part(buoy, 0, 1, 0))
    buoy_z = 0.5 * (base_b + part(buoy, 0, 0, 1))
    base_c = part(comp, 0, 0, 0)
    shear_xy = 4.0 / safe_total(
        base_c + part(comp, 1, 0, 0) + part(comp, 0, 1, 0) + part(comp, 1, 1, 0)
    )
    shear_xz = 4.0 / safe_total(
        base_c + part(comp, 1, 0, 0) + part(comp, 0, 0, 1) + part(comp, 1, 0, 1)
    )
    shear_yz = 4.0 / safe_total(
        base_c + part(comp, 0, 1, 0) + part(comp, 0, 0, 1) + part(comp, 0, 1, 1)
    )
    return ((buoy_x, buoy_y, buoy_z), (lam, lam + 2.0 * shear, shear_xy, shear_xz, shear_yz))


def velocity_update(velocity, padded_stress, buoys):
    stress_xx, stress_yy, stress_zz = (padded_stress[0], padded_stress[1], padded_stress[2])
    stress_xy, stress_xz, stress_yz = (padded_stress[3], padded_stress[4], padded_stress[5])
    accel_x = forward(stress_xx, 0) + backward(stress_xy, 1) + backward(stress_xz, 2)
    accel_y = backward(stress_xy, 0) + forward(stress_yy, 1) + backward(stress_yz, 2)
    accel_z = backward(stress_xz, 0) + backward(stress_yz, 1) + forward(stress_zz, 2)
    return velocity + time_step * jnp.stack(
        [buoys[0] * accel_x, buoys[1] * accel_y, buoys[2] * accel_z]
    )


def stress_update(stress, padded_velocity, moduli):
    lam, lam_two, shear_xy, shear_xz, shear_yz = moduli
    vel_x, vel_y, vel_z = (padded_velocity[0], padded_velocity[1], padded_velocity[2])
    strain_xx = backward(vel_x, 0)
    strain_yy = backward(vel_y, 1)
    strain_zz = backward(vel_z, 2)
    new_xx = stress[0] + time_step * (lam_two * strain_xx + lam * (strain_yy + strain_zz))
    new_yy = stress[1] + time_step * (lam_two * strain_yy + lam * (strain_xx + strain_zz))
    new_zz = stress[2] + time_step * (lam_two * strain_zz + lam * (strain_xx + strain_yy))
    new_xy = stress[3] + time_step * shear_xy * (forward(vel_x, 1) + forward(vel_y, 0))
    new_xz = stress[4] + time_step * shear_xz * (forward(vel_x, 2) + forward(vel_z, 0))
    new_yz = stress[5] + time_step * shear_yz * (forward(vel_y, 2) + forward(vel_z, 1))
    return jnp.stack([new_xx, new_yy, new_zz, new_xy, new_xz, new_yz])


def pad_depth(field):
    return jnp.pad(field, ((0, 0), (0, 0), (0, 0), (2, 2)))


def finish_material(extended):
    return jnp.pad(extended, ((0, 0), (0, 0), (0, 0), (0, 1)))


def per_device(velocity, stress, density, lame_lambda, lame_mu):
    recips = jnp.stack([1.0 / density, 1.0 / lame_mu])
    plane = from_behind(recips[:, 0:1], "gx", -1)
    extended = jnp.concatenate([recips, plane], axis=1)
    column = from_behind(extended[:, :, 0:1], "gy", -1)
    extended = jnp.concatenate([extended, column], axis=2)
    buoys, moduli = coefficients(finish_material(extended), lame_lambda, lame_mu)
    for step in range(2):
        padded = padded_2(stress, (("gx", 1), ("gy", 2)), 2)
        velocity = velocity_update(velocity, pad_depth(padded), buoys)
        padded = padded_2(velocity, (("gx", 1), ("gy", 2)), 2)
        stress = stress_update(stress, pad_depth(padded), moduli)
    return (velocity, stress)


def solution(mesh):
    in_specs = (
        P(None, "gx", "gy", None),
        P(None, "gx", "gy", None),
        P("gx", "gy", None),
        P("gx", "gy", None),
        P("gx", "gy", None),
    )
    out_specs = (P(None, "gx", "gy", None), P(None, "gx", "gy", None))
    return jax.shard_map(
        per_device, mesh=mesh, in_specs=in_specs, out_specs=out_specs, check_vma=False
    )
```

profile of v0, /device:TPU:1, one launch (start us, length us, event | category | flops | bytes accessed | tf_op | source)
XLA Modules:
  0.0 98.6 jit_solution(18269461182126325994)
XLA Ops:
  0.6 1.0 %divide_bitcast_fusion = (f32[1,8,32,128]{3,2,1,0:T(8,128)S(1)}, f32[1,8,32,128]{3,2,1,0:T(8,128)S(1)}) fusion(f32[8,32,128]{2,1,0:T(8,128)} %param.9, f32[8,32,128]{2,1,0:T(8,128)} %param.7), kind=kLoop, calls=%fused_computation.308 | loop fusion | flops 65536 | bytes 524288 | tf_op jit(solution)/shard_map/stack | solution.py:117
  1.7 1.4 %collective-permute-start = (f32[2,1,32,128]{3,2,1,0:T(8,128)S(1)}, f32[2,1,32,128]{3,2,1,0:T(8,128)S(1)}, u32[]{:S(2)}, u32[]{:S(2)}) collective-permute-start(f32[2,1,32,128]{3,2,1,0:T(8,128)S(1)} %pad_maximum_fusion.9), channel_id=1, source_target_pairs={{8,0},{16,8},{24,16},{9,1},{17,9},{25,17},{10,2},{18,10},{26,18},{... | collective-permute-start | bytes 98312 | tf_op jit(solution)/shard_map/ppermute | solution.py:14
  3.1 1.1 %fusion.183 = (f32[6,2,32,128]{3,2,1,0:T(8,128)S(1)}, f32[6,2,32,128]{3,2,1,0:T(8,128)S(1)}) fusion(f32[6,8,32,128]{3,2,1,0:T(8,128)} %param.6), kind=kLoop, calls=%fused_computation.327 | loop fusion | bytes 786432 | tf_op jit(solution)/shard_map/slice | solution.py:25
  4.2 4.6 %collective-permute-start.2 = (f32[6,2,32,128]{3,2,1,0:T(8,128)S(1)}, f32[6,2,32,128]{3,2,1,0:T(8,128)S(1)}, u32[]{:S(2)}, u32[]{:S(2)}) collective-permute-start(f32[6,2,32,128]{3,2,1,0:T(8,128)S(1)} %get-tuple-element.49), channel_id=1, source_target_pairs={{0,8},{8,16},{16,24},{1,9},{9,17},{17,25},{2,10},{10,18},{18,26},{... | collective-permute-start | bytes 589832 | tf_op jit(solution)/shard_map/ppermute | solution.py:22
  8.8 2.9 %collective-permute-start.1 = (f32[2,9,1,128]{3,2,1,0:T(1,128)S(1)}, f32[2,9,1,128]{3,2,1,0:T(1,128)S(1)}, u32[]{:S(2)}, u32[]{:S(2)}) collective-permute-start(f32[2,9,1,128]{3,2,1,0:T(1,128)S(1)} %pad_maximum_fusion.10), channel_id=1, source_target_pairs={{1,0},{2,1},{3,2},{4,3},{5,4},{6,5},{7,6},{9,8},{10,9},{11,10},{12... | collective-permute-start | bytes 27656 | tf_op jit(solution)/shard_map/ppermute | solution.py:14
  11.7 1.3 %collective-permute-start.3 = (f32[6,2,32,128]{3,2,1,0:T(8,128)S(1)}, f32[6,2,32,128]{3,2,1,0:T(8,128)S(1)}, u32[]{:S(2)}, u32[]{:S(2)}) collective-permute-start(f32[6,2,32,128]{3,2,1,0:T(8,128)S(1)} %get-tuple-element.48), channel_id=1, source_target_pairs={{8,0},{16,8},{24,16},{9,1},{17,9},{25,17},{10,2},{18,10},{26,18},{... | collective-permute-start | bytes 589832 | tf_op jit(solution)/shard_map/ppermute | solution.py:25
  13.0 1.7 %collective-permute-done.1 = f32[2,9,1,128]{3,2,1,0:T(1,128)S(1)} collective-permute-done((f32[2,9,1,128]{3,2,1,0:T(1,128)S(1)}, f32[2,9,1,128]{3,2,1,0:T(1,128)S(1)}, u32[]{:S(2)}, u32[]{:S(2)}) %collective-permute-start.1) | collective-permute-done | bytes 9248 | tf_op jit(solution)/shard_map/ppermute | solution.py:14
  14.9 6.1 %collective-permute-done.3 = f32[6,2,32,128]{3,2,1,0:T(8,128)S(1)} collective-permute-done((f32[6,2,32,128]{3,2,1,0:T(8,128)S(1)}, f32[6,2,32,128]{3,2,1,0:T(8,128)S(1)}, u32[]{:S(2)}, u32[]{:S(2)}) %collective-permute-start.3) | collective-permute-done | bytes 196640 | tf_op jit(solution)/shard_map/ppermute | solution.py:25
  21.0 4.2 %collective-permute-start.4 = (f32[6,12,2,128]{3,2,1,0:T(2,128)S(1)}, f32[6,12,2,128]{3,2,1,0:T(2,128)S(1)}, u32[]{:S(2)}, u32[]{:S(2)}) collective-permute-start(f32[6,12,2,128]{3,2,1,0:T(2,128)S(1)} %get-tuple-element.44), channel_id=1, source_target_pairs={{0,1},{1,2},{2,3},{3,4},{4,5},{5,6},{6,7},{8,9},{9,10},{10,11},{11... | collective-permute-start | bytes 221192 | tf_op jit(solution)/shard_map/ppermute | solution.py:22
  25.2 1.9 %collective-permute-start.5 = (f32[6,12,2,128]{3,2,1,0:T(2,128)S(1)}, f32[6,12,2,128]{3,2,1,0:T(2,128)S(1)}, u32[]{:S(2)}, u32[]{:S(2)}) collective-permute-start(f32[6,12,2,128]{3,2,1,0:T(2,128)S(1)} %get-tuple-element.45), channel_id=1, source_target_pairs={{1,0},{2,1},{3,2},{4,3},{5,4},{6,5},{7,6},{9,8},{10,9},{11,10},{12... | collective-permute-start | bytes 221192 | tf_op jit(solution)/shard_map/ppermute | solution.py:25
  27.2 3.7 %collective-permute-done.5 = f32[6,12,2,128]{3,2,1,0:T(2,128)S(1)} collective-permute-done((f32[6,12,2,128]{3,2,1,0:T(2,128)S(1)}, f32[6,12,2,128]{3,2,1,0:T(2,128)S(1)}, u32[]{:S(2)}, u32[]{:S(2)}) %collective-permute-start.5) | collective-permute-done | bytes 73760 | tf_op jit(solution)/shard_map/ppermute | solution.py:25
  30.9 1.1 %select_maximum_fusion.4 = f32[6,12,36,132]{3,2,1,0:T(8,128)S(1)} fusion(f32[6,12,2,128]{3,2,1,0:T(2,128)S(1)} %collective-permute-done.5, f32[6,12,32,128]{3,2,1,0:T(8,128)S(1)} %constant_dynamic-update-slice_fusion, f32[6,12,2,128]{3,2,1,0:T(2,128)S(1)} %collective-permute-done.4), kind=kLoop, calls=%fused_computation.6 | loop fusion | flops 2737152 | bytes 2695680 | tf_op jit(solution)/shard_map/concatenate | solution.py:26
  32.3 0.4 fusion.159
  32.7 0.4 fusion.145
  33.2 0.5 fusion.131
  33.7 0.5 copy-done.4
  34.3 4.3 %collective-permute-start.6 = (f32[3,2,32,128]{3,2,1,0:T(8,128)S(1)}, f32[3,2,32,128]{3,2,1,0:T(8,128)S(1)}, u32[]{:S(2)}, u32[]{:S(2)}) collective-permute-start(f32[3,2,32,128]{3,2,1,0:T(8,128)S(1)} %get-tuple-element.58), channel_id=1, source_target_pairs={{0,8},{8,16},{16,24},{1,9},{9,17},{17,25},{2,10},{10,18},{18,26},{... | collective-permute-start | bytes 294920 | tf_op jit(solution)/shard_map/ppermute | solution.py:22
  38.5 1.3 %collective-permute-start.7 = (f32[3,2,32,128]{3,2,1,0:T(8,128)S(1)}, f32[3,2,32,128]{3,2,1,0:T(8,128)S(1)}, u32[]{:S(2)}, u32[]{:S(2)}) collective-permute-start(f32[3,2,32,128]{3,2,1,0:T(8,128)S(1)} %get-tuple-element.59), channel_id=1, source_target_pairs={{8,0},{16,8},{24,16},{9,1},{17,9},{25,17},{10,2},{18,10},{26,18},{... | collective-permute-start | bytes 294920 | tf_op jit(solution)/shard_map/ppermute | solution.py:25
  40.1 3.7 %collective-permute-done.7 = f32[3,2,32,128]{3,2,1,0:T(8,128)S(1)} collective-permute-done((f32[3,2,32,128]{3,2,1,0:T(8,128)S(1)}, f32[3,2,32,128]{3,2,1,0:T(8,128)S(1)}, u32[]{:S(2)}, u32[]{:S(2)}) %collective-permute-start.7) | collective-permute-done | bytes 98336 | tf_op jit(solution)/shard_map/ppermute | solution.py:25
  43.9 3.9 %collective-permute-start.8 = (f32[3,12,2,128]{3,2,1,0:T(2,128)S(1)}, f32[3,12,2,128]{3,2,1,0:T(2,128)S(1)}, u32[]{:S(2)}, u32[]{:S(2)}) collective-permute-start(f32[3,12,2,128]{3,2,1,0:T(2,128)S(1)} %get-tuple-element.54), channel_id=1, source_target_pairs={{0,1},{1,2},{2,3},{3,4},{4,5},{5,6},{6,7},{8,9},{9,10},{10,11},{11... | collective-permute-start | bytes 110600 | tf_op jit(solution)/shard_map/ppermute | solution.py:22
  47.8 1.9 %collective-permute-start.9 = (f32[3,12,2,128]{3,2,1,0:T(2,128)S(1)}, f32[3,12,2,128]{3,2,1,0:T(2,128)S(1)}, u32[]{:S(2)}, u32[]{:S(2)}) collective-permute-start(f32[3,12,2,128]{3,2,1,0:T(2,128)S(1)} %get-tuple-element.55), channel_id=1, source_target_pairs={{1,0},{2,1},{3,2},{4,3},{5,4},{6,5},{7,6},{9,8},{10,9},{11,10},{12... | collective-permute-start | bytes 110600 | tf_op jit(solution)/shard_map/ppermute | solution.py:25
  49.8 3.3 %collective-permute-done.9 = f32[3,12,2,128]{3,2,1,0:T(2,128)S(1)} collective-permute-done((f32[3,12,2,128]{3,2,1,0:T(2,128)S(1)}, f32[3,12,2,128]{3,2,1,0:T(2,128)S(1)}, u32[]{:S(2)}, u32[]{:S(2)}) %collective-permute-start.9) | collective-permute-done | bytes 36896 | tf_op jit(solution)/shard_map/ppermute | solution.py:25
  53.1 0.6 select_maximum_fusion.10
  53.9 0.8 copy-done
  54.7 0.4 bitcast_dynamic-update-slice_fusion.8
  55.3 0.4 bitcast_dynamic-update-slice_fusion.5
  55.7 0.4 bitcast_dynamic-update-slice_fusion.4
  56.1 0.4 bitcast_dynamic-update-slice_fusion.3
  56.5 2.2 %collective-permute-start.10 = (f32[6,2,32,128]{3,2,1,0:T(8,128)S(1)}, f32[6,2,32,128]{3,2,1,0:T(8,128)S(1)}, u32[]{:S(2)}, u32[]{:S(2)}) collective-permute-start(f32[6,2,32,128]{3,2,1,0:T(8,128)S(1)} %get-tuple-element.46), channel_id=1, source_target_pairs={{0,8},{8,16},{16,24},{1,9},{9,17},{17,25},{2,10},{10,18},{18,26},{... | collective-permute-start | bytes 589832 | tf_op jit(solution)/shard_map/ppermute | solution.py:22
  58.8 1.3 %collective-permute-start.11 = (f32[6,2,32,128]{3,2,1,0:T(8,128)S(1)}, f32[6,2,32,128]{3,2,1,0:T(8,128)S(1)}, u32[]{:S(2)}, u32[]{:S(2)}) collective-permute-start(f32[6,2,32,128]{3,2,1,0:T(8,128)S(1)} %get-tuple-element.47), channel_id=1, source_target_pairs={{8,0},{16,8},{24,16},{9,1},{17,9},{25,17},{10,2},{18,10},{26,18},{... | collective-permute-start | bytes 589832 | tf_op jit(solution)/shard_map/ppermute | solution.py:25
  60.1 1.7 %collective-permute-done.10 = f32[6,2,32,128]{3,2,1,0:T(8,128)S(1)} collective-permute-done((f32[6,2,32,128]{3,2,1,0:T(8,128)S(1)}, f32[6,2,32,128]{3,2,1,0:T(8,128)S(1)}, u32[]{:S(2)}, u32[]{:S(2)}) %collective-permute-start.10) | collective-permute-done | bytes 196640 | tf_op jit(solution)/shard_map/ppermute | solution.py:22
  61.8 4.4 %collective-permute-done.11 = f32[6,2,32,128]{3,2,1,0:T(8,128)S(1)} collective-permute-done((f32[6,2,32,128]{3,2,1,0:T(8,128)S(1)}, f32[6,2,32,128]{3,2,1,0:T(8,128)S(1)}, u32[]{:S(2)}, u32[]{:S(2)}) %collective-permute-start.11) | collective-permute-done | bytes 196640 | tf_op jit(solution)/shard_map/ppermute | solution.py:25
  66.2 4.5 %collective-permute-start.12 = (f32[6,12,2,128]{3,2,1,0:T(2,128)S(1)}, f32[6,12,2,128]{3,2,1,0:T(2,128)S(1)}, u32[]{:S(2)}, u32[]{:S(2)}) collective-permute-start(f32[6,12,2,128]{3,2,1,0:T(2,128)S(1)} %get-tuple-element.42), channel_id=1, source_target_pairs={{0,1},{1,2},{2,3},{3,4},{4,5},{5,6},{6,7},{8,9},{9,10},{10,11},{11... | collective-permute-start | bytes 221192 | tf_op jit(solution)/shard_map/ppermute | solution.py:22
  70.8 1.9 %collective-permute-start.13 = (f32[6,12,2,128]{3,2,1,0:T(2,128)S(1)}, f32[6,12,2,128]{3,2,1,0:T(2,128)S(1)}, u32[]{:S(2)}, u32[]{:S(2)}) collective-permute-start(f32[6,12,2,128]{3,2,1,0:T(2,128)S(1)} %get-tuple-element.43), channel_id=1, source_target_pairs={{1,0},{2,1},{3,2},{4,3},{5,4},{6,5},{7,6},{9,8},{10,9},{11,10},{12... | collective-permute-start | bytes 221192 | tf_op jit(solution)/shard_map/ppermute | solution.py:25
  72.7 3.7 %collective-permute-done.13 = f32[6,12,2,128]{3,2,1,0:T(2,128)S(1)} collective-permute-done((f32[6,12,2,128]{3,2,1,0:T(2,128)S(1)}, f32[6,12,2,128]{3,2,1,0:T(2,128)S(1)}, u32[]{:S(2)}, u32[]{:S(2)}) %collective-permute-start.13) | collective-permute-done | bytes 73760 | tf_op jit(solution)/shard_map/ppermute | solution.py:25
  76.4 1.1 %select_maximum_fusion = f32[6,12,36,132]{3,2,1,0:T(8,128)S(1)} fusion(f32[6,12,2,128]{3,2,1,0:T(2,128)S(1)} %collective-permute-done.13, f32[6,12,2,128]{3,2,1,0:T(2,128)S(1)} %collective-permute-done.12, f32[6,2,32,128]{3,2,1,0:T(8,128)S(1)} %collective-permute-done.11, f32[6,8,32,128]{3,2,1,0:T(8,128)S(1)} %get-tuple-element.6, ...), kind=kLoop, calls=%fused_computation.2 | loop fusion | flops 4105728 | bytes 2695680 | tf_op jit(solution)/shard_map/concatenate | solution.py:26
  77.8 0.4 fusion.82
  78.3 0.4 fusion.69
  78.7 0.5 fusion.56
  79.4 1.8 %collective-permute-start.14 = (f32[3,2,32,128]{3,2,1,0:T(8,128)S(1)}, f32[3,2,32,128]{3,2,1,0:T(8,128)S(1)}, u32[]{:S(2)}, u32[]{:S(2)}) collective-permute-start(f32[3,2,32,128]{3,2,1,0:T(8,128)S(1)} %get-tuple-element.56), channel_id=1, source_target_pairs={{0,8},{8,16},{16,24},{1,9},{9,17},{17,25},{2,10},{10,18},{18,26},{... | collective-permute-start | bytes 294920 | tf_op jit(solution)/shard_map/ppermute | solution.py:22
  81.2 1.3 %collective-permute-start.15 = (f32[3,2,32,128]{3,2,1,0:T(8,128)S(1)}, f32[3,2,32,128]{3,2,1,0:T(8,128)S(1)}, u32[]{:S(2)}, u32[]{:S(2)}) collective-permute-start(f32[3,2,32,128]{3,2,1,0:T(8,128)S(1)} %get-tuple-element.57), channel_id=1, source_target_pairs={{8,0},{16,8},{24,16},{9,1},{17,9},{25,17},{10,2},{18,10},{26,18},{... | collective-permute-start | bytes 294920 | tf_op jit(solution)/shard_map/ppermute | solution.py:25
  82.8 3.7 %collective-permute-done.15 = f32[3,2,32,128]{3,2,1,0:T(8,128)S(1)} collective-permute-done((f32[3,2,32,128]{3,2,1,0:T(8,128)S(1)}, f32[3,2,32,128]{3,2,1,0:T(8,128)S(1)}, u32[]{:S(2)}, u32[]{:S(2)}) %collective-permute-start.15) | collective-permute-done | bytes 98336 | tf_op jit(solution)/shard_map/ppermute | solution.py:25
  86.6 3.5 %collective-permute-start.16 = (f32[3,12,2,128]{3,2,1,0:T(2,128)S(1)}, f32[3,12,2,128]{3,2,1,0:T(2,128)S(1)}, u32[]{:S(2)}, u32[]{:S(2)}) collective-permute-start(f32[3,12,2,128]{3,2,1,0:T(2,128)S(1)} %get-tuple-element.52), channel_id=1, source_target_pairs={{0,1},{1,2},{2,3},{3,4},{4,5},{5,6},{6,7},{8,9},{9,10},{10,11},{11... | collective-permute-start | bytes 110600 | tf_op jit(solution)/shard_map/ppermute | solution.py:22
  90.1 1.9 %collective-permute-start.17 = (f32[3,12,2,128]{3,2,1,0:T(2,128)S(1)}, f32[3,12,2,128]{3,2,1,0:T(2,128)S(1)}, u32[]{:S(2)}, u32[]{:S(2)}) collective-permute-start(f32[3,12,2,128]{3,2,1,0:T(2,128)S(1)} %get-tuple-element.53), channel_id=1, source_target_pairs={{1,0},{2,1},{3,2},{4,3},{5,4},{6,5},{7,6},{9,8},{10,9},{11,10},{12... | collective-permute-start | bytes 110600 | tf_op jit(solution)/shard_map/ppermute | solution.py:25
  92.0 3.3 %collective-permute-done.17 = f32[3,12,2,128]{3,2,1,0:T(2,128)S(1)} collective-permute-done((f32[3,12,2,128]{3,2,1,0:T(2,128)S(1)}, f32[3,12,2,128]{3,2,1,0:T(2,128)S(1)}, u32[]{:S(2)}, u32[]{:S(2)}) %collective-permute-start.17) | collective-permute-done | bytes 36896 | tf_op jit(solution)/shard_map/ppermute | solution.py:25
  95.3 0.6 select_maximum_fusion.6
  96.1 0.5 bitcast_dynamic-update-slice_fusion.2
  97.7 0.9 copy-done.5
  (44 shorter events, 3.3 us)
Async XLA Ops:
  1.6 13.1 %copy-start.1 = (f32[6,8,32,128]{3,2,1,0:T(8,128)S(1)}, f32[6,8,32,128]{3,2,1,0:T(8,128)}, u32[]{:S(2)}) copy-start(f32[6,8,32,128]{3,2,1,0:T(8,128)} %param.6) | copy-start | bytes 2359300
  1.7 7.1 %collective-permute-start = (f32[2,1,32,128]{3,2,1,0:T(8,128)S(1)}, f32[2,1,32,128]{3,2,1,0:T(8,128)S(1)}, u32[]{:S(2)}, u32[]{:S(2)}) collective-permute-start(f32[2,1,32,128]{3,2,1,0:T(8,128)S(1)} %pad_maximum_fusion.9), channel_id=1, source_target_pairs={{8,0},{16,8},{24,16},{9,1},{17,9},{25,17},{10,2},{18,10},{26,18},{... | collective-permute-start | bytes 98312 | tf_op jit(solution)/shard_map/ppermute | solution.py:14
  4.2 10.6 %collective-permute-start.2 = (f32[6,2,32,128]{3,2,1,0:T(8,128)S(1)}, f32[6,2,32,128]{3,2,1,0:T(8,128)S(1)}, u32[]{:S(2)}, u32[]{:S(2)}) collective-permute-start(f32[6,2,32,128]{3,2,1,0:T(8,128)S(1)} %get-tuple-element.49), channel_id=1, source_target_pairs={{0,8},{8,16},{16,24},{1,9},{9,17},{17,25},{2,10},{10,18},{18,26},{... | collective-permute-start | bytes 589832 | tf_op jit(solution)/shard_map/ppermute | solution.py:22
  8.8 5.9 %collective-permute-start.1 = (f32[2,9,1,128]{3,2,1,0:T(1,128)S(1)}, f32[2,9,1,128]{3,2,1,0:T(1,128)S(1)}, u32[]{:S(2)}, u32[]{:S(2)}) collective-permute-start(f32[2,9,1,128]{3,2,1,0:T(1,128)S(1)} %pad_maximum_fusion.10), channel_id=1, source_target_pairs={{1,0},{2,1},{3,2},{4,3},{5,4},{6,5},{7,6},{9,8},{10,9},{11,10},{12... | collective-permute-start | bytes 27656 | tf_op jit(solution)/shard_map/ppermute | solution.py:14
  11.7 9.3 %collective-permute-start.3 = (f32[6,2,32,128]{3,2,1,0:T(8,128)S(1)}, f32[6,2,32,128]{3,2,1,0:T(8,128)S(1)}, u32[]{:S(2)}, u32[]{:S(2)}) collective-permute-start(f32[6,2,32,128]{3,2,1,0:T(8,128)S(1)} %get-tuple-element.48), channel_id=1, source_target_pairs={{8,0},{16,8},{24,16},{9,1},{17,9},{25,17},{10,2},{18,10},{26,18},{... | collective-permute-start | bytes 589832 | tf_op jit(solution)/shard_map/ppermute | solution.py:25
  21.0 6.2 %collective-permute-start.4 = (f32[6,12,2,128]{3,2,1,0:T(2,128)S(1)}, f32[6,12,2,128]{3,2,1,0:T(2,128)S(1)}, u32[]{:S(2)}, u32[]{:S(2)}) collective-permute-start(f32[6,12,2,128]{3,2,1,0:T(2,128)S(1)} %get-tuple-element.44), channel_id=1, source_target_pairs={{0,1},{1,2},{2,3},{3,4},{4,5},{5,6},{6,7},{8,9},{9,10},{10,11},{11... | collective-permute-start | bytes 221192 | tf_op jit(solution)/shard_map/ppermute | solution.py:22
  25.2 5.7 %collective-permute-start.5 = (f32[6,12,2,128]{3,2,1,0:T(2,128)S(1)}, f32[6,12,2,128]{3,2,1,0:T(2,128)S(1)}, u32[]{:S(2)}, u32[]{:S(2)}) collective-permute-start(f32[6,12,2,128]{3,2,1,0:T(2,128)S(1)} %get-tuple-element.45), channel_id=1, source_target_pairs={{1,0},{2,1},{3,2},{4,3},{5,4},{6,5},{7,6},{9,8},{10,9},{11,10},{12... | collective-permute-start | bytes 221192 | tf_op jit(solution)/shard_map/ppermute | solution.py:25
  33.2 1.0 %copy-start.4 = (f32[3,8,32,128]{3,2,1,0:T(8,128)S(1)}, f32[3,8,32,128]{3,2,1,0:T(8,128)}, u32[]{:S(2)}) copy-start(f32[3,8,32,128]{3,2,1,0:T(8,128)} %param.5) | copy-start | bytes 1179652
  34.3 5.9 %collective-permute-start.6 = (f32[3,2,32,128]{3,2,1,0:T(8,128)S(1)}, f32[3,2,32,128]{3,2,1,0:T(8,128)S(1)}, u32[]{:S(2)}, u32[]{:S(2)}) collective-permute-start(f32[3,2,32,128]{3,2,1,0:T(8,128)S(1)} %get-tuple-element.58), channel_id=1, source_target_pairs={{0,8},{8,16},{16,24},{1,9},{9,17},{17,25},{2,10},{10,18},{18,26},{... | collective-permute-start | bytes 294920 | tf_op jit(solution)/shard_map/ppermute | solution.py:22
  38.5 5.4 %collective-permute-start.7 = (f32[3,2,32,128]{3,2,1,0:T(8,128)S(1)}, f32[3,2,32,128]{3,2,1,0:T(8,128)S(1)}, u32[]{:S(2)}, u32[]{:S(2)}) collective-permute-start(f32[3,2,32,128]{3,2,1,0:T(8,128)S(1)} %get-tuple-element.59), channel_id=1, source_target_pairs={{8,0},{16,8},{24,16},{9,1},{17,9},{25,17},{10,2},{18,10},{26,18},{... | collective-permute-start | bytes 294920 | tf_op jit(solution)/shard_map/ppermute | solution.py:25
  43.9 5.9 %collective-permute-start.8 = (f32[3,12,2,128]{3,2,1,0:T(2,128)S(1)}, f32[3,12,2,128]{3,2,1,0:T(2,128)S(1)}, u32[]{:S(2)}, u32[]{:S(2)}) collective-permute-start(f32[3,12,2,128]{3,2,1,0:T(2,128)S(1)} %get-tuple-element.54), channel_id=1, source_target_pairs={{0,1},{1,2},{2,3},{3,4},{4,5},{5,6},{6,7},{8,9},{9,10},{10,11},{11... | collective-permute-start | bytes 110600 | tf_op jit(solution)/shard_map/ppermute | solution.py:22
  47.8 5.3 %collective-permute-start.9 = (f32[3,12,2,128]{3,2,1,0:T(2,128)S(1)}, f32[3,12,2,128]{3,2,1,0:T(2,128)S(1)}, u32[]{:S(2)}, u32[]{:S(2)}) collective-permute-start(f32[3,12,2,128]{3,2,1,0:T(2,128)S(1)} %get-tuple-element.55), channel_id=1, source_target_pairs={{1,0},{2,1},{3,2},{4,3},{5,4},{6,5},{7,6},{9,8},{10,9},{11,10},{12... | collective-permute-start | bytes 110600 | tf_op jit(solution)/shard_map/ppermute | solution.py:25
  53.7 0.9 copy-start
  53.8 1.0 copy-start.3
  56.5 5.2 %collective-permute-start.10 = (f32[6,2,32,128]{3,2,1,0:T(8,128)S(1)}, f32[6,2,32,128]{3,2,1,0:T(8,128)S(1)}, u32[]{:S(2)}, u32[]{:S(2)}) collective-permute-start(f32[6,2,32,128]{3,2,1,0:T(8,128)S(1)} %get-tuple-element.46), channel_id=1, source_target_pairs={{0,8},{8,16},{16,24},{1,9},{9,17},{17,25},{2,10},{10,18},{18,26},{... | collective-permute-start | bytes 589832 | tf_op jit(solution)/shard_map/ppermute | solution.py:22
  58.8 7.4 %collective-permute-start.11 = (f32[6,2,32,128]{3,2,1,0:T(8,128)S(1)}, f32[6,2,32,128]{3,2,1,0:T(8,128)S(1)}, u32[]{:S(2)}, u32[]{:S(2)}) collective-permute-start(f32[6,2,32,128]{3,2,1,0:T(8,128)S(1)} %get-tuple-element.47), channel_id=1, source_target_pairs={{8,0},{16,8},{24,16},{9,1},{17,9},{25,17},{10,2},{18,10},{26,18},{... | collective-permute-start | bytes 589832 | tf_op jit(solution)/shard_map/ppermute | solution.py:25
  66.2 6.5 %collective-permute-start.12 = (f32[6,12,2,128]{3,2,1,0:T(2,128)S(1)}, f32[6,12,2,128]{3,2,1,0:T(2,128)S(1)}, u32[]{:S(2)}, u32[]{:S(2)}) collective-permute-start(f32[6,12,2,128]{3,2,1,0:T(2,128)S(1)} %get-tuple-element.42), channel_id=1, source_target_pairs={{0,1},{1,2},{2,3},{3,4},{4,5},{5,6},{6,7},{8,9},{9,10},{10,11},{11... | collective-permute-start | bytes 221192 | tf_op jit(solution)/shard_map/ppermute | solution.py:22
  70.8 5.7 %collective-permute-start.13 = (f32[6,12,2,128]{3,2,1,0:T(2,128)S(1)}, f32[6,12,2,128]{3,2,1,0:T(2,128)S(1)}, u32[]{:S(2)}, u32[]{:S(2)}) collective-permute-start(f32[6,12,2,128]{3,2,1,0:T(2,128)S(1)} %get-tuple-element.43), channel_id=1, source_target_pairs={{1,0},{2,1},{3,2},{4,3},{5,4},{6,5},{7,6},{9,8},{10,9},{11,10},{12... | collective-permute-start | bytes 221192 | tf_op jit(solution)/shard_map/ppermute | solution.py:25
  79.4 16.6 %copy-start.2 = (f32[3,8,32,128]{3,2,1,0:T(8,128)}, f32[3,8,32,128]{3,2,1,0:T(8,128)S(1)}, u32[]{:S(2)}) copy-start(f32[3,8,32,128]{3,2,1,0:T(8,128)S(1)} %fusion.3) | copy-start | bytes 1179652
  79.4 3.4 %collective-permute-start.14 = (f32[3,2,32,128]{3,2,1,0:T(8,128)S(1)}, f32[3,2,32,128]{3,2,1,0:T(8,128)S(1)}, u32[]{:S(2)}, u32[]{:S(2)}) collective-permute-start(f32[3,2,32,128]{3,2,1,0:T(8,128)S(1)} %get-tuple-element.56), channel_id=1, source_target_pairs={{0,8},{8,16},{16,24},{1,9},{9,17},{17,25},{2,10},{10,18},{18,26},{... | collective-permute-start | bytes 294920 | tf_op jit(solution)/shard_map/ppermute | solution.py:22
  81.2 5.4 %collective-permute-start.15 = (f32[3,2,32,128]{3,2,1,0:T(8,128)S(1)}, f32[3,2,32,128]{3,2,1,0:T(8,128)S(1)}, u32[]{:S(2)}, u32[]{:S(2)}) collective-permute-start(f32[3,2,32,128]{3,2,1,0:T(8,128)S(1)} %get-tuple-element.57), channel_id=1, source_target_pairs={{8,0},{16,8},{24,16},{9,1},{17,9},{25,17},{10,2},{18,10},{26,18},{... | collective-permute-start | bytes 294920 | tf_op jit(solution)/shard_map/ppermute | solution.py:25
  86.6 5.4 %collective-permute-start.16 = (f32[3,12,2,128]{3,2,1,0:T(2,128)S(1)}, f32[3,12,2,128]{3,2,1,0:T(2,128)S(1)}, u32[]{:S(2)}, u32[]{:S(2)}) collective-permute-start(f32[3,12,2,128]{3,2,1,0:T(2,128)S(1)} %get-tuple-element.52), channel_id=1, source_target_pairs={{0,1},{1,2},{2,3},{3,4},{4,5},{5,6},{6,7},{8,9},{9,10},{10,11},{11... | collective-permute-start | bytes 110600 | tf_op jit(solution)/shard_map/ppermute | solution.py:22
  90.1 5.3 %collective-permute-start.17 = (f32[3,12,2,128]{3,2,1,0:T(2,128)S(1)}, f32[3,12,2,128]{3,2,1,0:T(2,128)S(1)}, u32[]{:S(2)}, u32[]{:S(2)}) collective-permute-start(f32[3,12,2,128]{3,2,1,0:T(2,128)S(1)} %get-tuple-element.53), channel_id=1, source_target_pairs={{1,0},{2,1},{3,2},{4,3},{5,4},{6,5},{7,6},{9,8},{10,9},{11,10},{12... | collective-permute-start | bytes 110600 | tf_op jit(solution)/shard_map/ppermute | solution.py:25
  97.7 0.9 copy-start.5
where the time goes:
time: 99.3 us; the launch traced here: 98.6 us
  starting transfers between devices  46.2 us (47%)
  waiting for transfers between devices  36.1 us (36%)
  other arithmetic  11.1 us (11%)
  local copies, waits for them, and re-layouts  4.16 us (4%)
  between operations  1.14 us (1%)
    ppermute x8, waiting for transfers between devices, padded_2(): lax.ppermute(lax.slice_in_dim(block, 0, width, axis=dim), axis, backward)  32 us
    ppermute x8, starting transfers between devices, padded_2(): lax.ppermute(lax.slice_in_dim(block, block.shape[dim] - width, None, axis...  29 us
    ppermute x8, starting transfers between devices, padded_2(): lax.ppermute(lax.slice_in_dim(block, 0, width, axis=dim), axis, backward)  12.9 us
    ppermute x2, starting transfers between devices, from_behind(): return lax.ppermute(block, axis, route)  4.29 us
    concatenate x4, other arithmetic, padded_2(): block = jnp.concatenate([low, block, high], axis=dim)  3.51 us
    another operation x6, other arithmetic, velocity_update(): jnp.stack([buoys[0] * accel_x, buoys[1] * accel_y, buoys[2] * accel_z])  2.79 us
    unnamed x10, other arithmetic  2.62 us
    ppermute x8, waiting for transfers between devices, padded_2(): lax.ppermute(lax.slice_in_dim(block, block.shape[dim] - width, None, axis...  2.34 us
  transfers between devices with their start and end apart: 18, of which 12 were waited for; matrix products, arithmetic and copies ran while one was open for 1% of the time, Pallas kernels for 0%

commit v1 on v0

v1 whole, which is shorter than its diff:
```python
import jax
import jax.numpy as jnp
from jax import lax
from jax.experimental import pallas as pl
from jax.experimental.pallas import tpu as pltpu
from jax.sharding import PartitionSpec as P

near = 9.0 / 8.0
far = 1.0 / 24.0
time_step = 0.25
tile = 8
AXES = ("gx", "gy")


def pairings(count_x, count_y):
    other = 2 if count_x % 4 == 0 else 1

    def across(i, count):
        return ((i + 1) ^ 1) - 1

    def route(rule):
        pairs = []
        for i in range(count_x):
            for j in range(count_y):
                ti, tj = rule(i, j)
                pairs.append((i * count_y + j, ti * count_y + tj))
        return pairs

    def inner_x(i, j):
        return (i ^ 1, j)

    def outer_x(i, j):
        return (across(i, count_x), j) if 0 < i < count_x - 1 else (i, j ^ 1)

    def inner_y(i, j):
        return (i, j ^ 1)

    def outer_y(i, j):
        return (i, across(j, count_y)) if 0 < j < count_y - 1 else (i ^ other, j)

    return [route(rule) for rule in (inner_x, outer_x, inner_y, outer_y)]


def position():
    i, j = lax.axis_index("gx"), lax.axis_index("gy")
    return i, j, lax.rem(i, 2) == 0, lax.rem(j, 2) == 0


def unpack(inner, outer, low, high, even, first, last):
    for start in range(0, inner.shape[0], tile):
        rows = pl.ds(start, tile)
        a, b = inner[rows, :], outer[rows, :]
        low[rows, :] = jnp.where(first, 0.0, jnp.where(even, b, a))
        high[rows, :] = jnp.where(last, 0.0, jnp.where(even, a, b))


class Pack:
    def __init__(self, inner, outer, even):
        self.inner, self.outer, self.even = inner, outer, even

    def put(self, up, down):
        even, inner, outer = self.even, self.inner, self.outer

        @pl.when(even)
        def _():
            for rows, value in up():
                inner[rows, :] = value
            for rows, value in down():
                outer[rows, :] = value

        @pl.when(jnp.logical_not(even))
        def _():
            for rows, value in up():
                outer[rows, :] = value
            for rows, value in down():
                inner[rows, :] = value


def planes(items):
    out = []
    start = 0
    for ref, f, x in items:
        size = ref.shape[-2]
        value = ref[f, x] if f is not None else ref[x]
        out.append((pl.ds(start, size), value))
        start += size
    return out


def rows_of(items, count_x):
    out = []
    for x in range(count_x):
        start = tile * x
        for ref, f, row, count in items:
            value = ref[f, x, pl.ds(row, count), :] if f is not None else ref[x, pl.ds(row, count), :]
            out.append((pl.ds(start, count), value))
            start += count
    return out


def sides(i, j):
    return i == 0, i == lax.axis_size("gx") - 1, j == 0, j == lax.axis_size("gy") - 1


def lanes():
    return lax.broadcasted_iota(jnp.int32, (tile, 128), 1)


def z_shift(value, k, lane):
    size = value.shape[-1]
    moved = pltpu.roll(value, (-k) % size, 1)
    inside = lane < size - k if k > 0 else lane >= -k
    return jnp.where(inside, moved, 0.0)


def difference(at, base):
    return near * (at(base + 1) - at(base)) - far * (at(base + 2) - at(base - 1))


def first_pack(stress, density, shear, ax, bx, ay, by, recips):
    i, j, even_x, even_y = position()
    nx, ny = density.shape[0], density.shape[1]
    for x in range(nx):
        recips[0, x] = 1.0 / density[x]
        recips[1, x] = 1.0 / shear[x]
    Pack(ax, bx, even_x).put(
        lambda: planes([(stress, 3, nx - 2), (stress, 3, nx - 1), (stress, 4, nx - 2), (stress, 4, nx - 1), (stress, 0, nx - 1)]),
        lambda: planes([(stress, 3, 0), (stress, 4, 0), (stress, 0, 0), (stress, 0, 1), (recips, 0, 0), (recips, 1, 0)]),
    )
    Pack(ay, by, even_y).put(
        lambda: rows_of([(stress, 3, ny - 2, 2), (stress, 5, ny - 2, 2), (stress, 1, ny - 1, 1)], nx),
        lambda: rows_of([(stress, 3, 0, 1), (stress, 5, 0, 1), (stress, 1, 0, 2), (recips, 0, 0, 1), (recips, 1, 0, 1)], nx),
    )


class Field:
    def __init__(self, ref, f, low_x=None, high_x=None, low_y=None, high_y=None):
        self.ref, self.f = ref, f
        self.low_x, self.high_x, self.low_y, self.high_y = low_x, high_x, low_y, high_y

    def at(self, x, t):
        rows = pl.ds(tile * t, tile)
        nx, ny = self.ref.shape[-3], self.ref.shape[-2]
        if x < 0:
            ref, index = self.low_x
            return ref[pl.ds(ny * (index + x) + tile * t, tile), :]
        if x >= nx:
            ref, index = self.high_x
            return ref[pl.ds(ny * (index + x - nx) + tile * t, tile), :]
        return self.ref[self.f, x, rows, :]

    def y(self, x, t, k):
        ny = self.ref.shape[-2]
        start = tile * t + k
        if start < 0:
            return self.low_y[x, pl.ds(tile + k, tile), :]
        if start + tile > ny:
            return self.high_y[x, pl.ds(k, tile), :]
        return self.ref[self.f, x, pl.ds(start, tile), :]


def fill_edges(ref, f, edge, lows, highs, low_row, low_count, high_row, high_count):
    nx, ny = ref.shape[-3], ref.shape[-2]
    for x in range(nx):
        if low_count:
            edge[0, x, pl.ds(tile - low_count, low_count), :] = lows[pl.ds(tile * x + low_row, low_count), :]
            edge[0, x, pl.ds(tile, tile), :] = ref[f, x, pl.ds(0, tile), :]
        if high_count:
            edge[1, x, pl.ds(0, tile), :] = ref[f, x, pl.ds(ny - tile, tile), :]
            edge[1, x, pl.ds(tile, high_count), :] = highs[pl.ds(tile * x + high_row, high_count), :]


def receive(args, scratch):
    i, j, even_x, even_y = position()
    ax, bx, ay, by = args
    low_x, high_x, low_y, high_y = scratch
    first_x, last_x, first_y, last_y = sides(i, j)
    unpack(ax, bx, low_x, high_x, even_x, first_x, last_x)
    unpack(ay, by, low_y, high_y, even_y, first_y, last_y)
    return even_x, even_y


def velocity_kernel(step, *refs):
    if step == 0:
        (velocity, stress, recips, ax, bx, ay, by, out, pax, pbx, pay, pby, buoys,
         low_x, high_x, low_y, high_y, edges, edge_b) = refs
    else:
        (velocity, stress, buoys, ax, bx, ay, by, out, pax, pbx, pay, pby,
         low_x, high_x, low_y, high_y, edges) = refs
    nx, ny = stress.shape[1], stress.shape[2]
    even_x, even_y = receive((ax, bx, ay, by), (low_x, high_x, low_y, high_y))
    fill_edges(stress, 3, edges.at[0], low_y, high_y, 0, 2, 0, 1)
    fill_edges(stress, 5, edges.at[1], low_y, high_y, 2, 2, 1, 1)
    fill_edges(stress, 1, edges.at[2], low_y, high_y, 4, 1, 2, 2)
    xx = Field(stress, 0, (low_x, 5), (high_x, 2))
    yy = Field(stress, 1, low_y=edges.at[2, 0], high_y=edges.at[2, 1])
    zz = Field(stress, 2)
    xy = Field(stress, 3, (low_x, 2), (high_x, 0), edges.at[0, 0], edges.at[0, 1])
    xz = Field(stress, 4, (low_x, 4), (high_x, 1))
    yz = Field(stress, 5, low_y=edges.at[1, 0], high_y=edges.at[1, 1])
    if step == 0:
        fill_edges(recips, 0, edge_b, low_y, high_y, 0, 0, 4, 1)
        buoy = Field(recips, 0, None, (high_x, 4), None, edge_b.at[1])
    lane = lanes()
    for x in range(nx):
        for t in range(ny // tile):
            rows = pl.ds(tile * t, tile)

            def dx(field, base):
                return difference(lambda k: field.at(x + k, t), base)

            def dy(field, base):
                return difference(lambda k: field.y(x, t, k), base)

            def dz(field, base):
                value = field.at(x, t)
                return difference(lambda k: z_shift(value, k, lane) if k else value, base)

            if step == 0:
                here = buoy.at(x, t)
                half = 0.5 * time_step
                bx_ = half * (here + buoy.at(x + 1, t))
                by_ = half * (here + buoy.y(x, t, 1))
                bz_ = half * (here + z_shift(here, 1, lane))
                buoys[0, x, rows, :] = bx_
                buoys[1, x, rows, :] = by_
                buoys[2, x, rows, :] = bz_
            else:
                bx_, by_, bz_ = (buoys[c, x, rows, :] for c in range(3))
            out[0, x, rows, :] = velocity[0, x, rows, :] + bx_ * (dx(xx, 0) + dy(xy, -1) + dz(xz, -1))
            out[1, x, rows, :] = velocity[1, x, rows, :] + by_ * (dx(xy, -1) + dy(yy, 0) + dz(yz, -1))
            out[2, x, rows, :] = velocity[2, x, rows, :] + bz_ * (dx(xz, -1) + dy(yz, -1) + dz(zz, 0))

    def down():
        items = planes([(out, 0, 0), (out, 1, 0), (out, 1, 1), (out, 2, 0), (out, 2, 1)])
        if step == 0:
            start = sum(value.shape[0] for _, value in items)
            items.append((pl.ds(start, 1), high_y[pl.ds(5, 1), :]))
        return items

    Pack(pax, pbx, even_x).put(
        lambda: planes([(out, 0, nx - 2), (out, 0, nx - 1), (out, 1, nx - 1), (out, 2, nx - 1)]), down)
    Pack(pay, pby, even_y).put(
        lambda: rows_of([(out, 1, ny - 2, 2), (out, 0, ny - 1, 1), (out, 2, ny - 1, 1)], nx),
        lambda: rows_of([(out, 1, 0, 1), (out, 0, 0, 2), (out, 2, 0, 2)], nx),
    )


def stress_kernel(step, *refs):
    if step == 0:
        (velocity, stress, lam, shear, recips, halo_c, edge_c, ax, bx, ay, by,
         out, pax, pbx, pay, pby, shears, low_x, high_x, low_y, high_y, edges, corner) = refs
    else:
        (velocity, stress, lam, shear, shears, ax, bx, ay, by,
         out, low_x, high_x, low_y, high_y, edges) = refs
    nx, ny = stress.shape[1], stress.shape[2]
    even_x, even_y = receive((ax, bx, ay, by), (low_x, high_x, low_y, high_y))
    fill_edges(velocity, 1, edges.at[0], low_y, high_y, 0, 2, 0, 1)
    fill_edges(velocity, 0, edges.at[1], low_y, high_y, 2, 1, 1, 2)
    fill_edges(velocity, 2, edges.at[2], low_y, high_y, 3, 1, 3, 2)
    vx = Field(velocity, 0, (low_x, 2), (high_x, 0), edges.at[1, 0], edges.at[1, 1])
    vy = Field(velocity, 1, (low_x, 3), (high_x, 1), edges.at[0, 0], edges.at[0, 1])
    vz = Field(velocity, 2, (low_x, 4), (high_x, 3), edges.at[2, 0], edges.at[2, 1])
    lane = lanes()
    if step == 0:
        corner[pl.ds(0, tile), :] = halo_c[pl.ds(ny - tile, tile), :]
        corner[pl.ds(tile, 1), :] = high_x[pl.ds(5 * ny, 1), :]

        def comp(x, t, k):
            if k == 1 and t == ny // tile - 1:
                return corner[pl.ds(1, tile), :] if x == nx else edge_c[x, pl.ds(1, tile), :]
            if x == nx:
                return halo_c[pl.ds(tile * t + k, tile), :]
            return recips[1, x, pl.ds(tile * t + k, tile), :]

    for x in range(nx):
        for t in range(ny // tile):
            rows = pl.ds(tile * t, tile)

            def dx(field, base):
                return difference(lambda k: field.at(x + k, t), base)

            def dy(field, base):
                return difference(lambda k: field.y(x, t, k), base)

            def dz(field, base):
                value = field.at(x, t)
                return difference(lambda k: z_shift(value, k, lane) if k else value, base)

            if step == 0:
                here = comp(x, t, 0)
                next_x, next_y = comp(x + 1, t, 0), comp(x, t, 1)
                pair_x, pair_y = here + next_x, here + next_y
                four = 4.0 * time_step
                mxy = four / (pair_x + (next_y + comp(x + 1, t, 1)))
                mxz = four / (pair_x + z_shift(pair_x, 1, lane))
                myz = four / (pair_y + z_shift(pair_y, 1, lane))
                shears[0, x, rows, :] = mxy
                shears[1, x, rows, :] = mxz
                shears[2, x, rows, :] = myz
            else:
                mxy, mxz, myz = (shears[c, x, rows, :] for c in range(3))
            exx, eyy, ezz = dx(vx, -1), dy(vy, -1), dz(vz, -1)
            la = time_step * lam[x, rows, :]
            two = (2.0 * time_step) * shear[x, rows, :]
            common = la * (exx + eyy + ezz)
            out[0, x, rows, :] = stress[0, x, rows, :] + (common + two * exx)
            out[1, x, rows, :] = stress[1, x, rows, :] + (common + two * eyy)
            out[2, x, rows, :] = stress[2, x, rows, :] + (common + two * ezz)
            out[3, x, rows, :] = stress[3, x, rows, :] + mxy * (dy(vx, 0) + dx(vy, 0))
            out[4, x, rows, :] = stress[4, x, rows, :] + mxz * (dz(vx, 0) + dx(vz, 0))
            out[5, x, rows, :] = stress[5, x, rows, :] + myz * (dz(vy, 0) + dy(vz, 0))
    if step == 0:
        Pack(pax, pbx, even_x).put(
            lambda: planes([(out, 3, nx - 2), (out, 3, nx - 1), (out, 4, nx - 2), (out, 4, nx - 1), (out, 0, nx - 1)]),
            lambda: planes([(out, 3, 0), (out, 4, 0), (out, 0, 0), (out, 0, 1)]),
        )
        Pack(pay, pby, even_y).put(
            lambda: rows_of([(out, 3, ny - 2, 2), (out, 5, ny - 2, 2), (out, 1, ny - 1, 1)], nx),
            lambda: rows_of([(out, 3, 0, 1), (out, 5, 0, 1), (out, 1, 0, 2)], nx),
        )


def compliance_kernel(recips, ax, ay_in, by_in, bx, halo_c, edge_c):
    i, j, even_x, even_y = position()
    first_x, last_x, first_y, last_y = sides(i, j)
    nx, ny = recips.shape[1], recips.shape[2]
    for t in range(ny // tile):
        rows = pl.ds(5 * ny + tile * t, tile)
        halo_c[pl.ds(tile * t, tile), :] = jnp.where(last_x, 0.0, jnp.where(even_x, ax[rows, :], bx[rows, :]))
    for x in range(nx):
        edge_c[x, pl.ds(0, tile), :] = recips[1, x, pl.ds(ny - tile, tile), :]
        row = pl.ds(tile * x + 5, 1)
        edge_c[x, pl.ds(tile, 1), :] = jnp.where(last_y, 0.0, jnp.where(even_y, ay_in[row, :], by_in[row, :]))


def call(kernel, outs, scratch, args, flops):
    vmem = pl.BlockSpec(memory_space=pltpu.VMEM)
    return pl.pallas_call(
        kernel,
        out_shape=[jax.ShapeDtypeStruct(shape, jnp.float32) for shape in outs],
        in_specs=[vmem] * len(args),
        out_specs=[vmem] * len(outs),
        scratch_shapes=[pltpu.VMEM(shape, jnp.float32) for shape in scratch],
        compiler_params=pltpu.CompilerParams(vmem_limit_bytes=16 * 1024 * 1024),
        cost_estimate=pl.CostEstimate(flops=flops, bytes_accessed=2 * 1024 * 1024, transcendentals=0),
    )(*args)


def per_device(velocity, stress, density, lame_lambda, lame_mu):
    _, nx, ny, nz = velocity.shape
    routes = pairings(lax.axis_size("gx"), lax.axis_size("gy"))
    cells = nx * ny * nz

    def packages(x_rows):
        return [(x_rows, nz)] * 2 + [(nx * tile, nz)] * 2

    def exchange(arrays):
        return [lax.ppermute(array, AXES, route) for array, route in zip(arrays, routes)]

    def scratch(x_rows):
        return packages(x_rows) + [(3, 2, nx, 2 * tile, nz)]

    first, second, later = 6 * ny, 5 * ny + tile, 5 * ny
    *packed, recips = call(
        first_pack, packages(first) + [(2, nx, ny, nz)], [], (stress, density, lame_mu), 10 * cells)
    got = exchange(packed)
    velocity, *packed, buoys = call(
        lambda *refs: velocity_kernel(0, *refs),
        [velocity.shape] + packages(second) + [(3, nx, ny, nz)],
        scratch(first) + [(2, nx, 2 * tile, nz)],
        (velocity, stress, recips, *got), 60 * cells)
    halo_c, edge_c = call(
        lambda ax, bx, ay, by, recips, halo, edge: compliance_kernel(recips, ax, ay, by, bx, halo, edge),
        [(ny, nz), (nx, 2 * tile, nz)], [], (*got, recips), cells)
    got = exchange(packed)
    stress, *packed, shears = call(
        lambda *refs: stress_kernel(0, *refs),
        [stress.shape] + packages(later) + [(3, nx, ny, nz)],
        scratch(second) + [(2 * tile, nz)],
        (velocity, stress, lame_lambda, lame_mu, recips, halo_c, edge_c, *got), 80 * cells)
    got = exchange(packed)
    velocity, *packed = call(
        lambda *refs: velocity_kernel(1, *refs),
        [velocity.shape] + packages(later),
        scratch(later),
        (velocity, stress, buoys, *got), 60 * cells)
    got = exchange(packed)
    (stress,) = call(
        lambda *refs: stress_kernel(1, *refs),
        [stress.shape],
        scratch(later),
        (velocity, stress, lame_lambda, lame_mu, shears, *got), 80 * cells)
    return (velocity, stress)


def solution(mesh):
    in_specs = (
        P(None, "gx", "gy", None),
        P(None, "gx", "gy", None),
        P("gx", "gy", None),
        P("gx", "gy", None),
        P("gx", "gy", None),
    )
    out_specs = (P(None, "gx", "gy", None), P(None, "gx", "gy", None))
    return jax.shard_map(
        per_device, mesh=mesh, in_specs=in_specs, out_specs=out_specs, check_vma=False
    )
```

time: 99.3 us -> 36.1 us (0.36)
  the two profiles are of different devices: /device:TPU:1 before, /device:TPU:0 now
where the time goes in v1:
time: 36.1 us; the launch traced here: 35.8 us
  starting transfers between devices  16.7 us (46%)
  waiting for transfers between devices  10.6 us (29%)
  local copies, waits for them, and re-layouts  3.94 us (11%)
  Pallas kernels  3.8 us (11%)
  between operations  0.72 us (2%)
    ppermute x16, starting transfers between devices, exchange(): lax.ppermute(array, AXES, route)  16.7 us
    ppermute x16, waiting for transfers between devices, exchange(): lax.ppermute(array, AXES, route)  10.6 us
    unnamed x14, local copies, waits for them, and re-layouts  3.94 us
    pallas_call x6, Pallas kernels, call(): pl.pallas_call(kernel, out_shape=[jax.ShapeDtypeStruct(shape, jnp.float32...  3.8 us
  transfers between devices with their start and end apart: 16, of which 4 were waited for; matrix products, arithmetic and copies ran while one was open for 0% of the time, Pallas kernels for 0%

profile of v1, /device:TPU:0, one launch (start us, length us, event | category | flops | bytes accessed | tf_op | source)
XLA Modules:
  0.0 35.8 jit_solution(14132521722145324718)
XLA Ops:
  0.6 0.0 copy-start
  0.6 1.1 %copy-done = f32[6,8,32,128]{3,2,1,0:T(8,128)S(1)} copy-done((f32[6,8,32,128]{3,2,1,0:T(8,128)S(1)}, f32[6,8,32,128]{3,2,1,0:T(8,128)}, u32[]{:S(2)}) %copy-start) | copy-done | bytes 786456
  1.8 0.0 copy-start.2
  1.8 0.9 %copy-done.2 = f32[8,32,128]{2,1,0:T(8,128)S(1)} copy-done((f32[8,32,128]{2,1,0:T(8,128)S(1)}, f32[8,32,128]{2,1,0:T(8,128)}, u32[]{:S(2)}) %copy-start.2) | copy-done | bytes 131096
  2.7 0.0 copy-start.6
  2.7 0.9 %copy-done.6 = f32[8,32,128]{2,1,0:T(8,128)S(1)} copy-done((f32[8,32,128]{2,1,0:T(8,128)S(1)}, f32[8,32,128]{2,1,0:T(8,128)}, u32[]{:S(2)}) %copy-start.6) | copy-done | bytes 131096
  3.6 0.1 shard_map.68
  3.7 3.0 %collective-permute-start = (f32[192,128]{1,0:T(8,128)S(1)}, f32[192,128]{1,0:T(8,128)S(1)}, u32[]{:S(2)}, u32[]{:S(2)}) collective-permute-start(f32[192,128]{1,0:T(8,128)S(1)} %get-tuple-element.27), channel_id=1, source_target_pairs={{0,8},{1,9},{2,10},{3,11},{4,12},{5,13},{6,14},{7,15},{8,0},{9,1},... | collective-permute-start | bytes 294920 | tf_op jit(solution)/shard_map/ppermute | solution.py:359
  6.7 0.0 collective-permute-start.1
  6.7 0.5 %collective-permute-start.2 = (f32[64,128]{1,0:T(8,128)S(1)}, f32[64,128]{1,0:T(8,128)S(1)}, u32[]{:S(2)}, u32[]{:S(2)}) collective-permute-start(f32[64,128]{1,0:T(8,128)S(1)} %get-tuple-element.29), channel_id=1, source_target_pairs={{0,1},{1,0},{2,3},{3,2},{4,5},{5,4},{6,7},{7,6},{8,9},{9,8},{10,11... | collective-permute-start | bytes 98312 | tf_op jit(solution)/shard_map/ppermute | solution.py:359
  7.2 1.0 %collective-permute-start.3 = (f32[64,128]{1,0:T(8,128)S(1)}, f32[64,128]{1,0:T(8,128)S(1)}, u32[]{:S(2)}, u32[]{:S(2)}) collective-permute-start(f32[64,128]{1,0:T(8,128)S(1)} %get-tuple-element.30), channel_id=1, source_target_pairs={{0,16},{1,2},{2,1},{3,4},{4,3},{5,6},{6,5},{7,23},{8,24},{9,10},{1... | collective-permute-start | bytes 98312 | tf_op jit(solution)/shard_map/ppermute | solution.py:359
  8.2 0.0 collective-permute-done.2.refs_5_.ay
  8.2 2.9 %collective-permute-done.3.refs_6_.by = f32[64,128]{1,0:T(8,128)S(1)} collective-permute-done((f32[64,128]{1,0:T(8,128)S(1)}, f32[64,128]{1,0:T(8,128)S(1)}, u32[]{:S(2)}, u32[]{:S(2)}) %collective-permute-start.3) | collective-permute-done | bytes 32800 | tf_op jit(solution)/shard_map/ppermute | solution.py:359
  11.1 0.0 collective-permute-done.refs_3_.ax
  11.1 0.0 collective-permute-done.1.refs_4_.bx
  11.1 0.0 copy-done.4
  11.1 0.0 copy-start.1
  11.1 0.5 %shard_map.69 = (f32[3,8,32,128]{3,2,1,0:T(8,128)S(1)}, f32[168,128]{1,0:T(8,128)S(1)}, f32[168,128]{1,0:T(8,128)S(1)}, f32[64,128]{1,0:T(8,128)S(1)}, f32[64,12...) custom-call(f32[3,8,32,128]{3,2,1,0:T(8,128)S(1)} %copy-done.4, f32[6,8,32,128]{3,2,1,0:T(8,128)S(1)} %copy-done, ...), custom_call_target="tpu_custom_call" | custom-call | flops 1966080 | bytes 2097152 | tf_op jit(solution)/shard_map/pallas_call | solution.py:339
  11.6 3.6 %collective-permute-start.4 = (f32[168,128]{1,0:T(8,128)S(1)}, f32[168,128]{1,0:T(8,128)S(1)}, u32[]{:S(2)}, u32[]{:S(2)}) collective-permute-start(f32[168,128]{1,0:T(8,128)S(1)} %get-tuple-element.34), channel_id=1, source_target_pairs={{0,8},{1,9},{2,10},{3,11},{4,12},{5,13},{6,14},{7,15},{8,0},{9,1},... | collective-permute-start | bytes 258056 | tf_op jit(solution)/shard_map/ppermute | solution.py:359
  15.2 0.0 collective-permute-start.5
  15.2 0.5 %collective-permute-start.6 = (f32[64,128]{1,0:T(8,128)S(1)}, f32[64,128]{1,0:T(8,128)S(1)}, u32[]{:S(2)}, u32[]{:S(2)}) collective-permute-start(f32[64,128]{1,0:T(8,128)S(1)} %get-tuple-element.36), channel_id=1, source_target_pairs={{0,1},{1,0},{2,3},{3,2},{4,5},{5,4},{6,7},{7,6},{8,9},{9,8},{10,11... | collective-permute-start | bytes 98312 | tf_op jit(solution)/shard_map/ppermute | solution.py:359
  15.7 1.0 %collective-permute-start.7 = (f32[64,128]{1,0:T(8,128)S(1)}, f32[64,128]{1,0:T(8,128)S(1)}, u32[]{:S(2)}, u32[]{:S(2)}) collective-permute-start(f32[64,128]{1,0:T(8,128)S(1)} %get-tuple-element.37), channel_id=1, source_target_pairs={{0,16},{1,2},{2,1},{3,4},{4,3},{5,6},{6,5},{7,23},{8,24},{9,10},{1... | collective-permute-start | bytes 98312 | tf_op jit(solution)/shard_map/ppermute | solution.py:359
  16.8 0.0 collective-permute-done.6.refs_9_
  16.8 2.9 %collective-permute-done.7.refs_10_ = f32[64,128]{1,0:T(8,128)S(1)} collective-permute-done((f32[64,128]{1,0:T(8,128)S(1)}, f32[64,128]{1,0:T(8,128)S(1)}, u32[]{:S(2)}, u32[]{:S(2)}) %collective-permute-start.7) | collective-permute-done | bytes 32800 | tf_op jit(solution)/shard_map/ppermute | solution.py:359
  19.7 0.0 collective-permute-done.4.refs_7_
  19.7 0.0 collective-permute-done.5.refs_8_
  19.7 0.0 copy-done.1
  19.7 0.0 copy-done.3
  19.7 0.6 %shard_map.71 = (f32[6,8,32,128]{3,2,1,0:T(8,128)S(1)}, f32[160,128]{1,0:T(8,128)S(1)}, f32[160,128]{1,0:T(8,128)S(1)}, f32[64,128]{1,0:T(8,128)S(1)}, f32[64,12...) custom-call(f32[3,8,32,128]{3,2,1,0:T(8,128)S(1)} %get-tuple-element.31.refs_0_, f32[6,8,32,128]{3,2,1,0:T(8,128)S(1)} %copy-done.1, ...), custom_call_target="tpu_custom_call" | custom-call | flops 2621440 | bytes 2097152 | tf_op jit(solution)/shard_map/pallas_call | solution.py:339
  20.3 1.5 %collective-permute-start.8 = (f32[160,128]{1,0:T(8,128)S(1)}, f32[160,128]{1,0:T(8,128)S(1)}, u32[]{:S(2)}, u32[]{:S(2)}) collective-permute-start(f32[160,128]{1,0:T(8,128)S(1)} %get-tuple-element.40), channel_id=1, source_target_pairs={{0,8},{1,9},{2,10},{3,11},{4,12},{5,13},{6,14},{7,15},{8,0},{9,1},... | collective-permute-start | bytes 245768 | tf_op jit(solution)/shard_map/ppermute | solution.py:359
  21.8 0.0 collective-permute-start.9
  21.8 0.5 %collective-permute-start.10 = (f32[64,128]{1,0:T(8,128)S(1)}, f32[64,128]{1,0:T(8,128)S(1)}, u32[]{:S(2)}, u32[]{:S(2)}) collective-permute-start(f32[64,128]{1,0:T(8,128)S(1)} %get-tuple-element.42), channel_id=1, source_target_pairs={{0,1},{1,0},{2,3},{3,2},{4,5},{5,4},{6,7},{7,6},{8,9},{9,8},{10,11... | collective-permute-start | bytes 98312 | tf_op jit(solution)/shard_map/ppermute | solution.py:359
  22.3 1.6 %collective-permute-start.11 = (f32[64,128]{1,0:T(8,128)S(1)}, f32[64,128]{1,0:T(8,128)S(1)}, u32[]{:S(2)}, u32[]{:S(2)}) collective-permute-start(f32[64,128]{1,0:T(8,128)S(1)} %get-tuple-element.43), channel_id=1, source_target_pairs={{0,16},{1,2},{2,1},{3,4},{4,3},{5,6},{6,5},{7,23},{8,24},{9,10},{1... | collective-permute-start | bytes 98312 | tf_op jit(solution)/shard_map/ppermute | solution.py:359
  23.9 0.0 collective-permute-done.10.refs_5_
  23.9 2.3 %collective-permute-done.11.refs_6_ = f32[64,128]{1,0:T(8,128)S(1)} collective-permute-done((f32[64,128]{1,0:T(8,128)S(1)}, f32[64,128]{1,0:T(8,128)S(1)}, u32[]{:S(2)}, u32[]{:S(2)}) %collective-permute-start.11) | collective-permute-done | bytes 32800 | tf_op jit(solution)/shard_map/ppermute | solution.py:359
  26.2 0.0 collective-permute-done.8.refs_3_
  26.2 0.0 collective-permute-done.9.refs_4_
  26.2 1.2 %shard_map.72 = (f32[3,8,32,128]{3,2,1,0:T(8,128)}, f32[160,128]{1,0:T(8,128)S(1)}, f32[160,128]{1,0:T(8,128)S(1)}, f32[64,128]{1,0:T(8,128)S(1)}, f32[64,128]{1,0:T(8,128)S(1)}) custom-call(f32[3,8,32,128]{3,2,1,0:T(8,128)S(1)} %get-tuple-element.31.refs_0_, f32[6,8,32,128]{3,2,1,0:T(8,128)S(1)} %get-tuple-element.38.refs_1_, ...), custom_call_target="tpu_custom_call" | custom-call | flops 1966080 | bytes 2097152 | tf_op jit(solution)/shard_map/pallas_call | solution.py:339
  27.4 1.6 %collective-permute-start.12 = (f32[160,128]{1,0:T(8,128)S(1)}, f32[160,128]{1,0:T(8,128)S(1)}, u32[]{:S(2)}, u32[]{:S(2)}) collective-permute-start(f32[160,128]{1,0:T(8,128)S(1)} %get-tuple-element.46), channel_id=1, source_target_pairs={{0,8},{1,9},{2,10},{3,11},{4,12},{5,13},{6,14},{7,15},{8,0},{9,1},... | collective-permute-start | bytes 245768 | tf_op jit(solution)/shard_map/ppermute | solution.py:359
  29.0 0.0 collective-permute-start.13
  29.0 0.5 %collective-permute-start.14 = (f32[64,128]{1,0:T(8,128)S(1)}, f32[64,128]{1,0:T(8,128)S(1)}, u32[]{:S(2)}, u32[]{:S(2)}) collective-permute-start(f32[64,128]{1,0:T(8,128)S(1)} %get-tuple-element.48), channel_id=1, source_target_pairs={{0,1},{1,0},{2,3},{3,2},{4,5},{5,4},{6,7},{7,6},{8,9},{9,8},{10,11... | collective-permute-start | bytes 98312 | tf_op jit(solution)/shard_map/ppermute | solution.py:359
  29.5 1.4 %collective-permute-start.15 = (f32[64,128]{1,0:T(8,128)S(1)}, f32[64,128]{1,0:T(8,128)S(1)}, u32[]{:S(2)}, u32[]{:S(2)}) collective-permute-start(f32[64,128]{1,0:T(8,128)S(1)} %get-tuple-element.49), channel_id=1, source_target_pairs={{0,16},{1,2},{2,1},{3,4},{4,3},{5,6},{6,5},{7,23},{8,24},{9,10},{1... | collective-permute-start | bytes 98312 | tf_op jit(solution)/shard_map/ppermute | solution.py:359
  30.9 0.0 collective-permute-done.14.refs_7_
  30.9 2.5 %collective-permute-done.15.refs_8_ = f32[64,128]{1,0:T(8,128)S(1)} collective-permute-done((f32[64,128]{1,0:T(8,128)S(1)}, f32[64,128]{1,0:T(8,128)S(1)}, u32[]{:S(2)}, u32[]{:S(2)}) %collective-permute-start.15) | collective-permute-done | bytes 32800 | tf_op jit(solution)/shard_map/ppermute | solution.py:359
  33.4 0.0 collective-permute-done.12.refs_5_
  33.5 0.0 collective-permute-done.13.refs_6_
  33.5 1.0 %copy-done.5 = f32[3,8,32,128]{3,2,1,0:T(8,128)S(1)} copy-done((f32[3,8,32,128]{3,2,1,0:T(8,128)S(1)}, f32[3,8,32,128]{3,2,1,0:T(8,128)}, u32[]{:S(2)}) %copy-start.5) | copy-done | bytes 393240
  34.5 1.4 %shard_map.73 = f32[6,8,32,128]{3,2,1,0:T(8,128)} custom-call(f32[3,8,32,128]{3,2,1,0:T(8,128)S(1)} %copy-done.5, f32[6,8,32,128]{3,2,1,0:T(8,128)S(1)} %get-tuple-element.38.refs_1_, f32[8,32,128]{2,1,0:T(8,128)S(1)} %copy-done.3, f32[8,32,128]{2,1,0:T(8,128)S(1)} %copy-done.2, f32[3,8,32,128]{3,2,1,0:T(8,128)S(1)} %get-tuple-element.45.refs_4_, ...), custom_call_target="tpu_custom_call" | custom-call | flops 2621440 | bytes 2097152 | tf_op jit(solution)/shard_map/pallas_call | solution.py:339
  (4 shorter events, 0.0 us)
Async XLA Ops:
  0.6 1.1 %copy-start = (f32[6,8,32,128]{3,2,1,0:T(8,128)S(1)}, f32[6,8,32,128]{3,2,1,0:T(8,128)}, u32[]{:S(2)}) copy-start(f32[6,8,32,128]{3,2,1,0:T(8,128)} %refs_1_.3) | copy-start | bytes 2359300
  1.8 0.9 %copy-start.2 = (f32[8,32,128]{2,1,0:T(8,128)S(1)}, f32[8,32,128]{2,1,0:T(8,128)}, u32[]{:S(2)}) copy-start(f32[8,32,128]{2,1,0:T(8,128)} %refs_3_.3) | copy-start | bytes 393220
  2.7 0.9 %copy-start.6 = (f32[8,32,128]{2,1,0:T(8,128)S(1)}, f32[8,32,128]{2,1,0:T(8,128)}, u32[]{:S(2)}) copy-start(f32[8,32,128]{2,1,0:T(8,128)} %density.1) | copy-start | bytes 393220
  3.6 7.5 %copy-start.4 = (f32[3,8,32,128]{3,2,1,0:T(8,128)S(1)}, f32[3,8,32,128]{3,2,1,0:T(8,128)}, u32[]{:S(2)}) copy-start(f32[3,8,32,128]{3,2,1,0:T(8,128)} %refs_0_.1) | copy-start | bytes 1179652
  3.7 7.4 %collective-permute-start = (f32[192,128]{1,0:T(8,128)S(1)}, f32[192,128]{1,0:T(8,128)S(1)}, u32[]{:S(2)}, u32[]{:S(2)}) collective-permute-start(f32[192,128]{1,0:T(8,128)S(1)} %get-tuple-element.27), channel_id=1, source_target_pairs={{0,8},{1,9},{2,10},{3,11},{4,12},{5,13},{6,14},{7,15},{8,0},{9,1},... | collective-permute-start | bytes 294920 | tf_op jit(solution)/shard_map/ppermute | solution.py:359
  6.7 4.4 %collective-permute-start.1 = (f32[192,128]{1,0:T(8,128)S(1)}, f32[192,128]{1,0:T(8,128)S(1)}, u32[]{:S(2)}, u32[]{:S(2)}) collective-permute-start(f32[192,128]{1,0:T(8,128)S(1)} %get-tuple-element.28), channel_id=1, source_target_pairs={{0,1},{1,0},{2,3},{3,2},{4,5},{5,4},{6,7},{7,6},{8,16},{9,17},{10,... | collective-permute-start | bytes 294920 | tf_op jit(solution)/shard_map/ppermute | solution.py:359
  6.7 1.5 %collective-permute-start.2 = (f32[64,128]{1,0:T(8,128)S(1)}, f32[64,128]{1,0:T(8,128)S(1)}, u32[]{:S(2)}, u32[]{:S(2)}) collective-permute-start(f32[64,128]{1,0:T(8,128)S(1)} %get-tuple-element.29), channel_id=1, source_target_pairs={{0,1},{1,0},{2,3},{3,2},{4,5},{5,4},{6,7},{7,6},{8,9},{9,8},{10,11... | collective-permute-start | bytes 98312 | tf_op jit(solution)/shard_map/ppermute | solution.py:359
  7.2 3.9 %collective-permute-start.3 = (f32[64,128]{1,0:T(8,128)S(1)}, f32[64,128]{1,0:T(8,128)S(1)}, u32[]{:S(2)}, u32[]{:S(2)}) collective-permute-start(f32[64,128]{1,0:T(8,128)S(1)} %get-tuple-element.30), channel_id=1, source_target_pairs={{0,16},{1,2},{2,1},{3,4},{4,3},{5,6},{6,5},{7,23},{8,24},{9,10},{1... | collective-permute-start | bytes 98312 | tf_op jit(solution)/shard_map/ppermute | solution.py:359
  11.1 8.6 %copy-start.1 = (f32[6,8,32,128]{3,2,1,0:T(8,128)S(1)}, f32[6,8,32,128]{3,2,1,0:T(8,128)}, u32[]{:S(2)}) copy-start(f32[6,8,32,128]{3,2,1,0:T(8,128)} %refs_1_.3) | copy-start | bytes 2359300
  11.6 8.0 %collective-permute-start.4 = (f32[168,128]{1,0:T(8,128)S(1)}, f32[168,128]{1,0:T(8,128)S(1)}, u32[]{:S(2)}, u32[]{:S(2)}) collective-permute-start(f32[168,128]{1,0:T(8,128)S(1)} %get-tuple-element.34), channel_id=1, source_target_pairs={{0,8},{1,9},{2,10},{3,11},{4,12},{5,13},{6,14},{7,15},{8,0},{9,1},... | collective-permute-start | bytes 258056 | tf_op jit(solution)/shard_map/ppermute | solution.py:359
  15.2 4.4 %collective-permute-start.5 = (f32[168,128]{1,0:T(8,128)S(1)}, f32[168,128]{1,0:T(8,128)S(1)}, u32[]{:S(2)}, u32[]{:S(2)}) collective-permute-start(f32[168,128]{1,0:T(8,128)S(1)} %get-tuple-element.35), channel_id=1, source_target_pairs={{0,1},{1,0},{2,3},{3,2},{4,5},{5,4},{6,7},{7,6},{8,16},{9,17},{10,... | collective-permute-start | bytes 258056 | tf_op jit(solution)/shard_map/ppermute | solution.py:359
  15.2 1.6 %collective-permute-start.6 = (f32[64,128]{1,0:T(8,128)S(1)}, f32[64,128]{1,0:T(8,128)S(1)}, u32[]{:S(2)}, u32[]{:S(2)}) collective-permute-start(f32[64,128]{1,0:T(8,128)S(1)} %get-tuple-element.36), channel_id=1, source_target_pairs={{0,1},{1,0},{2,3},{3,2},{4,5},{5,4},{6,7},{7,6},{8,9},{9,8},{10,11... | collective-permute-start | bytes 98312 | tf_op jit(solution)/shard_map/ppermute | solution.py:359
  15.7 3.9 %copy-start.3 = (f32[8,32,128]{2,1,0:T(8,128)S(1)}, f32[8,32,128]{2,1,0:T(8,128)}, u32[]{:S(2)}) copy-start(f32[8,32,128]{2,1,0:T(8,128)} %refs_2_.3) | copy-start | bytes 393220
  15.7 3.9 %collective-permute-start.7 = (f32[64,128]{1,0:T(8,128)S(1)}, f32[64,128]{1,0:T(8,128)S(1)}, u32[]{:S(2)}, u32[]{:S(2)}) collective-permute-start(f32[64,128]{1,0:T(8,128)S(1)} %get-tuple-element.37), channel_id=1, source_target_pairs={{0,16},{1,2},{2,1},{3,4},{4,3},{5,6},{6,5},{7,23},{8,24},{9,10},{1... | collective-permute-start | bytes 98312 | tf_op jit(solution)/shard_map/ppermute | solution.py:359
  20.3 5.9 %collective-permute-start.8 = (f32[160,128]{1,0:T(8,128)S(1)}, f32[160,128]{1,0:T(8,128)S(1)}, u32[]{:S(2)}, u32[]{:S(2)}) collective-permute-start(f32[160,128]{1,0:T(8,128)S(1)} %get-tuple-element.40), channel_id=1, source_target_pairs={{0,8},{1,9},{2,10},{3,11},{4,12},{5,13},{6,14},{7,15},{8,0},{9,1},... | collective-permute-start | bytes 245768 | tf_op jit(solution)/shard_map/ppermute | solution.py:359
  21.8 4.4 %collective-permute-start.9 = (f32[160,128]{1,0:T(8,128)S(1)}, f32[160,128]{1,0:T(8,128)S(1)}, u32[]{:S(2)}, u32[]{:S(2)}) collective-permute-start(f32[160,128]{1,0:T(8,128)S(1)} %get-tuple-element.41), channel_id=1, source_target_pairs={{0,1},{1,0},{2,3},{3,2},{4,5},{5,4},{6,7},{7,6},{8,16},{9,17},{10,... | collective-permute-start | bytes 245768 | tf_op jit(solution)/shard_map/ppermute | solution.py:359
  21.8 2.1 %collective-permute-start.10 = (f32[64,128]{1,0:T(8,128)S(1)}, f32[64,128]{1,0:T(8,128)S(1)}, u32[]{:S(2)}, u32[]{:S(2)}) collective-permute-start(f32[64,128]{1,0:T(8,128)S(1)} %get-tuple-element.42), channel_id=1, source_target_pairs={{0,1},{1,0},{2,3},{3,2},{4,5},{5,4},{6,7},{7,6},{8,9},{9,8},{10,11... | collective-permute-start | bytes 98312 | tf_op jit(solution)/shard_map/ppermute | solution.py:359
  22.3 3.9 %collective-permute-start.11 = (f32[64,128]{1,0:T(8,128)S(1)}, f32[64,128]{1,0:T(8,128)S(1)}, u32[]{:S(2)}, u32[]{:S(2)}) collective-permute-start(f32[64,128]{1,0:T(8,128)S(1)} %get-tuple-element.43), channel_id=1, source_target_pairs={{0,16},{1,2},{2,1},{3,4},{4,3},{5,6},{6,5},{7,23},{8,24},{9,10},{1... | collective-permute-start | bytes 98312 | tf_op jit(solution)/shard_map/ppermute | solution.py:359
  27.4 6.0 %collective-permute-start.12 = (f32[160,128]{1,0:T(8,128)S(1)}, f32[160,128]{1,0:T(8,128)S(1)}, u32[]{:S(2)}, u32[]{:S(2)}) collective-permute-start(f32[160,128]{1,0:T(8,128)S(1)} %get-tuple-element.46), channel_id=1, source_target_pairs={{0,8},{1,9},{2,10},{3,11},{4,12},{5,13},{6,14},{7,15},{8,0},{9,1},... | collective-permute-start | bytes 245768 | tf_op jit(solution)/shard_map/ppermute | solution.py:359
  29.0 4.4 %collective-permute-start.13 = (f32[160,128]{1,0:T(8,128)S(1)}, f32[160,128]{1,0:T(8,128)S(1)}, u32[]{:S(2)}, u32[]{:S(2)}) collective-permute-start(f32[160,128]{1,0:T(8,128)S(1)} %get-tuple-element.47), channel_id=1, source_target_pairs={{0,1},{1,0},{2,3},{3,2},{4,5},{5,4},{6,7},{7,6},{8,16},{9,17},{10,... | collective-permute-start | bytes 245768 | tf_op jit(solution)/shard_map/ppermute | solution.py:359
  29.0 1.9 %collective-permute-start.14 = (f32[64,128]{1,0:T(8,128)S(1)}, f32[64,128]{1,0:T(8,128)S(1)}, u32[]{:S(2)}, u32[]{:S(2)}) collective-permute-start(f32[64,128]{1,0:T(8,128)S(1)} %get-tuple-element.48), channel_id=1, source_target_pairs={{0,1},{1,0},{2,3},{3,2},{4,5},{5,4},{6,7},{7,6},{8,9},{9,8},{10,11... | collective-permute-start | bytes 98312 | tf_op jit(solution)/shard_map/ppermute | solution.py:359
  29.5 3.9 %collective-permute-start.15 = (f32[64,128]{1,0:T(8,128)S(1)}, f32[64,128]{1,0:T(8,128)S(1)}, u32[]{:S(2)}, u32[]{:S(2)}) collective-permute-start(f32[64,128]{1,0:T(8,128)S(1)} %get-tuple-element.49), channel_id=1, source_target_pairs={{0,16},{1,2},{2,1},{3,4},{4,3},{5,6},{6,5},{7,23},{8,24},{9,10},{1... | collective-permute-start | bytes 98312 | tf_op jit(solution)/shard_map/ppermute | solution.py:359
  33.5 1.0 %copy-start.5 = (f32[3,8,32,128]{3,2,1,0:T(8,128)S(1)}, f32[3,8,32,128]{3,2,1,0:T(8,128)}, u32[]{:S(2)}) copy-start(f32[3,8,32,128]{3,2,1,0:T(8,128)} %get-tuple-element.24.refs_0_) | copy-start | bytes 1179652

commit v2 on v1

v2 whole, which is shorter than its diff:
```python
import jax
import jax.numpy as jnp
from jax import lax
from jax.experimental import pallas as pl
from jax.experimental.pallas import tpu as pltpu
from jax.sharding import PartitionSpec as P

near = 9.0 / 8.0
far = 1.0 / 24.0
time_step = 0.25
tile = 8
AXES = ("gx", "gy")


def pairings(count_x, count_y):
    other = 2 if count_x % 4 == 0 else 1

    def across(i, count):
        return ((i + 1) ^ 1) - 1

    def route(rule):
        pairs = []
        for i in range(count_x):
            for j in range(count_y):
                ti, tj = rule(i, j)
                pairs.append((i * count_y + j, ti * count_y + tj))
        return pairs

    def inner_x(i, j):
        return (i ^ 1, j)

    def outer_x(i, j):
        return (across(i, count_x), j) if 0 < i < count_x - 1 else (i, j ^ 1)

    def inner_y(i, j):
        return (i, j ^ 1)

    def outer_y(i, j):
        return (i, across(j, count_y)) if 0 < j < count_y - 1 else (i ^ other, j)

    return [route(rule) for rule in (inner_x, outer_x, inner_y, outer_y)]


def position():
    i, j = lax.axis_index("gx"), lax.axis_index("gy")
    return i, j, lax.rem(i, 2) == 0, lax.rem(j, 2) == 0


def unpack(inner, outer, low, high, even, first, last):
    for start in range(0, inner.shape[0], tile):
        rows = pl.ds(start, tile)
        a, b = inner[rows, :], outer[rows, :]
        low[rows, :] = jnp.where(first, 0.0, jnp.where(even, b, a))
        high[rows, :] = jnp.where(last, 0.0, jnp.where(even, a, b))


class Pack:
    def __init__(self, inner, outer, even):
        self.inner, self.outer, self.even = inner, outer, even

    def put(self, up, down):
        even, inner, outer = self.even, self.inner, self.outer

        @pl.when(even)
        def _():
            up(inner)
            down(outer)

        @pl.when(jnp.logical_not(even))
        def _():
            up(outer)
            down(inner)


def put_planes(items):
    def put(out):
        start = 0
        for ref, f, x in items:
            value = ref[f, x]
            out[pl.ds(start, value.shape[0]), :] = value
            start += value.shape[0]

    return put


def put_rows(items, count_x):
    def put(out):
        for x in range(count_x):
            start = tile * x
            for ref, f, row, count in items:
                out[pl.ds(start, count), :] = ref[f, x, pl.ds(row, count), :]
                start += count

    return put


def sides(i, j):
    return i == 0, i == lax.axis_size("gx") - 1, j == 0, j == lax.axis_size("gy") - 1


def lanes():
    return lax.broadcasted_iota(jnp.int32, (tile, 128), 1)


def z_shift(value, k, lane):
    size = value.shape[-1]
    moved = pltpu.roll(value, (-k) % size, 1)
    inside = lane < size - k if k > 0 else lane >= -k
    return jnp.where(inside, moved, 0.0)


def difference(at, base):
    return near * (at(base + 1) - at(base)) - far * (at(base + 2) - at(base - 1))


class Field:
    def __init__(self, ref, f, low_x=None, high_x=None, edge=None):
        self.ref, self.f = ref, f
        self.low_x, self.high_x, self.edge = low_x, high_x, edge

    def at(self, x, t):
        nx, ny = self.ref.shape[-3], self.ref.shape[-2]
        if x < 0:
            ref, index = self.low_x
            return ref[pl.ds(ny * (index + x) + tile * t, tile), :]
        if x >= nx:
            ref, index = self.high_x
            return ref[pl.ds(ny * (index + x - nx) + tile * t, tile), :]
        return self.ref[self.f, x, pl.ds(tile * t, tile), :]

    def y(self, x, t, k):
        ny = self.ref.shape[-2]
        start = tile * t + k
        if start < 0:
            return self.edge[0, x, pl.ds(tile + k, tile), :]
        if start + tile > ny:
            return self.edge[1, x, pl.ds(k, tile), :]
        return self.ref[self.f, x, pl.ds(start, tile), :]


class Differences:
    def __init__(self, x, t, lane):
        self.x, self.t, self.lane = x, t, lane

    def dx(self, field, base):
        return difference(lambda k: field.at(self.x + k, self.t), base)

    def dy(self, field, base):
        return difference(lambda k: field.y(self.x, self.t, k), base)

    def dz(self, field, base):
        value = field.at(self.x, self.t)
        return difference(lambda k: z_shift(value, k, self.lane) if k else value, base)


def inner_plane(x, base, nx):
    return x + base - 1 >= 0 and x + base + 2 < nx


def inner_tile(t, ny):
    return 0 < t < ny // tile - 1


def fill_edges(ref, f, edge, lows, highs, low_row, low_count, high_row, high_count):
    nx, ny = ref.shape[-3], ref.shape[-2]
    for x in range(nx):
        if low_count:
            edge[0, x, pl.ds(tile - low_count, low_count), :] = lows[pl.ds(tile * x + low_row, low_count), :]
            edge[0, x, pl.ds(tile, tile), :] = ref[f, x, pl.ds(0, tile), :]
        if high_count:
            edge[1, x, pl.ds(0, tile), :] = ref[f, x, pl.ds(ny - tile, tile), :]
            edge[1, x, pl.ds(tile, high_count), :] = highs[pl.ds(tile * x + high_row, high_count), :]


def receive(got, halos):
    i, j, even_x, even_y = position()
    ax, bx, ay, by = got
    low_x, high_x, low_y, high_y = halos
    first_x, last_x, first_y, last_y = sides(i, j)
    unpack(ax, bx, low_x, high_x, even_x, first_x, last_x)
    unpack(ay, by, low_y, high_y, even_y, first_y, last_y)
    return even_x, even_y, last_x, last_y


def first_pack(stress, density, shear, ax, bx, ay, by, tiles, sems):
    i, j, even_x, even_y = position()
    nx, ny = density.shape[0], density.shape[1]
    planes_up = [(stress, 3, nx - 2), (stress, 3, nx - 1), (stress, 4, nx - 2), (stress, 4, nx - 1), (stress, 0, nx - 1)]
    planes_down = [(stress, 3, 0), (stress, 4, 0), (stress, 0, 0), (stress, 0, 1), (density, None, 0), (shear, None, 0)]
    columns = [(stress, 3, ny - tile), (stress, 5, ny - tile), (stress, 1, ny - tile),
               (stress, 3, 0), (stress, 5, 0), (stress, 1, 0), (density, None, 0), (shear, None, 0)]

    def plane_copies(items, out, sem):
        copies = []
        for n, (ref, f, x) in enumerate(items):
            source = ref.at[x] if f is None else ref.at[f, x]
            copies.append(pltpu.make_async_copy(source, out.at[pl.ds(n * ny, ny), :], sem.at[n]))
        return copies

    copies = []
    for n, (ref, f, row) in enumerate(columns):
        source = ref if f is None else ref.at[f]
        copies.append(pltpu.make_async_copy(source.at[:, pl.ds(row, tile), :], tiles.at[n], sems.at[2, n]))
    for copy in copies:
        copy.start()

    @pl.when(even_x)
    def _():
        for copy in plane_copies(planes_up, ax, sems.at[0]) + plane_copies(planes_down, bx, sems.at[1]):
            copy.start()

    @pl.when(jnp.logical_not(even_x))
    def _():
        for copy in plane_copies(planes_up, bx, sems.at[0]) + plane_copies(planes_down, ax, sems.at[1]):
            copy.start()

    for copy in copies:
        copy.wait()
    Pack(ay, by, even_y).put(
        put_rows([(tiles, 0, tile - 2, 2), (tiles, 1, tile - 2, 2), (tiles, 2, tile - 1, 1)], nx),
        put_rows([(tiles, 3, 0, 1), (tiles, 4, 0, 1), (tiles, 5, 0, 2), (tiles, 6, 0, 1), (tiles, 7, 0, 1)], nx),
    )
    for copy in plane_copies(planes_up, ax, sems.at[0]) + plane_copies(planes_down, bx, sems.at[1]):
        copy.wait()


def velocity_terms(stress, low_x, high_x, edges):
    xx = Field(stress, 0, (low_x, 5), (high_x, 2))
    yy = Field(stress, 1, edge=edges.at[2] if edges is not None else None)
    zz = Field(stress, 2)
    xy = Field(stress, 3, (low_x, 2), (high_x, 0), edges.at[0] if edges is not None else None)
    xz = Field(stress, 4, (low_x, 4), (high_x, 1))
    yz = Field(stress, 5, edge=edges.at[1] if edges is not None else None)
    return ((xx, 0), (xy, -1), (xz, -1)), ((xy, -1), (yy, 0), (yz, -1)), ((xz, -1), (yz, -1), (zz, 0))


def velocity_inside(step, *refs):
    if step == 0:
        velocity, stress, density, out, buoy, buoys = refs
    else:
        velocity, stress, buoys, out = refs
    nx, ny = stress.shape[1], stress.shape[2]
    lane = lanes()
    terms = velocity_terms(stress, None, None, None)
    if step == 0:
        for x in range(nx):
            buoy[0, x] = 1.0 / density[x]
        buoy_field = Field(buoy, 0)
    for x in range(nx):
        for t in range(ny // tile):
            rows = pl.ds(tile * t, tile)
            d = Differences(x, t, lane)
            if step == 0:
                here = buoy_field.at(x, t)
                half = 0.5 * time_step
                if x < nx - 1:
                    buoys[0, x, rows, :] = half * (here + buoy_field.at(x + 1, t))
                if t < ny // tile - 1:
                    buoys[1, x, rows, :] = half * (here + buoy_field.y(x, t, 1))
                buoys[2, x, rows, :] = half * (here + z_shift(here, 1, lane))
            for c, ((fx, sx), (fy, sy), (fz, sz)) in enumerate(terms):
                total = d.dz(fz, sz)
                whole_x, whole_y = inner_plane(x, sx, nx), inner_tile(t, ny)
                if whole_x:
                    total += d.dx(fx, sx)
                if whole_y:
                    total += d.dy(fy, sy)
                if whole_x and whole_y:
                    total = velocity[c, x, rows, :] + buoys[c, x, rows, :] * total
                out[c, x, rows, :] = total


def velocity_edges(step, *refs):
    if step == 0:
        (velocity, stress, buoy, buoys, part, ax, bx, ay, by, out, buoys_end, pax, pbx, pay, pby,
         low_x, high_x, low_y, high_y, edges, edge_b) = refs
    else:
        (velocity, stress, buoys, buoys_end, part, ax, bx, ay, by, out, pax, pbx, pay, pby,
         low_x, high_x, low_y, high_y, edges) = refs
    nx, ny = stress.shape[1], stress.shape[2]
    even_x, even_y, last_x, last_y = receive((ax, bx, ay, by), (low_x, high_x, low_y, high_y))
    fill_edges(stress, 3, edges.at[0], low_y, high_y, 0, 2, 0, 1)
    fill_edges(stress, 5, edges.at[1], low_y, high_y, 2, 2, 1, 1)
    fill_edges(stress, 1, edges.at[2], low_y, high_y, 4, 1, 2, 2)
    terms = velocity_terms(stress, low_x, high_x, edges)
    lane = lanes()
    if step == 0:
        half = 0.5 * time_step
        for t in range(ny // tile):
            rows = pl.ds(tile * t, tile)
            above = jnp.where(last_x, 0.0, 1.0 / jnp.where(last_x, 1.0, high_x[pl.ds(4 * ny + tile * t, tile), :]))
            buoys_end[rows, :] = half * (buoy[0, nx - 1, rows, :] + above)
        rows = pl.ds(ny - tile, tile)
        for x in range(nx):
            here = buoy[0, x, rows, :]
            row = high_y[pl.ds(tile * x + 4, 1), :]
            edge_b[pl.ds(0, tile), :] = here
            edge_b[pl.ds(tile, 1), :] = jnp.where(last_y, 0.0, 1.0 / jnp.where(last_y, 1.0, row))
            buoys_end[pl.ds(ny + tile * x, tile), :] = half * (here + edge_b[pl.ds(1, tile), :])
    for x in range(nx):
        for t in range(ny // tile):
            rows = pl.ds(tile * t, tile)
            d = Differences(x, t, lane)
            for c, ((fx, sx), (fy, sy), _) in enumerate(terms):
                whole_x, whole_y = inner_plane(x, sx, nx), inner_tile(t, ny)
                total = part[c, x, rows, :]
                if whole_x and whole_y:
                    out[c, x, rows, :] = total
                    continue
                if not whole_x:
                    total += d.dx(fx, sx)
                if not whole_y:
                    total += d.dy(fy, sy)
                if c == 0 and x == nx - 1:
                    factor = buoys_end[rows, :]
                elif c == 1 and t == ny // tile - 1:
                    factor = buoys_end[pl.ds(ny + tile * x, tile), :]
                else:
                    factor = buoys[c, x, rows, :]
                out[c, x, rows, :] = velocity[c, x, rows, :] + factor * total

    planes_down = put_planes([(out, 0, 0), (out, 1, 0), (out, 1, 1), (out, 2, 0), (out, 2, 1)])

    def down(package):
        planes_down(package)
        if step == 0:
            row = high_y[pl.ds(5, 1), :]
            package[pl.ds(5 * ny, 1), :] = jnp.where(last_y, 0.0, 1.0 / jnp.where(last_y, 1.0, row))

    Pack(pax, pbx, even_x).put(
        put_planes([(out, 0, nx - 2), (out, 0, nx - 1), (out, 1, nx - 1), (out, 2, nx - 1)]), down)
    Pack(pay, pby, even_y).put(
        put_rows([(out, 1, ny - 2, 2), (out, 0, ny - 1, 1), (out, 2, ny - 1, 1)], nx),
        put_rows([(out, 1, 0, 1), (out, 0, 0, 2), (out, 2, 0, 2)], nx),
    )


def stress_fields(velocity, low_x, high_x, edges):
    vx = Field(velocity, 0, (low_x, 2), (high_x, 0), edges.at[1] if edges is not None else None)
    vy = Field(velocity, 1, (low_x, 3), (high_x, 1), edges.at[0] if edges is not None else None)
    vz = Field(velocity, 2, (low_x, 4), (high_x, 3), edges.at[2] if edges is not None else None)
    return vx, vy, vz


def new_normal(stress, lam, shear, x, rows, strains):
    la = time_step * lam[x, rows, :]
    two = (2.0 * time_step) * shear[x, rows, :]
    common = la * (strains[0] + strains[1] + strains[2])
    return [stress[c, x, rows, :] + (common + two * strains[c]) for c in range(3)]


def stress_inside(step, *refs):
    if step == 0:
        velocity, stress, lam, shear, ax, bx, ay, by, out, shears, halo_c, comps, edge_c = refs
    else:
        velocity, stress, lam, shear, shears, out, final_velocity, sem = refs
    nx, ny = stress.shape[1], stress.shape[2]
    lane = lanes()
    vx, vy, vz = stress_fields(velocity, None, None, None)
    if step == 1:
        copy = pltpu.make_async_copy(velocity, final_velocity, sem)
        copy.start()
    if step == 0:
        i, j, even_x, even_y = position()
        _, last_x, _, last_y = sides(i, j)
        for x in range(nx):
            comps[x] = 1.0 / shear[x]
            edge_c[x, pl.ds(0, tile), :] = comps[x, pl.ds(ny - tile, tile), :]
            row = pl.ds(tile * x + 5, 1)
            value = jnp.where(last_y, 1.0, jnp.where(even_y, ay[row, :], by[row, :]))
            edge_c[x, pl.ds(tile, 1), :] = jnp.where(last_y, 0.0, 1.0 / value)
        for t in range(ny // tile):
            rows = pl.ds(5 * ny + tile * t, tile)
            value = jnp.where(last_x, 1.0, jnp.where(even_x, ax[rows, :], bx[rows, :]))
            halo_c[pl.ds(tile * t, tile), :] = jnp.where(last_x, 0.0, 1.0 / value)
        halo_c[pl.ds(ny, tile), :] = edge_c[nx - 1, pl.ds(1, tile), :]

        def comp(x, t, k):
            if x == nx:
                return halo_c[pl.ds(tile * t + k, tile), :]
            if k == 1 and t == ny // tile - 1:
                return edge_c[x, pl.ds(1, tile), :]
            return comps[x, pl.ds(tile * t + k, tile), :]

    for x in range(nx):
        for t in range(ny // tile):
            rows = pl.ds(tile * t, tile)
            d = Differences(x, t, lane)
            if step == 0:
                here = comp(x, t, 0)
                next_x, next_y = comp(x + 1, t, 0), comp(x, t, 1)
                pair_x, pair_y = here + next_x, here + next_y
                four = 4.0 * time_step
                if x == nx - 1 and t == ny // tile - 1:
                    shears[0, x, rows, :] = pair_x + next_y
                else:
                    shears[0, x, rows, :] = four / (pair_x + (next_y + comp(x + 1, t, 1)))
                shears[1, x, rows, :] = four / (pair_x + z_shift(pair_x, 1, lane))
                shears[2, x, rows, :] = four / (pair_y + z_shift(pair_y, 1, lane))
            whole_y = inner_tile(t, ny)
            whole_x = inner_plane(x, -1, nx)
            zero = jnp.zeros((tile, 128), jnp.float32)
            strains = [d.dx(vx, -1) if whole_x else zero, d.dy(vy, -1) if whole_y else zero, d.dz(vz, -1)]
            if whole_x and whole_y:
                strains = new_normal(stress, lam, shear, x, rows, strains)
            for c in range(3):
                out[c, x, rows, :] = strains[c]
            whole_x = inner_plane(x, 0, nx)
            total = zero
            if whole_y:
                total += d.dy(vx, 0)
            if whole_x:
                total += d.dx(vy, 0)
            if whole_x and whole_y:
                total = stress[3, x, rows, :] + shears[0, x, rows, :] * total
            out[3, x, rows, :] = total
            total = d.dz(vx, 0)
            if whole_x:
                total = stress[4, x, rows, :] + shears[1, x, rows, :] * (total + d.dx(vz, 0))
            out[4, x, rows, :] = total
            total = d.dz(vy, 0)
            if whole_y:
                total = stress[5, x, rows, :] + shears[2, x, rows, :] * (total + d.dy(vz, 0))
            out[5, x, rows, :] = total
    if step == 1:
        copy.wait()


def stress_edges(step, *refs):
    if step == 0:
        (velocity, stress, lam, shear, halo_c, shears, part, ax, bx, ay, by,
         out, shear_end, pax, pbx, pay, pby, low_x, high_x, low_y, high_y, edges, corner) = refs
    else:
        (velocity, stress, lam, shear, shears, shear_end, part, ax, bx, ay, by,
         final_stress, low_x, high_x, low_y, high_y, edges, out, sems) = refs
    nx, ny = stress.shape[1], stress.shape[2]
    even_x, even_y, _, _ = receive((ax, bx, ay, by), (low_x, high_x, low_y, high_y))
    fill_edges(velocity, 1, edges.at[0], low_y, high_y, 0, 2, 0, 1)
    fill_edges(velocity, 0, edges.at[1], low_y, high_y, 2, 1, 1, 2)
    fill_edges(velocity, 2, edges.at[2], low_y, high_y, 3, 1, 3, 2)
    vx, vy, vz = stress_fields(velocity, low_x, high_x, edges)
    lane = lanes()
    if step == 0:
        last = pl.ds(ny - tile, tile)
        corner[pl.ds(0, tile), :] = halo_c[last, :]
        corner[pl.ds(tile, 1), :] = high_x[pl.ds(5 * ny, 1), :]
        shear_end[...] = (4.0 * time_step) / (shears[0, nx - 1, last, :] + corner[pl.ds(1, tile), :])
    copies = []
    for x in sorted(range(nx), key=lambda x: not inner_plane(x, 0, nx) or not inner_plane(x, -1, nx)):
        for t in range(ny // tile):
            rows = pl.ds(tile * t, tile)
            d = Differences(x, t, lane)
            whole_y = inner_tile(t, ny)
            whole_x = inner_plane(x, -1, nx)
            strains = [part[c, x, rows, :] for c in range(3)]
            if not (whole_x and whole_y):
                if not whole_x:
                    strains[0] = d.dx(vx, -1)
                if not whole_y:
                    strains[1] = d.dy(vy, -1)
                strains = new_normal(stress, lam, shear, x, rows, strains)
            for c in range(3):
                out[c, x, rows, :] = strains[c]
            whole_x = inner_plane(x, 0, nx)
            total = part[3, x, rows, :]
            if not (whole_x and whole_y):
                if not whole_y:
                    total += d.dy(vx, 0)
                if not whole_x:
                    total += d.dx(vy, 0)
                at_end = x == nx - 1 and t == ny // tile - 1
                factor = shear_end[...] if at_end else shears[0, x, rows, :]
                total = stress[3, x, rows, :] + factor * total
            out[3, x, rows, :] = total
            total = part[4, x, rows, :]
            if not whole_x:
                total = stress[4, x, rows, :] + shears[1, x, rows, :] * (total + d.dx(vz, 0))
            out[4, x, rows, :] = total
            total = part[5, x, rows, :]
            if not whole_y:
                total = stress[5, x, rows, :] + shears[2, x, rows, :] * (total + d.dy(vz, 0))
            out[5, x, rows, :] = total
        if step == 1:
            copy = pltpu.make_async_copy(out.at[:, x], final_stress.at[:, x], sems.at[x])
            copy.start()
            copies.append(copy)
    for copy in copies:
        copy.wait()
    if step == 0:
        Pack(pax, pbx, even_x).put(
            put_planes([(out, 3, nx - 2), (out, 3, nx - 1), (out, 4, nx - 2), (out, 4, nx - 1), (out, 0, nx - 1)]),
            put_planes([(out, 3, 0), (out, 4, 0), (out, 0, 0), (out, 0, 1)]),
        )
        Pack(pay, pby, even_y).put(
            put_rows([(out, 3, ny - 2, 2), (out, 5, ny - 2, 2), (out, 1, ny - 1, 1)], nx),
            put_rows([(out, 3, 0, 1), (out, 5, 0, 1), (out, 1, 0, 2)], nx),
        )


def call(kernel, outs, scratch, args, flops, hbm_in=(), hbm_out=()):
    def spec(far_away):
        return pl.BlockSpec(memory_space=pltpu.HBM if far_away else pltpu.VMEM)

    scratch = [pltpu.VMEM(shape, jnp.float32) if isinstance(shape, tuple) else shape for shape in scratch]
    return pl.pallas_call(
        kernel,
        out_shape=[jax.ShapeDtypeStruct(shape, jnp.float32) for shape in outs],
        in_specs=[spec(n in hbm_in) for n in range(len(args))],
        out_specs=[spec(n in hbm_out) for n in range(len(outs))],
        scratch_shapes=scratch,
        compiler_params=pltpu.CompilerParams(vmem_limit_bytes=16 * 1024 * 1024),
        cost_estimate=pl.CostEstimate(flops=flops, bytes_accessed=2 * 1024 * 1024, transcendentals=0),
    )(*args)


def per_device(velocity, stress, density, lame_lambda, lame_mu):
    _, nx, ny, nz = velocity.shape
    routes = pairings(lax.axis_size("gx"), lax.axis_size("gy"))
    cells = nx * ny * nz
    one, three = (1, nx, ny, nz), (3, nx, ny, nz)
    dma = pltpu.SemaphoreType.DMA

    def packages(x_rows):
        return [(x_rows, nz)] * 2 + [(nx * tile, nz)] * 2

    def exchange(arrays):
        return [lax.ppermute(array, AXES, route) for array, route in zip(arrays, routes)]

    def halos(x_rows):
        return packages(x_rows) + [(3, 2, nx, 2 * tile, nz)]

    def kernel(function, step):
        return lambda *refs: function(step, *refs)

    first, second, later = 6 * ny, 5 * ny + tile, 5 * ny
    packed = call(
        first_pack, packages(first), [(8, nx, tile, nz), dma((3, 8))],
        (stress, density, lame_mu), cells, hbm_in=(0, 1, 2))
    got = exchange(packed)
    part, buoy, buoys = call(
        kernel(velocity_inside, 0), [three, one, three], [], (velocity, stress, density), 60 * cells)
    new_velocity, buoys_end, *packed = call(
        kernel(velocity_edges, 0), [three, (ny + nx * tile, nz)] + packages(second), halos(first) + [(2 * tile, nz)],
        (velocity, stress, buoy, buoys, part, *got), 20 * cells)
    materials = got
    got = exchange(packed)
    part, shears, halo_c = call(
        kernel(stress_inside, 0), [stress.shape, three, (ny + tile, nz)], [(nx, ny, nz), (nx, 2 * tile, nz)],
        (new_velocity, stress, lame_lambda, lame_mu, *materials), 80 * cells)
    new_stress, shear_end, *packed = call(
        kernel(stress_edges, 0), [stress.shape, (tile, nz)] + packages(later), halos(second) + [(2 * tile, nz)],
        (new_velocity, stress, lame_lambda, lame_mu, halo_c, shears, part, *got), 20 * cells)
    velocity, stress = new_velocity, new_stress
    got = exchange(packed)
    (part,) = call(
        kernel(velocity_inside, 1), [three], [], (velocity, stress, buoys), 60 * cells)
    velocity, *packed = call(
        kernel(velocity_edges, 1), [three] + packages(later), halos(later),
        (velocity, stress, buoys, buoys_end, part, *got), 20 * cells)
    got = exchange(packed)
    part, final_velocity = call(
        kernel(stress_inside, 1), [stress.shape, three], [dma],
        (velocity, stress, lame_lambda, lame_mu, shears), 80 * cells, hbm_out=(1,))
    (final_stress,) = call(
        kernel(stress_edges, 1), [stress.shape], halos(later) + [stress.shape, dma((nx,))],
        (velocity, stress, lame_lambda, lame_mu, shears, shear_end, part, *got), 20 * cells, hbm_out=(0,))
    return (final_velocity, final_stress)


def solution(mesh):
    in_specs = (
        P(None, "gx", "gy", None),
        P(None, "gx", "gy", None),
        P("gx", "gy", None),
        P("gx", "gy", None),
        P("gx", "gy", None),
    )
    out_specs = (P(None, "gx", "gy", None), P(None, "gx", "gy", None))
    return jax.shard_map(
        per_device, mesh=mesh, in_specs=in_specs, out_specs=out_specs, check_vma=False
    )
```

time: 36.1 us -> 33.6 us (0.931)
  waiting for transfers between devices: 10.6 us -> 7.28 us
  Pallas kernels: 3.8 us -> 4.57 us
    ppermute x16, waiting for transfers between devices: 10.6 us -> 7.28 us  [exchange(): lax.ppermute(array, AXES, route)]
    pallas_call x6 -> x9, Pallas kernels: 3.8 us -> 4.57 us  [call(): pl.pallas_call(kernel, out_shape=[jax.ShapeDtypeStruct(shape, jnp.float32...]
  transfers between devices with their start and end apart: 16 -> 16, of which waited for: 4 -> 4; matrix products, arithmetic and copies ran while one was open for 0% -> 0% of each run, Pallas kernels for 0% -> 7%
where the time goes in v2:
time: 33.6 us; the launch traced here: 33.3 us
  starting transfers between devices  16.8 us (50%)
  waiting for transfers between devices  7.28 us (22%)
  Pallas kernels  4.57 us (14%)
  local copies, waits for them, and re-layouts  3.94 us (12%)
  between operations  0.75 us (2%)
    ppermute x16, starting transfers between devices, exchange(): lax.ppermute(array, AXES, route)  16.8 us
    ppermute x16, waiting for transfers between devices, exchange(): lax.ppermute(array, AXES, route)  7.28 us
    pallas_call x9, Pallas kernels, call(): pl.pallas_call(kernel, out_shape=[jax.ShapeDtypeStruct(shape, jnp.float32...  4.57 us
    unnamed x14, local copies, waits for them, and re-layouts  3.94 us
  transfers between devices with their start and end apart: 16, of which 4 were waited for; matrix products, arithmetic and copies ran while one was open for 0% of the time, Pallas kernels for 7%

profile of v2, /device:TPU:0, one launch (start us, length us, event | category | flops | bytes accessed | tf_op | source)
XLA Modules:
  0.0 33.3 jit_solution(11118800276433603430)
XLA Ops:
  0.6 0.0 copy-start
  0.6 1.1 %copy-done = f32[6,8,32,128]{3,2,1,0:T(8,128)S(1)} copy-done((f32[6,8,32,128]{3,2,1,0:T(8,128)S(1)}, f32[6,8,32,128]{3,2,1,0:T(8,128)}, u32[]{:S(2)}) %copy-start) | copy-done | bytes 786456
  1.8 0.9 %copy-done.2 = f32[8,32,128]{2,1,0:T(8,128)S(1)} copy-done((f32[8,32,128]{2,1,0:T(8,128)S(1)}, f32[8,32,128]{2,1,0:T(8,128)}, u32[]{:S(2)}) %copy-start.2) | copy-done | bytes 131096
  2.7 0.9 %copy-done.6 = f32[8,32,128]{2,1,0:T(8,128)S(1)} copy-done((f32[8,32,128]{2,1,0:T(8,128)S(1)}, f32[8,32,128]{2,1,0:T(8,128)}, u32[]{:S(2)}) %copy-start.6) | copy-done | bytes 131096
  3.6 0.6 %shard_map.69 = (f32[192,128]{1,0:T(8,128)S(1)}, f32[192,128]{1,0:T(8,128)S(1)}, f32[64,128]{1,0:T(8,128)S(1)}, f32[64,128]{1,0:T(8,128)S(1)}) custom-call(f32[6,8,32,128]{3,2,1,0:T(8,128)S(1)} %copy-done, f32[8,32,128]{2,1,0:T(8,128)S(1)} %copy-done.6, f32[8,32,128]{2,1,0:T(8,128)S(1)} %copy-done.2), custom_call_target="tpu_custom_call" | custom-call | flops 32768 | bytes 2097152 | tf_op jit(solution)/shard_map/pallas_call | solution.py:505
  4.1 3.0 %collective-permute-start = (f32[192,128]{1,0:T(8,128)S(1)}, f32[192,128]{1,0:T(8,128)S(1)}, u32[]{:S(2)}, u32[]{:S(2)}) collective-permute-start(f32[192,128]{1,0:T(8,128)S(1)} %get-tuple-element.34), channel_id=1, source_target_pairs={{0,8},{1,9},{2,10},{3,11},{4,12},{5,13},{6,14},{7,15},{8,0},{9,1},... | collective-permute-start | bytes 294920 | tf_op jit(solution)/shard_map/ppermute | solution.py:527
  7.1 0.0 collective-permute-start.1
  7.1 0.5 %collective-permute-start.2 = (f32[64,128]{1,0:T(8,128)S(1)}, f32[64,128]{1,0:T(8,128)S(1)}, u32[]{:S(2)}, u32[]{:S(2)}) collective-permute-start(f32[64,128]{1,0:T(8,128)S(1)} %get-tuple-element.36), channel_id=1, source_target_pairs={{0,1},{1,0},{2,3},{3,2},{4,5},{5,4},{6,7},{7,6},{8,9},{9,8},{10,11... | collective-permute-start | bytes 98312 | tf_op jit(solution)/shard_map/ppermute | solution.py:527
  7.7 1.0 %collective-permute-start.3 = (f32[64,128]{1,0:T(8,128)S(1)}, f32[64,128]{1,0:T(8,128)S(1)}, u32[]{:S(2)}, u32[]{:S(2)}) collective-permute-start(f32[64,128]{1,0:T(8,128)S(1)} %get-tuple-element.37), channel_id=1, source_target_pairs={{0,16},{1,2},{2,1},{3,4},{4,3},{5,6},{6,5},{7,23},{8,24},{9,10},{1... | collective-permute-start | bytes 98312 | tf_op jit(solution)/shard_map/ppermute | solution.py:527
  8.7 1.0 %copy-done.5 = f32[3,8,32,128]{3,2,1,0:T(8,128)S(1)} copy-done((f32[3,8,32,128]{3,2,1,0:T(8,128)S(1)}, f32[3,8,32,128]{3,2,1,0:T(8,128)}, u32[]{:S(2)}) %copy-start.5) | copy-done | bytes 393240
  9.7 0.4 %shard_map.68 = (f32[3,8,32,128]{3,2,1,0:T(8,128)S(1)}, f32[1,8,32,128]{3,2,1,0:T(8,128)S(1)}, f32[3,8,32,128]{3,2,1,0:T(8,128)S(1)}) custom-call(f32[3,8,32,128]{3,2,1,0:T(8,128)S(1)} %copy-done.5, f32[6,8,32,128]{3,2,1,0:T(8,128)S(1)} %copy-done.1, f32[8,32,128]{2,1,0:T(8,128)S(1)} %copy-done.6), custom_call_target="tpu_custom_call" | custom-call | flops 1966080 | bytes 2097152 | tf_op jit(solution)/shard_map/pallas_call | solution.py:505
  10.1 0.0 collective-permute-done.2.refs_7_.refs_6_
  10.1 1.5 %collective-permute-done.3.refs_8_.refs_7_ = f32[64,128]{1,0:T(8,128)S(1)} collective-permute-done((f32[64,128]{1,0:T(8,128)S(1)}, f32[64,128]{1,0:T(8,128)S(1)}, u32[]{:S(2)}, u32[]{:S(2)}) %collective-permute-start.3) | collective-permute-done | bytes 32800 | tf_op jit(solution)/shard_map/ppermute | solution.py:527
  11.6 0.0 collective-permute-done.refs_5_.refs_4_
  11.6 0.0 collective-permute-done.1.refs_6_.refs_5_
  11.6 0.0 copy-start.4
  11.6 0.2 shard_map.70
  11.8 3.6 %collective-permute-start.4 = (f32[168,128]{1,0:T(8,128)S(1)}, f32[168,128]{1,0:T(8,128)S(1)}, u32[]{:S(2)}, u32[]{:S(2)}) collective-permute-start(f32[168,128]{1,0:T(8,128)S(1)} %get-tuple-element.42), channel_id=1, source_target_pairs={{0,8},{1,9},{2,10},{3,11},{4,12},{5,13},{6,14},{7,15},{8,0},{9,1},... | collective-permute-start | bytes 258056 | tf_op jit(solution)/shard_map/ppermute | solution.py:527
  15.4 0.0 collective-permute-start.5
  15.4 0.5 %collective-permute-start.6 = (f32[64,128]{1,0:T(8,128)S(1)}, f32[64,128]{1,0:T(8,128)S(1)}, u32[]{:S(2)}, u32[]{:S(2)}) collective-permute-start(f32[64,128]{1,0:T(8,128)S(1)} %get-tuple-element.44), channel_id=1, source_target_pairs={{0,1},{1,0},{2,3},{3,2},{4,5},{5,4},{6,7},{7,6},{8,9},{9,8},{10,11... | collective-permute-start | bytes 98312 | tf_op jit(solution)/shard_map/ppermute | solution.py:527
  15.9 1.0 %collective-permute-start.7 = (f32[64,128]{1,0:T(8,128)S(1)}, f32[64,128]{1,0:T(8,128)S(1)}, u32[]{:S(2)}, u32[]{:S(2)}) collective-permute-start(f32[64,128]{1,0:T(8,128)S(1)} %get-tuple-element.45), channel_id=1, source_target_pairs={{0,16},{1,2},{2,1},{3,4},{4,3},{5,6},{6,5},{7,23},{8,24},{9,10},{1... | collective-permute-start | bytes 98312 | tf_op jit(solution)/shard_map/ppermute | solution.py:527
  17.0 0.0 copy-done.4
  17.0 0.5 %shard_map.71 = (f32[6,8,32,128]{3,2,1,0:T(8,128)S(1)}, f32[3,8,32,128]{3,2,1,0:T(8,128)S(1)}, f32[40,128]{1,0:T(8,128)S(1)}) custom-call(f32[3,8,32,128]{3,2,1,0:T(8,128)S(1)} %get-tuple-element.38.refs_0_, f32[6,8,32,128]{3,2,1,0:T(8,128)S(1)} %copy-done.1, f32[8,32,128]{2,1,0:T(8,128)S(1)} %copy-done.4, f32[8,32,128]{2,1,0:T(8,128)S(1)} %copy-done.3, ...), custom_call_target="tpu_custom_call" | custom-call | flops 2621440 | bytes 2097152 | tf_op jit(solution)/shard_map/pallas_call | solution.py:505
  17.5 0.0 collective-permute-done.6.refs_9_
  17.5 2.4 %collective-permute-done.7.refs_10_ = f32[64,128]{1,0:T(8,128)S(1)} collective-permute-done((f32[64,128]{1,0:T(8,128)S(1)}, f32[64,128]{1,0:T(8,128)S(1)}, u32[]{:S(2)}, u32[]{:S(2)}) %collective-permute-start.7) | collective-permute-done | bytes 32800 | tf_op jit(solution)/shard_map/ppermute | solution.py:527
  19.8 0.0 collective-permute-done.4.refs_7_
  19.8 0.0 collective-permute-done.5.refs_8_
  19.9 0.2 shard_map.72
  20.1 1.5 %collective-permute-start.8 = (f32[160,128]{1,0:T(8,128)S(1)}, f32[160,128]{1,0:T(8,128)S(1)}, u32[]{:S(2)}, u32[]{:S(2)}) collective-permute-start(f32[160,128]{1,0:T(8,128)S(1)} %get-tuple-element.48), channel_id=1, source_target_pairs={{0,8},{1,9},{2,10},{3,11},{4,12},{5,13},{6,14},{7,15},{8,0},{9,1},... | collective-permute-start | bytes 245768 | tf_op jit(solution)/shard_map/ppermute | solution.py:527
  21.5 0.0 collective-permute-start.9
  21.5 0.5 %collective-permute-start.10 = (f32[64,128]{1,0:T(8,128)S(1)}, f32[64,128]{1,0:T(8,128)S(1)}, u32[]{:S(2)}, u32[]{:S(2)}) collective-permute-start(f32[64,128]{1,0:T(8,128)S(1)} %get-tuple-element.50), channel_id=1, source_target_pairs={{0,1},{1,0},{2,3},{3,2},{4,5},{5,4},{6,7},{7,6},{8,9},{9,8},{10,11... | collective-permute-start | bytes 98312 | tf_op jit(solution)/shard_map/ppermute | solution.py:527
  22.1 1.6 %collective-permute-start.11 = (f32[64,128]{1,0:T(8,128)S(1)}, f32[64,128]{1,0:T(8,128)S(1)}, u32[]{:S(2)}, u32[]{:S(2)}) collective-permute-start(f32[64,128]{1,0:T(8,128)S(1)} %get-tuple-element.51), channel_id=1, source_target_pairs={{0,16},{1,2},{2,1},{3,4},{4,3},{5,6},{6,5},{7,23},{8,24},{9,10},{1... | collective-permute-start | bytes 98312 | tf_op jit(solution)/shard_map/ppermute | solution.py:527
  23.7 0.4 %shard_map.73.refs_4_ = f32[3,8,32,128]{3,2,1,0:T(8,128)S(1)} custom-call(f32[3,8,32,128]{3,2,1,0:T(8,128)S(1)} %get-tuple-element.38.refs_0_, f32[6,8,32,128]{3,2,1,0:T(8,128)S(1)} %get-tuple-element.46.refs_1_, f32[3,8,32,128]{3,2,1,0:T(8,128)S(1)} %get-tuple-element.32.refs_3_.refs_2_), custom_call_target="tpu_custom_call" | custom-call | flops 1966080 | bytes 2097152 | tf_op jit(solution)/shard_map/pallas_call | solution.py:505
  24.0 0.0 collective-permute-done.10.refs_7_
  24.1 1.9 %collective-permute-done.11.refs_8_ = f32[64,128]{1,0:T(8,128)S(1)} collective-permute-done((f32[64,128]{1,0:T(8,128)S(1)}, f32[64,128]{1,0:T(8,128)S(1)}, u32[]{:S(2)}, u32[]{:S(2)}) %collective-permute-start.11) | collective-permute-done | bytes 32800 | tf_op jit(solution)/shard_map/ppermute | solution.py:527
  26.0 0.0 collective-permute-done.8.refs_5_
  26.0 0.0 collective-permute-done.9.refs_6_
  26.0 0.2 shard_map.74
  26.2 1.7 %collective-permute-start.12 = (f32[160,128]{1,0:T(8,128)S(1)}, f32[160,128]{1,0:T(8,128)S(1)}, u32[]{:S(2)}, u32[]{:S(2)}) collective-permute-start(f32[160,128]{1,0:T(8,128)S(1)} %get-tuple-element.56), channel_id=1, source_target_pairs={{0,8},{1,9},{2,10},{3,11},{4,12},{5,13},{6,14},{7,15},{8,0},{9,1},... | collective-permute-start | bytes 245768 | tf_op jit(solution)/shard_map/ppermute | solution.py:527
  27.9 0.0 collective-permute-start.13
  27.9 0.5 %collective-permute-start.14 = (f32[64,128]{1,0:T(8,128)S(1)}, f32[64,128]{1,0:T(8,128)S(1)}, u32[]{:S(2)}, u32[]{:S(2)}) collective-permute-start(f32[64,128]{1,0:T(8,128)S(1)} %get-tuple-element.58), channel_id=1, source_target_pairs={{0,1},{1,0},{2,3},{3,2},{4,5},{5,4},{6,7},{7,6},{8,9},{9,8},{10,11... | collective-permute-start | bytes 98312 | tf_op jit(solution)/shard_map/ppermute | solution.py:527
  28.4 1.4 %collective-permute-start.15 = (f32[64,128]{1,0:T(8,128)S(1)}, f32[64,128]{1,0:T(8,128)S(1)}, u32[]{:S(2)}, u32[]{:S(2)}) collective-permute-start(f32[64,128]{1,0:T(8,128)S(1)} %get-tuple-element.59), channel_id=1, source_target_pairs={{0,16},{1,2},{2,1},{3,4},{4,3},{5,6},{6,5},{7,23},{8,24},{9,10},{1... | collective-permute-start | bytes 98312 | tf_op jit(solution)/shard_map/ppermute | solution.py:527
  29.8 1.1 %shard_map.75 = (f32[6,8,32,128]{3,2,1,0:T(8,128)S(1)}, f32[3,8,32,128]{3,2,1,0:T(8,128)}) custom-call(f32[3,8,32,128]{3,2,1,0:T(8,128)S(1)} %get-tuple-element.52.refs_0_, f32[6,8,32,128]{3,2,1,0:T(8,128)S(1)} %get-tuple-element.46.refs_1_, f32[8,32,128]{2,1,0:T(8,128)S(1)} %copy-done.4, f32[8,32,128]{2,1,0:T(8,128)S(1)} %copy-done.3, ...), custom_call_target="tpu_custom_call" | custom-call | flops 2621440 | bytes 2097152 | tf_op jit(solution)/shard_map/pallas_call | solution.py:505
  30.8 0.0 collective-permute-done.14.refs_9_
  30.8 1.5 %collective-permute-done.15.refs_10_ = f32[64,128]{1,0:T(8,128)S(1)} collective-permute-done((f32[64,128]{1,0:T(8,128)S(1)}, f32[64,128]{1,0:T(8,128)S(1)}, u32[]{:S(2)}, u32[]{:S(2)}) %collective-permute-start.15) | collective-permute-done | bytes 32800 | tf_op jit(solution)/shard_map/ppermute | solution.py:527
  32.3 0.0 collective-permute-done.12.refs_7_
  32.3 0.0 collective-permute-done.13.refs_8_
  32.3 1.0 %shard_map.76 = f32[6,8,32,128]{3,2,1,0:T(8,128)} custom-call(f32[3,8,32,128]{3,2,1,0:T(8,128)S(1)} %get-tuple-element.52.refs_0_, f32[6,8,32,128]{3,2,1,0:T(8,128)S(1)} %get-tuple-element.46.refs_1_, f32[8,32,128]{2,1,0:T(8,128)S(1)} %copy-done.4, f32[8,32,128]{2,1,0:T(8,128)S(1)} %copy-done.3, f32[3,8,32,128]{3,2,1,0:T(8,128)S(1)} %get-tuple-element.40.refs_5_.refs_4_, ...), custom_call_target="tpu_custom_call" | custom-call | flops 655360 | bytes 2097152 | tf_op jit(solution)/shard_map/pallas_call | solution.py:505
  (7 shorter events, 0.0 us)
Async XLA Ops:
  0.6 1.1 %copy-start = (f32[6,8,32,128]{3,2,1,0:T(8,128)S(1)}, f32[6,8,32,128]{3,2,1,0:T(8,128)}, u32[]{:S(2)}) copy-start(f32[6,8,32,128]{3,2,1,0:T(8,128)} %refs_1_.7) | copy-start | bytes 2359300
  1.8 0.9 %copy-start.2 = (f32[8,32,128]{2,1,0:T(8,128)S(1)}, f32[8,32,128]{2,1,0:T(8,128)}, u32[]{:S(2)}) copy-start(f32[8,32,128]{2,1,0:T(8,128)} %refs_3_.7) | copy-start | bytes 393220
  2.7 0.9 %copy-start.6 = (f32[8,32,128]{2,1,0:T(8,128)S(1)}, f32[8,32,128]{2,1,0:T(8,128)}, u32[]{:S(2)}) copy-start(f32[8,32,128]{2,1,0:T(8,128)} %density.1) | copy-start | bytes 393220
  3.6 5.1 %copy-start.1 = (f32[6,8,32,128]{3,2,1,0:T(8,128)S(1)}, f32[6,8,32,128]{3,2,1,0:T(8,128)}, u32[]{:S(2)}) copy-start(f32[6,8,32,128]{3,2,1,0:T(8,128)} %refs_1_.7) | copy-start | bytes 2359300
  4.1 7.4 %collective-permute-start = (f32[192,128]{1,0:T(8,128)S(1)}, f32[192,128]{1,0:T(8,128)S(1)}, u32[]{:S(2)}, u32[]{:S(2)}) collective-permute-start(f32[192,128]{1,0:T(8,128)S(1)} %get-tuple-element.34), channel_id=1, source_target_pairs={{0,8},{1,9},{2,10},{3,11},{4,12},{5,13},{6,14},{7,15},{8,0},{9,1},... | collective-permute-start | bytes 294920 | tf_op jit(solution)/shard_map/ppermute | solution.py:527
  7.1 4.4 %collective-permute-start.1 = (f32[192,128]{1,0:T(8,128)S(1)}, f32[192,128]{1,0:T(8,128)S(1)}, u32[]{:S(2)}, u32[]{:S(2)}) collective-permute-start(f32[192,128]{1,0:T(8,128)S(1)} %get-tuple-element.35), channel_id=1, source_target_pairs={{0,1},{1,0},{2,3},{3,2},{4,5},{5,4},{6,7},{7,6},{8,16},{9,17},{10,... | collective-permute-start | bytes 294920 | tf_op jit(solution)/shard_map/ppermute | solution.py:527
  7.1 3.0 %collective-permute-start.2 = (f32[64,128]{1,0:T(8,128)S(1)}, f32[64,128]{1,0:T(8,128)S(1)}, u32[]{:S(2)}, u32[]{:S(2)}) collective-permute-start(f32[64,128]{1,0:T(8,128)S(1)} %get-tuple-element.36), channel_id=1, source_target_pairs={{0,1},{1,0},{2,3},{3,2},{4,5},{5,4},{6,7},{7,6},{8,9},{9,8},{10,11... | collective-permute-start | bytes 98312 | tf_op jit(solution)/shard_map/ppermute | solution.py:527
  7.7 3.9 %collective-permute-start.3 = (f32[64,128]{1,0:T(8,128)S(1)}, f32[64,128]{1,0:T(8,128)S(1)}, u32[]{:S(2)}, u32[]{:S(2)}) collective-permute-start(f32[64,128]{1,0:T(8,128)S(1)} %get-tuple-element.37), channel_id=1, source_target_pairs={{0,16},{1,2},{2,1},{3,4},{4,3},{5,6},{6,5},{7,23},{8,24},{9,10},{1... | collective-permute-start | bytes 98312 | tf_op jit(solution)/shard_map/ppermute | solution.py:527
  8.7 1.0 %copy-start.5 = (f32[3,8,32,128]{3,2,1,0:T(8,128)S(1)}, f32[3,8,32,128]{3,2,1,0:T(8,128)}, u32[]{:S(2)}) copy-start(f32[3,8,32,128]{3,2,1,0:T(8,128)} %refs_0_.3) | copy-start | bytes 1179652
  11.6 5.4 %copy-start.3 = (f32[8,32,128]{2,1,0:T(8,128)S(1)}, f32[8,32,128]{2,1,0:T(8,128)}, u32[]{:S(2)}) copy-start(f32[8,32,128]{2,1,0:T(8,128)} %refs_3_.7) | copy-start | bytes 393220
  11.6 5.4 %copy-start.4 = (f32[8,32,128]{2,1,0:T(8,128)S(1)}, f32[8,32,128]{2,1,0:T(8,128)}, u32[]{:S(2)}) copy-start(f32[8,32,128]{2,1,0:T(8,128)} %refs_2_.9) | copy-start | bytes 393220
  11.8 8.0 %collective-permute-start.4 = (f32[168,128]{1,0:T(8,128)S(1)}, f32[168,128]{1,0:T(8,128)S(1)}, u32[]{:S(2)}, u32[]{:S(2)}) collective-permute-start(f32[168,128]{1,0:T(8,128)S(1)} %get-tuple-element.42), channel_id=1, source_target_pairs={{0,8},{1,9},{2,10},{3,11},{4,12},{5,13},{6,14},{7,15},{8,0},{9,1},... | collective-permute-start | bytes 258056 | tf_op jit(solution)/shard_map/ppermute | solution.py:527
  15.4 4.4 %collective-permute-start.5 = (f32[168,128]{1,0:T(8,128)S(1)}, f32[168,128]{1,0:T(8,128)S(1)}, u32[]{:S(2)}, u32[]{:S(2)}) collective-permute-start(f32[168,128]{1,0:T(8,128)S(1)} %get-tuple-element.43), channel_id=1, source_target_pairs={{0,1},{1,0},{2,3},{3,2},{4,5},{5,4},{6,7},{7,6},{8,16},{9,17},{10,... | collective-permute-start | bytes 258056 | tf_op jit(solution)/shard_map/ppermute | solution.py:527
  15.4 2.0 %collective-permute-start.6 = (f32[64,128]{1,0:T(8,128)S(1)}, f32[64,128]{1,0:T(8,128)S(1)}, u32[]{:S(2)}, u32[]{:S(2)}) collective-permute-start(f32[64,128]{1,0:T(8,128)S(1)} %get-tuple-element.44), channel_id=1, source_target_pairs={{0,1},{1,0},{2,3},{3,2},{4,5},{5,4},{6,7},{7,6},{8,9},{9,8},{10,11... | collective-permute-start | bytes 98312 | tf_op jit(solution)/shard_map/ppermute | solution.py:527
  15.9 3.9 %collective-permute-start.7 = (f32[64,128]{1,0:T(8,128)S(1)}, f32[64,128]{1,0:T(8,128)S(1)}, u32[]{:S(2)}, u32[]{:S(2)}) collective-permute-start(f32[64,128]{1,0:T(8,128)S(1)} %get-tuple-element.45), channel_id=1, source_target_pairs={{0,16},{1,2},{2,1},{3,4},{4,3},{5,6},{6,5},{7,23},{8,24},{9,10},{1... | collective-permute-start | bytes 98312 | tf_op jit(solution)/shard_map/ppermute | solution.py:527
  20.1 5.9 %collective-permute-start.8 = (f32[160,128]{1,0:T(8,128)S(1)}, f32[160,128]{1,0:T(8,128)S(1)}, u32[]{:S(2)}, u32[]{:S(2)}) collective-permute-start(f32[160,128]{1,0:T(8,128)S(1)} %get-tuple-element.48), channel_id=1, source_target_pairs={{0,8},{1,9},{2,10},{3,11},{4,12},{5,13},{6,14},{7,15},{8,0},{9,1},... | collective-permute-start | bytes 245768 | tf_op jit(solution)/shard_map/ppermute | solution.py:527
  21.5 4.4 %collective-permute-start.9 = (f32[160,128]{1,0:T(8,128)S(1)}, f32[160,128]{1,0:T(8,128)S(1)}, u32[]{:S(2)}, u32[]{:S(2)}) collective-permute-start(f32[160,128]{1,0:T(8,128)S(1)} %get-tuple-element.49), channel_id=1, source_target_pairs={{0,1},{1,0},{2,3},{3,2},{4,5},{5,4},{6,7},{7,6},{8,16},{9,17},{10,... | collective-permute-start | bytes 245768 | tf_op jit(solution)/shard_map/ppermute | solution.py:527
  21.5 2.5 %collective-permute-start.10 = (f32[64,128]{1,0:T(8,128)S(1)}, f32[64,128]{1,0:T(8,128)S(1)}, u32[]{:S(2)}, u32[]{:S(2)}) collective-permute-start(f32[64,128]{1,0:T(8,128)S(1)} %get-tuple-element.50), channel_id=1, source_target_pairs={{0,1},{1,0},{2,3},{3,2},{4,5},{5,4},{6,7},{7,6},{8,9},{9,8},{10,11... | collective-permute-start | bytes 98312 | tf_op jit(solution)/shard_map/ppermute | solution.py:527
  22.1 3.9 %collective-permute-start.11 = (f32[64,128]{1,0:T(8,128)S(1)}, f32[64,128]{1,0:T(8,128)S(1)}, u32[]{:S(2)}, u32[]{:S(2)}) collective-permute-start(f32[64,128]{1,0:T(8,128)S(1)} %get-tuple-element.51), channel_id=1, source_target_pairs={{0,16},{1,2},{2,1},{3,4},{4,3},{5,6},{6,5},{7,23},{8,24},{9,10},{1... | collective-permute-start | bytes 98312 | tf_op jit(solution)/shard_map/ppermute | solution.py:527
  26.2 6.1 %collective-permute-start.12 = (f32[160,128]{1,0:T(8,128)S(1)}, f32[160,128]{1,0:T(8,128)S(1)}, u32[]{:S(2)}, u32[]{:S(2)}) collective-permute-start(f32[160,128]{1,0:T(8,128)S(1)} %get-tuple-element.56), channel_id=1, source_target_pairs={{0,8},{1,9},{2,10},{3,11},{4,12},{5,13},{6,14},{7,15},{8,0},{9,1},... | collective-permute-start | bytes 245768 | tf_op jit(solution)/shard_map/ppermute | solution.py:527
  27.9 4.4 %collective-permute-start.13 = (f32[160,128]{1,0:T(8,128)S(1)}, f32[160,128]{1,0:T(8,128)S(1)}, u32[]{:S(2)}, u32[]{:S(2)}) collective-permute-start(f32[160,128]{1,0:T(8,128)S(1)} %get-tuple-element.57), channel_id=1, source_target_pairs={{0,1},{1,0},{2,3},{3,2},{4,5},{5,4},{6,7},{7,6},{8,16},{9,17},{10,... | collective-permute-start | bytes 245768 | tf_op jit(solution)/shard_map/ppermute | solution.py:527
  27.9 2.9 %collective-permute-start.14 = (f32[64,128]{1,0:T(8,128)S(1)}, f32[64,128]{1,0:T(8,128)S(1)}, u32[]{:S(2)}, u32[]{:S(2)}) collective-permute-start(f32[64,128]{1,0:T(8,128)S(1)} %get-tuple-element.58), channel_id=1, source_target_pairs={{0,1},{1,0},{2,3},{3,2},{4,5},{5,4},{6,7},{7,6},{8,9},{9,8},{10,11... | collective-permute-start | bytes 98312 | tf_op jit(solution)/shard_map/ppermute | solution.py:527
  28.4 3.9 %collective-permute-start.15 = (f32[64,128]{1,0:T(8,128)S(1)}, f32[64,128]{1,0:T(8,128)S(1)}, u32[]{:S(2)}, u32[]{:S(2)}) collective-permute-start(f32[64,128]{1,0:T(8,128)S(1)} %get-tuple-element.59), channel_id=1, source_target_pairs={{0,16},{1,2},{2,1},{3,4},{4,3},{5,6},{6,5},{7,23},{8,24},{9,10},{1... | collective-permute-start | bytes 98312 | tf_op jit(solution)/shard_map/ppermute | solution.py:527

commit v3 on v2

--- a/solution.py
+++ b/solution.py
@@ -502,9 +502,10 @@
         return pl.BlockSpec(memory_space=pltpu.HBM if far_away else pltpu.VMEM)
 
     scratch = [pltpu.VMEM(shape, jnp.float32) if isinstance(shape, tuple) else shape for shape in scratch]
+    args = [pltpu.with_memory_space_constraint(a, pltpu.HBM) if n in hbm_in else a for n, a in enumerate(args)]
     return pl.pallas_call(
         kernel,
-        out_shape=[jax.ShapeDtypeStruct(shape, jnp.float32) for shape in outs],
+        out_shape=[(pltpu.HBM if n in hbm_out else pltpu.VMEM)(shape, jnp.float32) for n, shape in enumerate(outs)],
         in_specs=[spec(n in hbm_in) for n in range(len(args))],
         out_specs=[spec(n in hbm_out) for n in range(len(outs))],
         scratch_shapes=scratch,

time: 33.6 us -> 31.3 us (0.932)
  local copies, waits for them, and re-layouts: 3.94 us -> 1.01 us
  Pallas kernels: 4.57 us -> 5.22 us
    unnamed x14 -> x10, local copies, waits for them, and re-layouts: 3.94 us -> 1.01 us
    pallas_call x9, Pallas kernels: 4.57 us -> 5.22 us  [call(): pl.pallas_call(kernel, out_shape=[(pltpu.HBM if n in hbm_out else pltpu.V...]
where the time goes in v3:
time: 31.3 us; the launch traced here: 31.1 us
  starting transfers between devices  16.8 us (54%)
  waiting for transfers between devices  7.28 us (23%)
  Pallas kernels  5.22 us (17%)
  local copies, waits for them, and re-layouts  1.01 us (3%)
  between operations  0.76 us (2%)
    ppermute x16, starting transfers between devices, exchange(): lax.ppermute(array, AXES, route)  16.8 us
    ppermute x16, waiting for transfers between devices, exchange(): lax.ppermute(array, AXES, route)  7.28 us
    pallas_call x9, Pallas kernels, call(): pl.pallas_call(kernel, out_shape=[(pltpu.HBM if n in hbm_out else pltpu.V...  5.22 us
    unnamed x10, local copies, waits for them, and re-layouts  1.01 us
  transfers between devices with their start and end apart: 16, of which 4 were waited for; matrix products, arithmetic and copies ran while one was open for 0% of the time, Pallas kernels for 7%

profile of v3, /device:TPU:0, one launch (start us, length us, event | category | flops | bytes accessed | tf_op | source)
XLA Modules:
  0.0 31.1 jit_solution(16861828487428249170)
XLA Ops:
  0.6 0.0 copy-start
  0.6 0.0 copy-start.4
  0.6 1.2 %shard_map.69 = (f32[192,128]{1,0:T(8,128)S(1)}, f32[192,128]{1,0:T(8,128)S(1)}, f32[64,128]{1,0:T(8,128)S(1)}, f32[64,128]{1,0:T(8,128)S(1)}) custom-call(f32[6,8,32,128]{3,2,1,0:T(8,128)} %refs_1_.7, f32[8,32,128]{2,1,0:T(8,128)} %density.1, f32[8,32,128]{2,1,0:T(8,128)} %refs_3_.7), custom_call_target="tpu_custom_call" | custom-call | flops 32768 | bytes 2097152 | tf_op jit(solution)/shard_map/pallas_call | solution.py:506
  1.9 3.0 %collective-permute-start = (f32[192,128]{1,0:T(8,128)S(1)}, f32[192,128]{1,0:T(8,128)S(1)}, u32[]{:S(2)}, u32[]{:S(2)}) collective-permute-start(f32[192,128]{1,0:T(8,128)S(1)} %get-tuple-element.34), channel_id=1, source_target_pairs={{0,8},{1,9},{2,10},{3,11},{4,12},{5,13},{6,14},{7,15},{8,0},{9,1},... | collective-permute-start | bytes 294920 | tf_op jit(solution)/shard_map/ppermute | solution.py:528
  4.9 0.0 collective-permute-start.1
  4.9 0.5 %collective-permute-start.2 = (f32[64,128]{1,0:T(8,128)S(1)}, f32[64,128]{1,0:T(8,128)S(1)}, u32[]{:S(2)}, u32[]{:S(2)}) collective-permute-start(f32[64,128]{1,0:T(8,128)S(1)} %get-tuple-element.36), channel_id=1, source_target_pairs={{0,1},{1,0},{2,3},{3,2},{4,5},{5,4},{6,7},{7,6},{8,9},{9,8},{10,11... | collective-permute-start | bytes 98312 | tf_op jit(solution)/shard_map/ppermute | solution.py:528
  5.4 1.0 %collective-permute-start.3 = (f32[64,128]{1,0:T(8,128)S(1)}, f32[64,128]{1,0:T(8,128)S(1)}, u32[]{:S(2)}, u32[]{:S(2)}) collective-permute-start(f32[64,128]{1,0:T(8,128)S(1)} %get-tuple-element.37), channel_id=1, source_target_pairs={{0,16},{1,2},{2,1},{3,4},{4,3},{5,6},{6,5},{7,23},{8,24},{9,10},{1... | collective-permute-start | bytes 98312 | tf_op jit(solution)/shard_map/ppermute | solution.py:528
  6.4 0.0 copy-done
  6.4 0.0 copy-done.4
  6.4 1.0 %copy-done.3 = f32[3,8,32,128]{3,2,1,0:T(8,128)S(1)} copy-done((f32[3,8,32,128]{3,2,1,0:T(8,128)S(1)}, f32[3,8,32,128]{3,2,1,0:T(8,128)}, u32[]{:S(2)}) %copy-start.3) | copy-done | bytes 393240
  7.4 0.4 %shard_map.68 = (f32[3,8,32,128]{3,2,1,0:T(8,128)S(1)}, f32[1,8,32,128]{3,2,1,0:T(8,128)S(1)}, f32[3,8,32,128]{3,2,1,0:T(8,128)S(1)}) custom-call(f32[3,8,32,128]{3,2,1,0:T(8,128)S(1)} %copy-done.3, f32[6,8,32,128]{3,2,1,0:T(8,128)S(1)} %copy-done, f32[8,32,128]{2,1,0:T(8,128)S(1)} %copy-done.4), custom_call_target="tpu_custom_call" | custom-call | flops 1966080 | bytes 2097152 | tf_op jit(solution)/shard_map/pallas_call | solution.py:506
  7.8 0.0 collective-permute-done.2.refs_7_.refs_6_
  7.8 1.5 %collective-permute-done.3.refs_8_.refs_7_ = f32[64,128]{1,0:T(8,128)S(1)} collective-permute-done((f32[64,128]{1,0:T(8,128)S(1)}, f32[64,128]{1,0:T(8,128)S(1)}, u32[]{:S(2)}, u32[]{:S(2)}) %collective-permute-start.3) | collective-permute-done | bytes 32800 | tf_op jit(solution)/shard_map/ppermute | solution.py:528
  9.3 0.0 collective-permute-done.refs_5_.refs_4_
  9.3 0.0 collective-permute-done.1.refs_6_.refs_5_
  9.3 0.0 copy-start.2
  9.3 0.2 shard_map.70
  9.5 3.6 %collective-permute-start.4 = (f32[168,128]{1,0:T(8,128)S(1)}, f32[168,128]{1,0:T(8,128)S(1)}, u32[]{:S(2)}, u32[]{:S(2)}) collective-permute-start(f32[168,128]{1,0:T(8,128)S(1)} %get-tuple-element.42), channel_id=1, source_target_pairs={{0,8},{1,9},{2,10},{3,11},{4,12},{5,13},{6,14},{7,15},{8,0},{9,1},... | collective-permute-start | bytes 258056 | tf_op jit(solution)/shard_map/ppermute | solution.py:528
  13.1 0.0 collective-permute-start.5
  13.1 0.5 %collective-permute-start.6 = (f32[64,128]{1,0:T(8,128)S(1)}, f32[64,128]{1,0:T(8,128)S(1)}, u32[]{:S(2)}, u32[]{:S(2)}) collective-permute-start(f32[64,128]{1,0:T(8,128)S(1)} %get-tuple-element.44), channel_id=1, source_target_pairs={{0,1},{1,0},{2,3},{3,2},{4,5},{5,4},{6,7},{7,6},{8,9},{9,8},{10,11... | collective-permute-start | bytes 98312 | tf_op jit(solution)/shard_map/ppermute | solution.py:528
  13.7 1.0 %collective-permute-start.7 = (f32[64,128]{1,0:T(8,128)S(1)}, f32[64,128]{1,0:T(8,128)S(1)}, u32[]{:S(2)}, u32[]{:S(2)}) collective-permute-start(f32[64,128]{1,0:T(8,128)S(1)} %get-tuple-element.45), channel_id=1, source_target_pairs={{0,16},{1,2},{2,1},{3,4},{4,3},{5,6},{6,5},{7,23},{8,24},{9,10},{1... | collective-permute-start | bytes 98312 | tf_op jit(solution)/shard_map/ppermute | solution.py:528
  14.7 0.0 copy-done.1
  14.7 0.5 %shard_map.71 = (f32[6,8,32,128]{3,2,1,0:T(8,128)S(1)}, f32[3,8,32,128]{3,2,1,0:T(8,128)S(1)}, f32[40,128]{1,0:T(8,128)S(1)}) custom-call(f32[3,8,32,128]{3,2,1,0:T(8,128)S(1)} %get-tuple-element.38.refs_0_, f32[6,8,32,128]{3,2,1,0:T(8,128)S(1)} %copy-done, f32[8,32,128]{2,1,0:T(8,128)S(1)} %copy-done.2, f32[8,32,128]{2,1,0:T(8,128)S(1)} %copy-done.1, ...), custom_call_target="tpu_custom_call" | custom-call | flops 2621440 | bytes 2097152 | tf_op jit(solution)/shard_map/pallas_call | solution.py:506
  15.2 0.0 collective-permute-done.6.refs_9_
  15.2 2.4 %collective-permute-done.7.refs_10_ = f32[64,128]{1,0:T(8,128)S(1)} collective-permute-done((f32[64,128]{1,0:T(8,128)S(1)}, f32[64,128]{1,0:T(8,128)S(1)}, u32[]{:S(2)}, u32[]{:S(2)}) %collective-permute-start.7) | collective-permute-done | bytes 32800 | tf_op jit(solution)/shard_map/ppermute | solution.py:528
  17.6 0.0 collective-permute-done.4.refs_7_
  17.6 0.0 collective-permute-done.5.refs_8_
  17.6 0.2 shard_map.72
  17.8 1.5 %collective-permute-start.8 = (f32[160,128]{1,0:T(8,128)S(1)}, f32[160,128]{1,0:T(8,128)S(1)}, u32[]{:S(2)}, u32[]{:S(2)}) collective-permute-start(f32[160,128]{1,0:T(8,128)S(1)} %get-tuple-element.48), channel_id=1, source_target_pairs={{0,8},{1,9},{2,10},{3,11},{4,12},{5,13},{6,14},{7,15},{8,0},{9,1},... | collective-permute-start | bytes 245768 | tf_op jit(solution)/shard_map/ppermute | solution.py:528
  19.3 0.0 collective-permute-start.9
  19.3 0.5 %collective-permute-start.10 = (f32[64,128]{1,0:T(8,128)S(1)}, f32[64,128]{1,0:T(8,128)S(1)}, u32[]{:S(2)}, u32[]{:S(2)}) collective-permute-start(f32[64,128]{1,0:T(8,128)S(1)} %get-tuple-element.50), channel_id=1, source_target_pairs={{0,1},{1,0},{2,3},{3,2},{4,5},{5,4},{6,7},{7,6},{8,9},{9,8},{10,11... | collective-permute-start | bytes 98312 | tf_op jit(solution)/shard_map/ppermute | solution.py:528
  19.8 1.6 %collective-permute-start.11 = (f32[64,128]{1,0:T(8,128)S(1)}, f32[64,128]{1,0:T(8,128)S(1)}, u32[]{:S(2)}, u32[]{:S(2)}) collective-permute-start(f32[64,128]{1,0:T(8,128)S(1)} %get-tuple-element.51), channel_id=1, source_target_pairs={{0,16},{1,2},{2,1},{3,4},{4,3},{5,6},{6,5},{7,23},{8,24},{9,10},{1... | collective-permute-start | bytes 98312 | tf_op jit(solution)/shard_map/ppermute | solution.py:528
  21.4 0.4 %shard_map.73.refs_4_ = f32[3,8,32,128]{3,2,1,0:T(8,128)S(1)} custom-call(f32[3,8,32,128]{3,2,1,0:T(8,128)S(1)} %get-tuple-element.38.refs_0_, f32[6,8,32,128]{3,2,1,0:T(8,128)S(1)} %get-tuple-element.46.refs_1_, f32[3,8,32,128]{3,2,1,0:T(8,128)S(1)} %get-tuple-element.32.refs_3_.refs_2_), custom_call_target="tpu_custom_call" | custom-call | flops 1966080 | bytes 2097152 | tf_op jit(solution)/shard_map/pallas_call | solution.py:506
  21.8 0.0 collective-permute-done.10.refs_7_
  21.8 1.9 %collective-permute-done.11.refs_8_ = f32[64,128]{1,0:T(8,128)S(1)} collective-permute-done((f32[64,128]{1,0:T(8,128)S(1)}, f32[64,128]{1,0:T(8,128)S(1)}, u32[]{:S(2)}, u32[]{:S(2)}) %collective-permute-start.11) | collective-permute-done | bytes 32800 | tf_op jit(solution)/shard_map/ppermute | solution.py:528
  23.7 0.0 collective-permute-done.8.refs_5_
  23.7 0.0 collective-permute-done.9.refs_6_
  23.7 0.2 shard_map.74
  23.9 1.7 %collective-permute-start.12 = (f32[160,128]{1,0:T(8,128)S(1)}, f32[160,128]{1,0:T(8,128)S(1)}, u32[]{:S(2)}, u32[]{:S(2)}) collective-permute-start(f32[160,128]{1,0:T(8,128)S(1)} %get-tuple-element.56), channel_id=1, source_target_pairs={{0,8},{1,9},{2,10},{3,11},{4,12},{5,13},{6,14},{7,15},{8,0},{9,1},... | collective-permute-start | bytes 245768 | tf_op jit(solution)/shard_map/ppermute | solution.py:528
  25.6 0.0 collective-permute-start.13
  25.6 0.5 %collective-permute-start.14 = (f32[64,128]{1,0:T(8,128)S(1)}, f32[64,128]{1,0:T(8,128)S(1)}, u32[]{:S(2)}, u32[]{:S(2)}) collective-permute-start(f32[64,128]{1,0:T(8,128)S(1)} %get-tuple-element.58), channel_id=1, source_target_pairs={{0,1},{1,0},{2,3},{3,2},{4,5},{5,4},{6,7},{7,6},{8,9},{9,8},{10,11... | collective-permute-start | bytes 98312 | tf_op jit(solution)/shard_map/ppermute | solution.py:528
  26.1 1.4 %collective-permute-start.15 = (f32[64,128]{1,0:T(8,128)S(1)}, f32[64,128]{1,0:T(8,128)S(1)}, u32[]{:S(2)}, u32[]{:S(2)}) collective-permute-start(f32[64,128]{1,0:T(8,128)S(1)} %get-tuple-element.59), channel_id=1, source_target_pairs={{0,16},{1,2},{2,1},{3,4},{4,3},{5,6},{6,5},{7,23},{8,24},{9,10},{1... | collective-permute-start | bytes 98312 | tf_op jit(solution)/shard_map/ppermute | solution.py:528
  27.5 1.1 %shard_map.75 = (f32[6,8,32,128]{3,2,1,0:T(8,128)S(1)}, f32[3,8,32,128]{3,2,1,0:T(8,128)}) custom-call(f32[3,8,32,128]{3,2,1,0:T(8,128)S(1)} %get-tuple-element.52.refs_0_, f32[6,8,32,128]{3,2,1,0:T(8,128)S(1)} %get-tuple-element.46.refs_1_, f32[8,32,128]{2,1,0:T(8,128)S(1)} %copy-done.2, f32[8,32,128]{2,1,0:T(8,128)S(1)} %copy-done.1, ...), custom_call_target="tpu_custom_call" | custom-call | flops 2621440 | bytes 2097152 | tf_op jit(solution)/shard_map/pallas_call | solution.py:506
  28.6 0.0 collective-permute-done.14.refs_9_
  28.6 1.5 %collective-permute-done.15.refs_10_ = f32[64,128]{1,0:T(8,128)S(1)} collective-permute-done((f32[64,128]{1,0:T(8,128)S(1)}, f32[64,128]{1,0:T(8,128)S(1)}, u32[]{:S(2)}, u32[]{:S(2)}) %collective-permute-start.15) | collective-permute-done | bytes 32800 | tf_op jit(solution)/shard_map/ppermute | solution.py:528
  30.1 0.0 collective-permute-done.12.refs_7_
  30.1 0.0 collective-permute-done.13.refs_8_
  30.1 1.0 %shard_map.76 = f32[6,8,32,128]{3,2,1,0:T(8,128)} custom-call(f32[3,8,32,128]{3,2,1,0:T(8,128)S(1)} %get-tuple-element.52.refs_0_, f32[6,8,32,128]{3,2,1,0:T(8,128)S(1)} %get-tuple-element.46.refs_1_, f32[8,32,128]{2,1,0:T(8,128)S(1)} %copy-done.2, f32[8,32,128]{2,1,0:T(8,128)S(1)} %copy-done.1, f32[3,8,32,128]{3,2,1,0:T(8,128)S(1)} %get-tuple-element.40.refs_5_.refs_4_, ...), custom_call_target="tpu_custom_call" | custom-call | flops 655360 | bytes 2097152 | tf_op jit(solution)/shard_map/pallas_call | solution.py:506
  (3 shorter events, 0.0 us)
Async XLA Ops:
  0.6 5.8 %copy-start = (f32[6,8,32,128]{3,2,1,0:T(8,128)S(1)}, f32[6,8,32,128]{3,2,1,0:T(8,128)}, u32[]{:S(2)}) copy-start(f32[6,8,32,128]{3,2,1,0:T(8,128)} %refs_1_.7) | copy-start | bytes 2359300
  0.6 5.8 %copy-start.4 = (f32[8,32,128]{2,1,0:T(8,128)S(1)}, f32[8,32,128]{2,1,0:T(8,128)}, u32[]{:S(2)}) copy-start(f32[8,32,128]{2,1,0:T(8,128)} %density.1) | copy-start | bytes 393220
  1.9 7.4 %collective-permute-start = (f32[192,128]{1,0:T(8,128)S(1)}, f32[192,128]{1,0:T(8,128)S(1)}, u32[]{:S(2)}, u32[]{:S(2)}) collective-permute-start(f32[192,128]{1,0:T(8,128)S(1)} %get-tuple-element.34), channel_id=1, source_target_pairs={{0,8},{1,9},{2,10},{3,11},{4,12},{5,13},{6,14},{7,15},{8,0},{9,1},... | collective-permute-start | bytes 294920 | tf_op jit(solution)/shard_map/ppermute | solution.py:528
  4.9 4.4 %collective-permute-start.1 = (f32[192,128]{1,0:T(8,128)S(1)}, f32[192,128]{1,0:T(8,128)S(1)}, u32[]{:S(2)}, u32[]{:S(2)}) collective-permute-start(f32[192,128]{1,0:T(8,128)S(1)} %get-tuple-element.35), channel_id=1, source_target_pairs={{0,1},{1,0},{2,3},{3,2},{4,5},{5,4},{6,7},{7,6},{8,16},{9,17},{10,... | collective-permute-start | bytes 294920 | tf_op jit(solution)/shard_map/ppermute | solution.py:528
  4.9 3.0 %collective-permute-start.2 = (f32[64,128]{1,0:T(8,128)S(1)}, f32[64,128]{1,0:T(8,128)S(1)}, u32[]{:S(2)}, u32[]{:S(2)}) collective-permute-start(f32[64,128]{1,0:T(8,128)S(1)} %get-tuple-element.36), channel_id=1, source_target_pairs={{0,1},{1,0},{2,3},{3,2},{4,5},{5,4},{6,7},{7,6},{8,9},{9,8},{10,11... | collective-permute-start | bytes 98312 | tf_op jit(solution)/shard_map/ppermute | solution.py:528
  5.4 3.9 %collective-permute-start.3 = (f32[64,128]{1,0:T(8,128)S(1)}, f32[64,128]{1,0:T(8,128)S(1)}, u32[]{:S(2)}, u32[]{:S(2)}) collective-permute-start(f32[64,128]{1,0:T(8,128)S(1)} %get-tuple-element.37), channel_id=1, source_target_pairs={{0,16},{1,2},{2,1},{3,4},{4,3},{5,6},{6,5},{7,23},{8,24},{9,10},{1... | collective-permute-start | bytes 98312 | tf_op jit(solution)/shard_map/ppermute | solution.py:528
  6.4 1.0 %copy-start.3 = (f32[3,8,32,128]{3,2,1,0:T(8,128)S(1)}, f32[3,8,32,128]{3,2,1,0:T(8,128)}, u32[]{:S(2)}) copy-start(f32[3,8,32,128]{3,2,1,0:T(8,128)} %refs_0_.3) | copy-start | bytes 1179652
  9.3 5.4 %copy-start.1 = (f32[8,32,128]{2,1,0:T(8,128)S(1)}, f32[8,32,128]{2,1,0:T(8,128)}, u32[]{:S(2)}) copy-start(f32[8,32,128]{2,1,0:T(8,128)} %refs_3_.7) | copy-start | bytes 393220
  9.3 5.4 %copy-start.2 = (f32[8,32,128]{2,1,0:T(8,128)S(1)}, f32[8,32,128]{2,1,0:T(8,128)}, u32[]{:S(2)}) copy-start(f32[8,32,128]{2,1,0:T(8,128)} %refs_2_.9) | copy-start | bytes 393220
  9.5 8.0 %collective-permute-start.4 = (f32[168,128]{1,0:T(8,128)S(1)}, f32[168,128]{1,0:T(8,128)S(1)}, u32[]{:S(2)}, u32[]{:S(2)}) collective-permute-start(f32[168,128]{1,0:T(8,128)S(1)} %get-tuple-element.42), channel_id=1, source_target_pairs={{0,8},{1,9},{2,10},{3,11},{4,12},{5,13},{6,14},{7,15},{8,0},{9,1},... | collective-permute-start | bytes 258056 | tf_op jit(solution)/shard_map/ppermute | solution.py:528
  13.1 4.4 %collective-permute-start.5 = (f32[168,128]{1,0:T(8,128)S(1)}, f32[168,128]{1,0:T(8,128)S(1)}, u32[]{:S(2)}, u32[]{:S(2)}) collective-permute-start(f32[168,128]{1,0:T(8,128)S(1)} %get-tuple-element.43), channel_id=1, source_target_pairs={{0,1},{1,0},{2,3},{3,2},{4,5},{5,4},{6,7},{7,6},{8,16},{9,17},{10,... | collective-permute-start | bytes 258056 | tf_op jit(solution)/shard_map/ppermute | solution.py:528
  13.1 2.0 %collective-permute-start.6 = (f32[64,128]{1,0:T(8,128)S(1)}, f32[64,128]{1,0:T(8,128)S(1)}, u32[]{:S(2)}, u32[]{:S(2)}) collective-permute-start(f32[64,128]{1,0:T(8,128)S(1)} %get-tuple-element.44), channel_id=1, source_target_pairs={{0,1},{1,0},{2,3},{3,2},{4,5},{5,4},{6,7},{7,6},{8,9},{9,8},{10,11... | collective-permute-start | bytes 98312 | tf_op jit(solution)/shard_map/ppermute | solution.py:528
  13.7 3.9 %collective-permute-start.7 = (f32[64,128]{1,0:T(8,128)S(1)}, f32[64,128]{1,0:T(8,128)S(1)}, u32[]{:S(2)}, u32[]{:S(2)}) collective-permute-start(f32[64,128]{1,0:T(8,128)S(1)} %get-tuple-element.45), channel_id=1, source_target_pairs={{0,16},{1,2},{2,1},{3,4},{4,3},{5,6},{6,5},{7,23},{8,24},{9,10},{1... | collective-permute-start | bytes 98312 | tf_op jit(solution)/shard_map/ppermute | solution.py:528
  17.8 5.9 %collective-permute-start.8 = (f32[160,128]{1,0:T(8,128)S(1)}, f32[160,128]{1,0:T(8,128)S(1)}, u32[]{:S(2)}, u32[]{:S(2)}) collective-permute-start(f32[160,128]{1,0:T(8,128)S(1)} %get-tuple-element.48), channel_id=1, source_target_pairs={{0,8},{1,9},{2,10},{3,11},{4,12},{5,13},{6,14},{7,15},{8,0},{9,1},... | collective-permute-start | bytes 245768 | tf_op jit(solution)/shard_map/ppermute | solution.py:528
  19.3 4.4 %collective-permute-start.9 = (f32[160,128]{1,0:T(8,128)S(1)}, f32[160,128]{1,0:T(8,128)S(1)}, u32[]{:S(2)}, u32[]{:S(2)}) collective-permute-start(f32[160,128]{1,0:T(8,128)S(1)} %get-tuple-element.49), channel_id=1, source_target_pairs={{0,1},{1,0},{2,3},{3,2},{4,5},{5,4},{6,7},{7,6},{8,16},{9,17},{10,... | collective-permute-start | bytes 245768 | tf_op jit(solution)/shard_map/ppermute | solution.py:528
  19.3 2.5 %collective-permute-start.10 = (f32[64,128]{1,0:T(8,128)S(1)}, f32[64,128]{1,0:T(8,128)S(1)}, u32[]{:S(2)}, u32[]{:S(2)}) collective-permute-start(f32[64,128]{1,0:T(8,128)S(1)} %get-tuple-element.50), channel_id=1, source_target_pairs={{0,1},{1,0},{2,3},{3,2},{4,5},{5,4},{6,7},{7,6},{8,9},{9,8},{10,11... | collective-permute-start | bytes 98312 | tf_op jit(solution)/shard_map/ppermute | solution.py:528
  19.8 3.9 %collective-permute-start.11 = (f32[64,128]{1,0:T(8,128)S(1)}, f32[64,128]{1,0:T(8,128)S(1)}, u32[]{:S(2)}, u32[]{:S(2)}) collective-permute-start(f32[64,128]{1,0:T(8,128)S(1)} %get-tuple-element.51), channel_id=1, source_target_pairs={{0,16},{1,2},{2,1},{3,4},{4,3},{5,6},{6,5},{7,23},{8,24},{9,10},{1... | collective-permute-start | bytes 98312 | tf_op jit(solution)/shard_map/ppermute | solution.py:528
  23.9 6.1 %collective-permute-start.12 = (f32[160,128]{1,0:T(8,128)S(1)}, f32[160,128]{1,0:T(8,128)S(1)}, u32[]{:S(2)}, u32[]{:S(2)}) collective-permute-start(f32[160,128]{1,0:T(8,128)S(1)} %get-tuple-element.56), channel_id=1, source_target_pairs={{0,8},{1,9},{2,10},{3,11},{4,12},{5,13},{6,14},{7,15},{8,0},{9,1},... | collective-permute-start | bytes 245768 | tf_op jit(solution)/shard_map/ppermute | solution.py:528
  25.6 4.4 %collective-permute-start.13 = (f32[160,128]{1,0:T(8,128)S(1)}, f32[160,128]{1,0:T(8,128)S(1)}, u32[]{:S(2)}, u32[]{:S(2)}) collective-permute-start(f32[160,128]{1,0:T(8,128)S(1)} %get-tuple-element.57), channel_id=1, source_target_pairs={{0,1},{1,0},{2,3},{3,2},{4,5},{5,4},{6,7},{7,6},{8,16},{9,17},{10,... | collective-permute-start | bytes 245768 | tf_op jit(solution)/shard_map/ppermute | solution.py:528
  25.6 2.9 %collective-permute-start.14 = (f32[64,128]{1,0:T(8,128)S(1)}, f32[64,128]{1,0:T(8,128)S(1)}, u32[]{:S(2)}, u32[]{:S(2)}) collective-permute-start(f32[64,128]{1,0:T(8,128)S(1)} %get-tuple-element.58), channel_id=1, source_target_pairs={{0,1},{1,0},{2,3},{3,2},{4,5},{5,4},{6,7},{7,6},{8,9},{9,8},{10,11... | collective-permute-start | bytes 98312 | tf_op jit(solution)/shard_map/ppermute | solution.py:528
  26.1 3.9 %collective-permute-start.15 = (f32[64,128]{1,0:T(8,128)S(1)}, f32[64,128]{1,0:T(8,128)S(1)}, u32[]{:S(2)}, u32[]{:S(2)}) collective-permute-start(f32[64,128]{1,0:T(8,128)S(1)} %get-tuple-element.59), channel_id=1, source_target_pairs={{0,16},{1,2},{2,1},{3,4},{4,3},{5,6},{6,5},{7,23},{8,24},{9,10},{1... | collective-permute-start | bytes 98312 | tf_op jit(solution)/shard_map/ppermute | solution.py:528

commit v4 on v3

--- a/solution.py
+++ b/solution.py
@@ -38,7 +38,7 @@
     def outer_y(i, j):
         return (i, across(j, count_y)) if 0 < j < count_y - 1 else (i ^ other, j)
 
-    return [route(rule) for rule in (inner_x, outer_x, inner_y, outer_y)]
+    return [route(rule) for rule in (outer_x, inner_x, outer_y, inner_y)]
 
 
 def position():
@@ -85,8 +85,9 @@
 
 def put_rows(items, count_x):
     def put(out):
+        each = out.shape[0] // count_x
         for x in range(count_x):
-            start = tile * x
+            start = each * x
             for ref, f, row, count in items:
                 out[pl.ds(start, count), :] = ref[f, x, pl.ds(row, count), :]
                 start += count
@@ -163,18 +164,19 @@
 
 def fill_edges(ref, f, edge, lows, highs, low_row, low_count, high_row, high_count):
     nx, ny = ref.shape[-3], ref.shape[-2]
+    each = lows.shape[0] // nx
     for x in range(nx):
         if low_count:
-            edge[0, x, pl.ds(tile - low_count, low_count), :] = lows[pl.ds(tile * x + low_row, low_count), :]
+            edge[0, x, pl.ds(tile - low_count, low_count), :] = lows[pl.ds(each * x + low_row, low_count), :]
             edge[0, x, pl.ds(tile, tile), :] = ref[f, x, pl.ds(0, tile), :]
         if high_count:
             edge[1, x, pl.ds(0, tile), :] = ref[f, x, pl.ds(ny - tile, tile), :]
-            edge[1, x, pl.ds(tile, high_count), :] = highs[pl.ds(tile * x + high_row, high_count), :]
+            edge[1, x, pl.ds(tile, high_count), :] = highs[pl.ds(each * x + high_row, high_count), :]
 
 
 def receive(got, halos):
     i, j, even_x, even_y = position()
-    ax, bx, ay, by = got
+    bx, ax, by, ay = got
     low_x, high_x, low_y, high_y = halos
     first_x, last_x, first_y, last_y = sides(i, j)
     unpack(ax, bx, low_x, high_x, even_x, first_x, last_x)
@@ -182,45 +184,48 @@
     return even_x, even_y, last_x, last_y
 
 
-def first_pack(stress, density, shear, ax, bx, ay, by, tiles, sems):
+def first_pack(stress, density, shear, bx, ax, by, ay, tiles, sems):
     i, j, even_x, even_y = position()
     nx, ny = density.shape[0], density.shape[1]
-    planes_up = [(stress, 3, nx - 2), (stress, 3, nx - 1), (stress, 4, nx - 2), (stress, 4, nx - 1), (stress, 0, nx - 1)]
-    planes_down = [(stress, 3, 0), (stress, 4, 0), (stress, 0, 0), (stress, 0, 1), (density, None, 0), (shear, None, 0)]
-    columns = [(stress, 3, ny - tile), (stress, 5, ny - tile), (stress, 1, ny - tile),
-               (stress, 3, 0), (stress, 5, 0), (stress, 1, 0), (density, None, 0), (shear, None, 0)]
-
-    def plane_copies(items, out, sem):
-        copies = []
-        for n, (ref, f, x) in enumerate(items):
-            source = ref.at[x] if f is None else ref.at[f, x]
-            copies.append(pltpu.make_async_copy(source, out.at[pl.ds(n * ny, ny), :], sem.at[n]))
-        return copies
-
-    copies = []
-    for n, (ref, f, row) in enumerate(columns):
-        source = ref if f is None else ref.at[f]
-        copies.append(pltpu.make_async_copy(source.at[:, pl.ds(row, tile), :], tiles.at[n], sems.at[2, n]))
+    copies = [
+        pltpu.make_async_copy(stress.at[:, :, pl.ds(ny - tile, tile), :], tiles.at[pl.ds(0, 6)], sems.at[0]),
+        pltpu.make_async_copy(stress.at[:, :, pl.ds(0, tile), :], tiles.at[pl.ds(6, 6)], sems.at[0]),
+        pltpu.make_async_copy(density.at[:, pl.ds(0, tile), :], tiles.at[12], sems.at[0]),
+        pltpu.make_async_copy(shear.at[:, pl.ds(0, tile), :], tiles.at[13], sems.at[0]),
+    ]
     for copy in copies:
         copy.start()
 
+    def up(out):
+        return [
+            pltpu.make_async_copy(stress.at[f, x], out.at[pl.ds(n * ny, ny), :], sems.at[1])
+            for n, (f, x) in enumerate([(3, nx - 2), (3, nx - 1), (4, nx - 2), (4, nx - 1), (0, nx - 1)])
+        ]
+
+    def down(out):
+        sources = [stress.at[3, 0], stress.at[4, 0], stress.at[0, 0], stress.at[0, 1], density.at[0], shear.at[0]]
+        return [
+            pltpu.make_async_copy(source, out.at[pl.ds(n * ny, ny), :], sems.at[2])
+            for n, source in enumerate(sources)
+        ]
+
     @pl.when(even_x)
     def _():
-        for copy in plane_copies(planes_up, ax, sems.at[0]) + plane_copies(planes_down, bx, sems.at[1]):
+        for copy in up(ax) + down(bx):
             copy.start()
 
     @pl.when(jnp.logical_not(even_x))
     def _():
-        for copy in plane_copies(planes_up, bx, sems.at[0]) + plane_copies(planes_down, ax, sems.at[1]):
+        for copy in up(bx) + down(ax):
             copy.start()
 
     for copy in copies:
         copy.wait()
     Pack(ay, by, even_y).put(
-        put_rows([(tiles, 0, tile - 2, 2), (tiles, 1, tile - 2, 2), (tiles, 2, tile - 1, 1)], nx),
-        put_rows([(tiles, 3, 0, 1), (tiles, 4, 0, 1), (tiles, 5, 0, 2), (tiles, 6, 0, 1), (tiles, 7, 0, 1)], nx),
+        put_rows([(tiles, 3, tile - 2, 2), (tiles, 5, tile - 2, 2), (tiles, 1, tile - 1, 1)], nx),
+        put_rows([(tiles, 9, 0, 1), (tiles, 11, 0, 1), (tiles, 7, 0, 2), (tiles, 12, 0, 1), (tiles, 13, 0, 1)], nx),
     )
-    for copy in plane_copies(planes_up, ax, sems.at[0]) + plane_copies(planes_down, bx, sems.at[1]):
+    for copy in up(ax) + down(bx):
         copy.wait()
 
 
@@ -272,13 +277,13 @@
 
 def velocity_edges(step, *refs):
     if step == 0:
-        (velocity, stress, buoy, buoys, part, ax, bx, ay, by, out, buoys_end, pax, pbx, pay, pby,
+        (velocity, stress, buoy, buoys, part, bx, ax, by, ay, out, buoys_end, pbx, pax, pby, pay,
          low_x, high_x, low_y, high_y, edges, edge_b) = refs
     else:
-        (velocity, stress, buoys, buoys_end, part, ax, bx, ay, by, out, pax, pbx, pay, pby,
+        (velocity, stress, buoys, buoys_end, part, bx, ax, by, ay, out, pbx, pax, pby, pay,
          low_x, high_x, low_y, high_y, edges) = refs
     nx, ny = stress.shape[1], stress.shape[2]
-    even_x, even_y, last_x, last_y = receive((ax, bx, ay, by), (low_x, high_x, low_y, high_y))
+    even_x, even_y, last_x, last_y = receive((bx, ax, by, ay), (low_x, high_x, low_y, high_y))
     fill_edges(stress, 3, edges.at[0], low_y, high_y, 0, 2, 0, 1)
     fill_edges(stress, 5, edges.at[1], low_y, high_y, 2, 2, 1, 1)
     fill_edges(stress, 1, edges.at[2], low_y, high_y, 4, 1, 2, 2)
@@ -293,7 +298,7 @@
         rows = pl.ds(ny - tile, tile)
         for x in range(nx):
             here = buoy[0, x, rows, :]
-            row = high_y[pl.ds(tile * x + 4, 1), :]
+            row = high_y[pl.ds(high_y.shape[0] // nx * x + 4, 1), :]
             edge_b[pl.ds(0, tile), :] = here
             edge_b[pl.ds(tile, 1), :] = jnp.where(last_y, 0.0, 1.0 / jnp.where(last_y, 1.0, row))
             buoys_end[pl.ds(ny + tile * x, tile), :] = half * (here + edge_b[pl.ds(1, tile), :])
@@ -351,7 +356,7 @@
 
 def stress_inside(step, *refs):
     if step == 0:
-        velocity, stress, lam, shear, ax, bx, ay, by, out, shears, halo_c, comps, edge_c = refs
+        velocity, stress, lam, shear, bx, ax, by, ay, out, shears, halo_c, comps, edge_c = refs
     else:
         velocity, stress, lam, shear, shears, out, final_velocity, sem = refs
     nx, ny = stress.shape[1], stress.shape[2]
@@ -366,7 +371,7 @@
         for x in range(nx):
             comps[x] = 1.0 / shear[x]
             edge_c[x, pl.ds(0, tile), :] = comps[x, pl.ds(ny - tile, tile), :]
-            row = pl.ds(tile * x + 5, 1)
+            row = pl.ds(ay.shape[0] // nx * x + 5, 1)
             value = jnp.where(last_y, 1.0, jnp.where(even_y, ay[row, :], by[row, :]))
             edge_c[x, pl.ds(tile, 1), :] = jnp.where(last_y, 0.0, 1.0 / value)
         for t in range(ny // tile):
@@ -428,13 +433,13 @@
 
 def stress_edges(step, *refs):
     if step == 0:
-        (velocity, stress, lam, shear, halo_c, shears, part, ax, bx, ay, by,
-         out, shear_end, pax, pbx, pay, pby, low_x, high_x, low_y, high_y, edges, corner) = refs
+        (velocity, stress, lam, shear, halo_c, shears, part, bx, ax, by, ay,
+         out, shear_end, pbx, pax, pby, pay, low_x, high_x, low_y, high_y, edges, corner) = refs
     else:
-        (velocity, stress, lam, shear, shears, shear_end, part, ax, bx, ay, by,
+        (velocity, stress, lam, shear, shears, shear_end, part, bx, ax, by, ay,
          final_stress, low_x, high_x, low_y, high_y, edges, out, sems) = refs
     nx, ny = stress.shape[1], stress.shape[2]
-    even_x, even_y, _, _ = receive((ax, bx, ay, by), (low_x, high_x, low_y, high_y))
+    even_x, even_y, _, _ = receive((bx, ax, by, ay), (low_x, high_x, low_y, high_y))
     fill_edges(velocity, 1, edges.at[0], low_y, high_y, 0, 2, 0, 1)
     fill_edges(velocity, 0, edges.at[1], low_y, high_y, 2, 1, 1, 2)
     fill_edges(velocity, 2, edges.at[2], low_y, high_y, 3, 1, 3, 2)
@@ -521,27 +526,27 @@
     one, three = (1, nx, ny, nz), (3, nx, ny, nz)
     dma = pltpu.SemaphoreType.DMA
 
-    def packages(x_rows):
-        return [(x_rows, nz)] * 2 + [(nx * tile, nz)] * 2
+    def packages(x_rows, y_rows=5):
+        return [(x_rows, nz)] * 2 + [(nx * y_rows, nz)] * 2
 
     def exchange(arrays):
         return [lax.ppermute(array, AXES, route) for array, route in zip(arrays, routes)]
 
-    def halos(x_rows):
-        return packages(x_rows) + [(3, 2, nx, 2 * tile, nz)]
+    def halos(*rows):
+        return packages(*rows) + [(3, 2, nx, 2 * tile, nz)]
 
     def kernel(function, step):
         return lambda *refs: function(step, *refs)
 
-    first, second, later = 6 * ny, 5 * ny + tile, 5 * ny
+    first, second, later = (6 * ny, 6), 5 * ny + tile, 5 * ny
     packed = call(
-        first_pack, packages(first), [(8, nx, tile, nz), dma((3, 8))],
+        first_pack, packages(*first), [(14, nx, tile, nz), dma((4,))],
         (stress, density, lame_mu), cells, hbm_in=(0, 1, 2))
     got = exchange(packed)
     part, buoy, buoys = call(
         kernel(velocity_inside, 0), [three, one, three], [], (velocity, stress, density), 60 * cells)
     new_velocity, buoys_end, *packed = call(
-        kernel(velocity_edges, 0), [three, (ny + nx * tile, nz)] + packages(second), halos(first) + [(2 * tile, nz)],
+        kernel(velocity_edges, 0), [three, (ny + nx * tile, nz)] + packages(second), halos(*first) + [(2 * tile, nz)],
         (velocity, stress, buoy, buoys, part, *got), 20 * cells)
     materials = got
     got = exchange(packed)

time: 31.3 us -> 30.7 us (0.981)
  waiting for transfers between devices: 7.28 us -> 6.09 us
  starting transfers between devices: 16.8 us -> 17.4 us
    ppermute x16, waiting for transfers between devices: 7.28 us -> 6.09 us  [exchange(): lax.ppermute(array, AXES, route)]
    ppermute x16, starting transfers between devices: 16.8 us -> 17.4 us  [exchange(): lax.ppermute(array, AXES, route)]
  transfers between devices with their start and end apart: 16 -> 16, of which waited for: 4 -> 6; matrix products, arithmetic and copies ran while one was open for 0% -> 0% of each run, Pallas kernels for 7% -> 8%
where the time goes in v4:
time: 30.7 us; the launch traced here: 30.4 us
  starting transfers between devices  17.4 us (57%)
  waiting for transfers between devices  6.09 us (20%)
  Pallas kernels  5.18 us (17%)
  local copies, waits for them, and re-layouts  1.01 us (3%)
  between operations  0.75 us (2%)
    ppermute x16, starting transfers between devices, exchange(): lax.ppermute(array, AXES, route)  17.4 us
    ppermute x16, waiting for transfers between devices, exchange(): lax.ppermute(array, AXES, route)  6.09 us
    pallas_call x9, Pallas kernels, call(): pl.pallas_call(kernel, out_shape=[(pltpu.HBM if n in hbm_out else pltpu.V...  5.18 us
    unnamed x10, local copies, waits for them, and re-layouts  1.01 us
  transfers between devices with their start and end apart: 16, of which 6 were waited for; matrix products, arithmetic and copies ran while one was open for 0% of the time, Pallas kernels for 8%

profile of v4, /device:TPU:0, one launch (start us, length us, event | category | flops | bytes accessed | tf_op | source)
XLA Modules:
  0.0 30.4 jit_solution(14821659788655335136)
XLA Ops:
  0.6 0.0 copy-start
  0.6 0.0 copy-start.4
  0.6 1.2 %shard_map.69 = (f32[192,128]{1,0:T(8,128)S(1)}, f32[192,128]{1,0:T(8,128)S(1)}, f32[48,128]{1,0:T(8,128)S(1)}, f32[48,128]{1,0:T(8,128)S(1)}) custom-call(f32[6,8,32,128]{3,2,1,0:T(8,128)} %refs_1_.7, f32[8,32,128]{2,1,0:T(8,128)} %density.1, f32[8,32,128]{2,1,0:T(8,128)} %refs_3_.7), custom_call_target="tpu_custom_call" | custom-call | flops 32768 | bytes 2097152 | tf_op jit(solution)/shard_map/pallas_call | solution.py:511
  1.8 0.5 %collective-permute-start = (f32[192,128]{1,0:T(8,128)S(1)}, f32[192,128]{1,0:T(8,128)S(1)}, u32[]{:S(2)}, u32[]{:S(2)}) collective-permute-start(f32[192,128]{1,0:T(8,128)S(1)} %get-tuple-element.34), channel_id=1, source_target_pairs={{0,1},{1,0},{2,3},{3,2},{4,5},{5,4},{6,7},{7,6},{8,16},{9,17},{10,... | collective-permute-start | bytes 294920 | tf_op jit(solution)/shard_map/ppermute | solution.py:533
  2.3 4.0 %collective-permute-start.1 = (f32[192,128]{1,0:T(8,128)S(1)}, f32[192,128]{1,0:T(8,128)S(1)}, u32[]{:S(2)}, u32[]{:S(2)}) collective-permute-start(f32[192,128]{1,0:T(8,128)S(1)} %get-tuple-element.35), channel_id=1, source_target_pairs={{0,8},{1,9},{2,10},{3,11},{4,12},{5,13},{6,14},{7,15},{8,0},{9,1},... | collective-permute-start | bytes 294920 | tf_op jit(solution)/shard_map/ppermute | solution.py:533
  6.3 0.1 collective-permute-start.2
  6.4 1.6 %collective-permute-start.3 = (f32[48,128]{1,0:T(8,128)S(1)}, f32[48,128]{1,0:T(8,128)S(1)}, u32[]{:S(2)}, u32[]{:S(2)}) collective-permute-start(f32[48,128]{1,0:T(8,128)S(1)} %get-tuple-element.37), channel_id=1, source_target_pairs={{0,1},{1,0},{2,3},{3,2},{4,5},{5,4},{6,7},{7,6},{8,9},{9,8},{10,11... | collective-permute-start | bytes 73736 | tf_op jit(solution)/shard_map/ppermute | solution.py:533
  8.0 0.0 copy-done
  8.0 0.0 copy-done.4
  8.0 1.0 %copy-done.3 = f32[3,8,32,128]{3,2,1,0:T(8,128)S(1)} copy-done((f32[3,8,32,128]{3,2,1,0:T(8,128)S(1)}, f32[3,8,32,128]{3,2,1,0:T(8,128)}, u32[]{:S(2)}) %copy-start.3) | copy-done | bytes 393240
  9.0 0.4 %shard_map.68 = (f32[3,8,32,128]{3,2,1,0:T(8,128)S(1)}, f32[1,8,32,128]{3,2,1,0:T(8,128)S(1)}, f32[3,8,32,128]{3,2,1,0:T(8,128)S(1)}) custom-call(f32[3,8,32,128]{3,2,1,0:T(8,128)S(1)} %copy-done.3, f32[6,8,32,128]{3,2,1,0:T(8,128)S(1)} %copy-done, f32[8,32,128]{2,1,0:T(8,128)S(1)} %copy-done.4), custom_call_target="tpu_custom_call" | custom-call | flops 1966080 | bytes 2097152 | tf_op jit(solution)/shard_map/pallas_call | solution.py:511
  9.4 0.7 %collective-permute-done.2.refs_7_.refs_6_ = f32[48,128]{1,0:T(8,128)S(1)} collective-permute-done((f32[48,128]{1,0:T(8,128)S(1)}, f32[48,128]{1,0:T(8,128)S(1)}, u32[]{:S(2)}, u32[]{:S(2)}) %collective-permute-start.2) | collective-permute-done | bytes 24608 | tf_op jit(solution)/shard_map/ppermute | solution.py:533
  10.1 0.0 collective-permute-done.3.refs_8_.refs_7_
  10.1 0.0 collective-permute-done.refs_5_.refs_4_
  10.2 0.8 %collective-permute-done.1.refs_6_.refs_5_ = f32[192,128]{1,0:T(8,128)S(1)} collective-permute-done((f32[192,128]{1,0:T(8,128)S(1)}, f32[192,128]{1,0:T(8,128)S(1)}, u32[]{:S(2)}, u32[]{:S(2)}) %collective-permute-start.1) | collective-permute-done | bytes 98336 | tf_op jit(solution)/shard_map/ppermute | solution.py:533
  10.9 0.2 shard_map.70
  11.2 0.1 collective-permute-start.4
  11.2 1.9 %collective-permute-start.5 = (f32[168,128]{1,0:T(8,128)S(1)}, f32[168,128]{1,0:T(8,128)S(1)}, u32[]{:S(2)}, u32[]{:S(2)}) collective-permute-start(f32[168,128]{1,0:T(8,128)S(1)} %get-tuple-element.43), channel_id=1, source_target_pairs={{0,8},{1,9},{2,10},{3,11},{4,12},{5,13},{6,14},{7,15},{8,0},{9,1},... | collective-permute-start | bytes 258056 | tf_op jit(solution)/shard_map/ppermute | solution.py:533
  13.1 0.2 collective-permute-start.6
  13.3 1.5 %collective-permute-start.7 = (f32[40,128]{1,0:T(8,128)S(1)}, f32[40,128]{1,0:T(8,128)S(1)}, u32[]{:S(2)}, u32[]{:S(2)}) collective-permute-start(f32[40,128]{1,0:T(8,128)S(1)} %get-tuple-element.45), channel_id=1, source_target_pairs={{0,1},{1,0},{2,3},{3,2},{4,5},{5,4},{6,7},{7,6},{8,9},{9,8},{10,11... | collective-permute-start | bytes 61448 | tf_op jit(solution)/shard_map/ppermute | solution.py:533
  14.8 0.0 copy-done.1
  14.8 0.0 copy-done.2
  14.8 0.5 %shard_map.71 = (f32[6,8,32,128]{3,2,1,0:T(8,128)S(1)}, f32[3,8,32,128]{3,2,1,0:T(8,128)S(1)}, f32[40,128]{1,0:T(8,128)S(1)}) custom-call(f32[3,8,32,128]{3,2,1,0:T(8,128)S(1)} %get-tuple-element.38.refs_0_, f32[6,8,32,128]{3,2,1,0:T(8,128)S(1)} %copy-done, f32[8,32,128]{2,1,0:T(8,128)S(1)} %copy-done.2, f32[8,32,128]{2,1,0:T(8,128)S(1)} %copy-done.1, ...), custom_call_target="tpu_custom_call" | custom-call | flops 2621440 | bytes 2097152 | tf_op jit(solution)/shard_map/pallas_call | solution.py:511
  15.3 1.6 %collective-permute-done.6.refs_9_ = f32[40,128]{1,0:T(8,128)S(1)} collective-permute-done((f32[40,128]{1,0:T(8,128)S(1)}, f32[40,128]{1,0:T(8,128)S(1)}, u32[]{:S(2)}, u32[]{:S(2)}) %collective-permute-start.6) | collective-permute-done | bytes 20512 | tf_op jit(solution)/shard_map/ppermute | solution.py:533
  16.9 0.0 collective-permute-done.7.refs_10_
  16.9 0.0 collective-permute-done.4.refs_7_
  16.9 0.2 collective-permute-done.5.refs_8_
  17.1 0.2 shard_map.72
  17.3 0.1 collective-permute-start.8
  17.4 2.0 %collective-permute-start.9 = (f32[160,128]{1,0:T(8,128)S(1)}, f32[160,128]{1,0:T(8,128)S(1)}, u32[]{:S(2)}, u32[]{:S(2)}) collective-permute-start(f32[160,128]{1,0:T(8,128)S(1)} %get-tuple-element.49), channel_id=1, source_target_pairs={{0,8},{1,9},{2,10},{3,11},{4,12},{5,13},{6,14},{7,15},{8,0},{9,1},... | collective-permute-start | bytes 245768 | tf_op jit(solution)/shard_map/ppermute | solution.py:533
  19.4 0.1 collective-permute-start.10
  19.5 1.6 %collective-permute-start.11 = (f32[40,128]{1,0:T(8,128)S(1)}, f32[40,128]{1,0:T(8,128)S(1)}, u32[]{:S(2)}, u32[]{:S(2)}) collective-permute-start(f32[40,128]{1,0:T(8,128)S(1)} %get-tuple-element.51), channel_id=1, source_target_pairs={{0,1},{1,0},{2,3},{3,2},{4,5},{5,4},{6,7},{7,6},{8,9},{9,8},{10,11... | collective-permute-start | bytes 61448 | tf_op jit(solution)/shard_map/ppermute | solution.py:533
  21.1 0.4 %shard_map.73.refs_4_ = f32[3,8,32,128]{3,2,1,0:T(8,128)S(1)} custom-call(f32[3,8,32,128]{3,2,1,0:T(8,128)S(1)} %get-tuple-element.38.refs_0_, f32[6,8,32,128]{3,2,1,0:T(8,128)S(1)} %get-tuple-element.46.refs_1_, f32[3,8,32,128]{3,2,1,0:T(8,128)S(1)} %get-tuple-element.32.refs_3_.refs_2_), custom_call_target="tpu_custom_call" | custom-call | flops 1966080 | bytes 2097152 | tf_op jit(solution)/shard_map/pallas_call | solution.py:511
  21.5 1.7 %collective-permute-done.10.refs_7_ = f32[40,128]{1,0:T(8,128)S(1)} collective-permute-done((f32[40,128]{1,0:T(8,128)S(1)}, f32[40,128]{1,0:T(8,128)S(1)}, u32[]{:S(2)}, u32[]{:S(2)}) %collective-permute-start.10) | collective-permute-done | bytes 20512 | tf_op jit(solution)/shard_map/ppermute | solution.py:533
  23.2 0.0 collective-permute-done.11.refs_8_
  23.2 0.0 collective-permute-done.8.refs_5_
  23.2 0.0 collective-permute-done.9.refs_6_
  23.2 0.2 shard_map.74
  23.5 0.1 collective-permute-start.12
  23.5 2.1 %collective-permute-start.13 = (f32[160,128]{1,0:T(8,128)S(1)}, f32[160,128]{1,0:T(8,128)S(1)}, u32[]{:S(2)}, u32[]{:S(2)}) collective-permute-start(f32[160,128]{1,0:T(8,128)S(1)} %get-tuple-element.57), channel_id=1, source_target_pairs={{0,8},{1,9},{2,10},{3,11},{4,12},{5,13},{6,14},{7,15},{8,0},{9,1},... | collective-permute-start | bytes 245768 | tf_op jit(solution)/shard_map/ppermute | solution.py:533
  25.6 0.0 collective-permute-start.14
  25.6 1.7 %collective-permute-start.15 = (f32[40,128]{1,0:T(8,128)S(1)}, f32[40,128]{1,0:T(8,128)S(1)}, u32[]{:S(2)}, u32[]{:S(2)}) collective-permute-start(f32[40,128]{1,0:T(8,128)S(1)} %get-tuple-element.59), channel_id=1, source_target_pairs={{0,1},{1,0},{2,3},{3,2},{4,5},{5,4},{6,7},{7,6},{8,9},{9,8},{10,11... | collective-permute-start | bytes 61448 | tf_op jit(solution)/shard_map/ppermute | solution.py:533
  27.3 1.1 %shard_map.75 = (f32[6,8,32,128]{3,2,1,0:T(8,128)S(1)}, f32[3,8,32,128]{3,2,1,0:T(8,128)}) custom-call(f32[3,8,32,128]{3,2,1,0:T(8,128)S(1)} %get-tuple-element.52.refs_0_, f32[6,8,32,128]{3,2,1,0:T(8,128)S(1)} %get-tuple-element.46.refs_1_, f32[8,32,128]{2,1,0:T(8,128)S(1)} %copy-done.2, f32[8,32,128]{2,1,0:T(8,128)S(1)} %copy-done.1, ...), custom_call_target="tpu_custom_call" | custom-call | flops 2621440 | bytes 2097152 | tf_op jit(solution)/shard_map/pallas_call | solution.py:511
  28.4 1.0 %collective-permute-done.14.refs_9_ = f32[40,128]{1,0:T(8,128)S(1)} collective-permute-done((f32[40,128]{1,0:T(8,128)S(1)}, f32[40,128]{1,0:T(8,128)S(1)}, u32[]{:S(2)}, u32[]{:S(2)}) %collective-permute-start.14) | collective-permute-done | bytes 20512 | tf_op jit(solution)/shard_map/ppermute | solution.py:533
  29.4 0.0 collective-permute-done.15.refs_10_
  29.4 0.0 collective-permute-done.12.refs_7_
  29.4 0.0 collective-permute-done.13.refs_8_
  29.4 1.0 %shard_map.76 = f32[6,8,32,128]{3,2,1,0:T(8,128)} custom-call(f32[3,8,32,128]{3,2,1,0:T(8,128)S(1)} %get-tuple-element.52.refs_0_, f32[6,8,32,128]{3,2,1,0:T(8,128)S(1)} %get-tuple-element.46.refs_1_, f32[8,32,128]{2,1,0:T(8,128)S(1)} %copy-done.2, f32[8,32,128]{2,1,0:T(8,128)S(1)} %copy-done.1, f32[3,8,32,128]{3,2,1,0:T(8,128)S(1)} %get-tuple-element.40.refs_5_.refs_4_, ...), custom_call_target="tpu_custom_call" | custom-call | flops 655360 | bytes 2097152 | tf_op jit(solution)/shard_map/pallas_call | solution.py:511
  (3 shorter events, 0.0 us)
Async XLA Ops:
  0.6 7.4 %copy-start = (f32[6,8,32,128]{3,2,1,0:T(8,128)S(1)}, f32[6,8,32,128]{3,2,1,0:T(8,128)}, u32[]{:S(2)}) copy-start(f32[6,8,32,128]{3,2,1,0:T(8,128)} %refs_1_.7) | copy-start | bytes 2359300
  0.6 7.4 %copy-start.4 = (f32[8,32,128]{2,1,0:T(8,128)S(1)}, f32[8,32,128]{2,1,0:T(8,128)}, u32[]{:S(2)}) copy-start(f32[8,32,128]{2,1,0:T(8,128)} %density.1) | copy-start | bytes 393220
  1.8 8.3 %collective-permute-start = (f32[192,128]{1,0:T(8,128)S(1)}, f32[192,128]{1,0:T(8,128)S(1)}, u32[]{:S(2)}, u32[]{:S(2)}) collective-permute-start(f32[192,128]{1,0:T(8,128)S(1)} %get-tuple-element.34), channel_id=1, source_target_pairs={{0,1},{1,0},{2,3},{3,2},{4,5},{5,4},{6,7},{7,6},{8,16},{9,17},{10,... | collective-permute-start | bytes 294920 | tf_op jit(solution)/shard_map/ppermute | solution.py:533
  2.3 8.6 %collective-permute-start.1 = (f32[192,128]{1,0:T(8,128)S(1)}, f32[192,128]{1,0:T(8,128)S(1)}, u32[]{:S(2)}, u32[]{:S(2)}) collective-permute-start(f32[192,128]{1,0:T(8,128)S(1)} %get-tuple-element.35), channel_id=1, source_target_pairs={{0,8},{1,9},{2,10},{3,11},{4,12},{5,13},{6,14},{7,15},{8,0},{9,1},... | collective-permute-start | bytes 294920 | tf_op jit(solution)/shard_map/ppermute | solution.py:533
  6.3 3.8 %collective-permute-start.2 = (f32[48,128]{1,0:T(8,128)S(1)}, f32[48,128]{1,0:T(8,128)S(1)}, u32[]{:S(2)}, u32[]{:S(2)}) collective-permute-start(f32[48,128]{1,0:T(8,128)S(1)} %get-tuple-element.36), channel_id=1, source_target_pairs={{0,16},{1,2},{2,1},{3,4},{4,3},{5,6},{6,5},{7,23},{8,24},{9,10},{1... | collective-permute-start | bytes 73736 | tf_op jit(solution)/shard_map/ppermute | solution.py:533
  6.4 3.7 %collective-permute-start.3 = (f32[48,128]{1,0:T(8,128)S(1)}, f32[48,128]{1,0:T(8,128)S(1)}, u32[]{:S(2)}, u32[]{:S(2)}) collective-permute-start(f32[48,128]{1,0:T(8,128)S(1)} %get-tuple-element.37), channel_id=1, source_target_pairs={{0,1},{1,0},{2,3},{3,2},{4,5},{5,4},{6,7},{7,6},{8,9},{9,8},{10,11... | collective-permute-start | bytes 73736 | tf_op jit(solution)/shard_map/ppermute | solution.py:533
  8.0 1.0 %copy-start.3 = (f32[3,8,32,128]{3,2,1,0:T(8,128)S(1)}, f32[3,8,32,128]{3,2,1,0:T(8,128)}, u32[]{:S(2)}) copy-start(f32[3,8,32,128]{3,2,1,0:T(8,128)} %refs_0_.3) | copy-start | bytes 1179652
  10.9 3.9 %copy-start.1 = (f32[8,32,128]{2,1,0:T(8,128)S(1)}, f32[8,32,128]{2,1,0:T(8,128)}, u32[]{:S(2)}) copy-start(f32[8,32,128]{2,1,0:T(8,128)} %refs_3_.7) | copy-start | bytes 393220
  10.9 3.9 %copy-start.2 = (f32[8,32,128]{2,1,0:T(8,128)S(1)}, f32[8,32,128]{2,1,0:T(8,128)}, u32[]{:S(2)}) copy-start(f32[8,32,128]{2,1,0:T(8,128)} %refs_2_.9) | copy-start | bytes 393220
  11.2 5.7 %collective-permute-start.4 = (f32[168,128]{1,0:T(8,128)S(1)}, f32[168,128]{1,0:T(8,128)S(1)}, u32[]{:S(2)}, u32[]{:S(2)}) collective-permute-start(f32[168,128]{1,0:T(8,128)S(1)} %get-tuple-element.42), channel_id=1, source_target_pairs={{0,1},{1,0},{2,3},{3,2},{4,5},{5,4},{6,7},{7,6},{8,16},{9,17},{10,... | collective-permute-start | bytes 258056 | tf_op jit(solution)/shard_map/ppermute | solution.py:533
  11.2 5.9 %collective-permute-start.5 = (f32[168,128]{1,0:T(8,128)S(1)}, f32[168,128]{1,0:T(8,128)S(1)}, u32[]{:S(2)}, u32[]{:S(2)}) collective-permute-start(f32[168,128]{1,0:T(8,128)S(1)} %get-tuple-element.43), channel_id=1, source_target_pairs={{0,8},{1,9},{2,10},{3,11},{4,12},{5,13},{6,14},{7,15},{8,0},{9,1},... | collective-permute-start | bytes 258056 | tf_op jit(solution)/shard_map/ppermute | solution.py:533
  13.1 3.8 %collective-permute-start.6 = (f32[40,128]{1,0:T(8,128)S(1)}, f32[40,128]{1,0:T(8,128)S(1)}, u32[]{:S(2)}, u32[]{:S(2)}) collective-permute-start(f32[40,128]{1,0:T(8,128)S(1)} %get-tuple-element.44), channel_id=1, source_target_pairs={{0,16},{1,2},{2,1},{3,4},{4,3},{5,6},{6,5},{7,23},{8,24},{9,10},{1... | collective-permute-start | bytes 61448 | tf_op jit(solution)/shard_map/ppermute | solution.py:533
  13.3 3.6 %collective-permute-start.7 = (f32[40,128]{1,0:T(8,128)S(1)}, f32[40,128]{1,0:T(8,128)S(1)}, u32[]{:S(2)}, u32[]{:S(2)}) collective-permute-start(f32[40,128]{1,0:T(8,128)S(1)} %get-tuple-element.45), channel_id=1, source_target_pairs={{0,1},{1,0},{2,3},{3,2},{4,5},{5,4},{6,7},{7,6},{8,9},{9,8},{10,11... | collective-permute-start | bytes 61448 | tf_op jit(solution)/shard_map/ppermute | solution.py:533
  17.3 5.9 %collective-permute-start.8 = (f32[160,128]{1,0:T(8,128)S(1)}, f32[160,128]{1,0:T(8,128)S(1)}, u32[]{:S(2)}, u32[]{:S(2)}) collective-permute-start(f32[160,128]{1,0:T(8,128)S(1)} %get-tuple-element.48), channel_id=1, source_target_pairs={{0,1},{1,0},{2,3},{3,2},{4,5},{5,4},{6,7},{7,6},{8,16},{9,17},{10,... | collective-permute-start | bytes 245768 | tf_op jit(solution)/shard_map/ppermute | solution.py:533
  17.4 5.8 %collective-permute-start.9 = (f32[160,128]{1,0:T(8,128)S(1)}, f32[160,128]{1,0:T(8,128)S(1)}, u32[]{:S(2)}, u32[]{:S(2)}) collective-permute-start(f32[160,128]{1,0:T(8,128)S(1)} %get-tuple-element.49), channel_id=1, source_target_pairs={{0,8},{1,9},{2,10},{3,11},{4,12},{5,13},{6,14},{7,15},{8,0},{9,1},... | collective-permute-start | bytes 245768 | tf_op jit(solution)/shard_map/ppermute | solution.py:533
  19.4 3.8 %collective-permute-start.10 = (f32[40,128]{1,0:T(8,128)S(1)}, f32[40,128]{1,0:T(8,128)S(1)}, u32[]{:S(2)}, u32[]{:S(2)}) collective-permute-start(f32[40,128]{1,0:T(8,128)S(1)} %get-tuple-element.50), channel_id=1, source_target_pairs={{0,16},{1,2},{2,1},{3,4},{4,3},{5,6},{6,5},{7,23},{8,24},{9,10},{1... | collective-permute-start | bytes 61448 | tf_op jit(solution)/shard_map/ppermute | solution.py:533
  19.5 3.7 %collective-permute-start.11 = (f32[40,128]{1,0:T(8,128)S(1)}, f32[40,128]{1,0:T(8,128)S(1)}, u32[]{:S(2)}, u32[]{:S(2)}) collective-permute-start(f32[40,128]{1,0:T(8,128)S(1)} %get-tuple-element.51), channel_id=1, source_target_pairs={{0,1},{1,0},{2,3},{3,2},{4,5},{5,4},{6,7},{7,6},{8,9},{9,8},{10,11... | collective-permute-start | bytes 61448 | tf_op jit(solution)/shard_map/ppermute | solution.py:533
  23.5 5.9 %collective-permute-start.12 = (f32[160,128]{1,0:T(8,128)S(1)}, f32[160,128]{1,0:T(8,128)S(1)}, u32[]{:S(2)}, u32[]{:S(2)}) collective-permute-start(f32[160,128]{1,0:T(8,128)S(1)} %get-tuple-element.56), channel_id=1, source_target_pairs={{0,1},{1,0},{2,3},{3,2},{4,5},{5,4},{6,7},{7,6},{8,16},{9,17},{10,... | collective-permute-start | bytes 245768 | tf_op jit(solution)/shard_map/ppermute | solution.py:533
  23.5 5.9 %collective-permute-start.13 = (f32[160,128]{1,0:T(8,128)S(1)}, f32[160,128]{1,0:T(8,128)S(1)}, u32[]{:S(2)}, u32[]{:S(2)}) collective-permute-start(f32[160,128]{1,0:T(8,128)S(1)} %get-tuple-element.57), channel_id=1, source_target_pairs={{0,8},{1,9},{2,10},{3,11},{4,12},{5,13},{6,14},{7,15},{8,0},{9,1},... | collective-permute-start | bytes 245768 | tf_op jit(solution)/shard_map/ppermute | solution.py:533
  25.6 3.8 %collective-permute-start.14 = (f32[40,128]{1,0:T(8,128)S(1)}, f32[40,128]{1,0:T(8,128)S(1)}, u32[]{:S(2)}, u32[]{:S(2)}) collective-permute-start(f32[40,128]{1,0:T(8,128)S(1)} %get-tuple-element.58), channel_id=1, source_target_pairs={{0,16},{1,2},{2,1},{3,4},{4,3},{5,6},{6,5},{7,23},{8,24},{9,10},{1... | collective-permute-start | bytes 61448 | tf_op jit(solution)/shard_map/ppermute | solution.py:533
  25.6 3.8 %collective-permute-start.15 = (f32[40,128]{1,0:T(8,128)S(1)}, f32[40,128]{1,0:T(8,128)S(1)}, u32[]{:S(2)}, u32[]{:S(2)}) collective-permute-start(f32[40,128]{1,0:T(8,128)S(1)} %get-tuple-element.59), channel_id=1, source_target_pairs={{0,1},{1,0},{2,3},{3,2},{4,5},{5,4},{6,7},{7,6},{8,9},{9,8},{10,11... | collective-permute-start | bytes 61448 | tf_op jit(solution)/shard_map/ppermute | solution.py:533

commit v5 on v4

--- a/solution.py
+++ b/solution.py
@@ -38,7 +38,7 @@
     def outer_y(i, j):
         return (i, across(j, count_y)) if 0 < j < count_y - 1 else (i ^ other, j)
 
-    return [route(rule) for rule in (outer_x, inner_x, outer_y, inner_y)]
+    return [route(rule) for rule in (inner_x, outer_x, outer_y, inner_y)]
 
 
 def position():
@@ -176,7 +176,7 @@
 
 def receive(got, halos):
     i, j, even_x, even_y = position()
-    bx, ax, by, ay = got
+    ax, bx, by, ay = got
     low_x, high_x, low_y, high_y = halos
     first_x, last_x, first_y, last_y = sides(i, j)
     unpack(ax, bx, low_x, high_x, even_x, first_x, last_x)
@@ -184,7 +184,7 @@
     return even_x, even_y, last_x, last_y
 
 
-def first_pack(stress, density, shear, bx, ax, by, ay, tiles, sems):
+def first_pack(stress, density, shear, ax, bx, by, ay, tiles, sems):
     i, j, even_x, even_y = position()
     nx, ny = density.shape[0], density.shape[1]
     copies = [
@@ -277,13 +277,13 @@
 
 def velocity_edges(step, *refs):
     if step == 0:
-        (velocity, stress, buoy, buoys, part, bx, ax, by, ay, out, buoys_end, pbx, pax, pby, pay,
+        (velocity, stress, buoy, buoys, part, ax, bx, by, ay, out, buoys_end, pax, pbx, pby, pay,
          low_x, high_x, low_y, high_y, edges, edge_b) = refs
     else:
-        (velocity, stress, buoys, buoys_end, part, bx, ax, by, ay, out, pbx, pax, pby, pay,
+        (velocity, stress, buoys, buoys_end, part, ax, bx, by, ay, out, pax, pbx, pby, pay,
          low_x, high_x, low_y, high_y, edges) = refs
     nx, ny = stress.shape[1], stress.shape[2]
-    even_x, even_y, last_x, last_y = receive((bx, ax, by, ay), (low_x, high_x, low_y, high_y))
+    even_x, even_y, last_x, last_y = receive((ax, bx, by, ay), (low_x, high_x, low_y, high_y))
     fill_edges(stress, 3, edges.at[0], low_y, high_y, 0, 2, 0, 1)
     fill_edges(stress, 5, edges.at[1], low_y, high_y, 2, 2, 1, 1)
     fill_edges(stress, 1, edges.at[2], low_y, high_y, 4, 1, 2, 2)
@@ -356,7 +356,7 @@
 
 def stress_inside(step, *refs):
     if step == 0:
-        velocity, stress, lam, shear, bx, ax, by, ay, out, shears, halo_c, comps, edge_c = refs
+        velocity, stress, lam, shear, ax, bx, by, ay, out, shears, halo_c, comps, edge_c = refs
     else:
         velocity, stress, lam, shear, shears, out, final_velocity, sem = refs
     nx, ny = stress.shape[1], stress.shape[2]
@@ -433,13 +433,13 @@
 
 def stress_edges(step, *refs):
     if step == 0:
-        (velocity, stress, lam, shear, halo_c, shears, part, bx, ax, by, ay,
-         out, shear_end, pbx, pax, pby, pay, low_x, high_x, low_y, high_y, edges, corner) = refs
+        (velocity, stress, lam, shear, halo_c, shears, part, ax, bx, by, ay,
+         out, shear_end, pax, pbx, pby, pay, low_x, high_x, low_y, high_y, edges, corner) = refs
     else:
-        (velocity, stress, lam, shear, shears, shear_end, part, bx, ax, by, ay,
+        (velocity, stress, lam, shear, shears, shear_end, part, ax, bx, by, ay,
          final_stress, low_x, high_x, low_y, high_y, edges, out, sems) = refs
     nx, ny = stress.shape[1], stress.shape[2]
-    even_x, even_y, _, _ = receive((bx, ax, by, ay), (low_x, high_x, low_y, high_y))
+    even_x, even_y, _, _ = receive((ax, bx, by, ay), (low_x, high_x, low_y, high_y))
     fill_edges(velocity, 1, edges.at[0], low_y, high_y, 0, 2, 0, 1)
     fill_edges(velocity, 0, edges.at[1], low_y, high_y, 2, 1, 1, 2)
     fill_edges(velocity, 2, edges.at[2], low_y, high_y, 3, 1, 3, 2)

time: 30.7 us -> 30.1 us (0.980)
  waiting for transfers between devices: 6.09 us -> 5.28 us
    ppermute x16, waiting for transfers between devices: 6.09 us -> 5.28 us  [exchange(): lax.ppermute(array, AXES, route)]
  transfers between devices with their start and end apart: 16 -> 16, of which waited for: 6 -> 4; matrix products, arithmetic and copies ran while one was open for 0% -> 0% of each run, Pallas kernels for 8% -> 8%
where the time goes in v5:
time: 30.1 us; the launch traced here: 29.9 us
  starting transfers between devices  17.6 us (58%)
  waiting for transfers between devices  5.28 us (18%)
  Pallas kernels  5.19 us (17%)
  local copies, waits for them, and re-layouts  1.02 us (3%)
  between operations  0.75 us (2%)
    ppermute x16, starting transfers between devices, exchange(): lax.ppermute(array, AXES, route)  17.6 us
    ppermute x16, waiting for transfers between devices, exchange(): lax.ppermute(array, AXES, route)  5.28 us
    pallas_call x9, Pallas kernels, call(): pl.pallas_call(kernel, out_shape=[(pltpu.HBM if n in hbm_out else pltpu.V...  5.19 us
    unnamed x10, local copies, waits for them, and re-layouts  1.02 us
  transfers between devices with their start and end apart: 16, of which 4 were waited for; matrix products, arithmetic and copies ran while one was open for 0% of the time, Pallas kernels for 8%

profile of v5, /device:TPU:0, one launch (start us, length us, event | category | flops | bytes accessed | tf_op | source)
XLA Modules:
  0.0 29.9 jit_solution(16304777525955568912)
XLA Ops:
  0.6 0.0 copy-start
  0.6 0.0 copy-start.4
  0.6 1.2 %shard_map.69 = (f32[192,128]{1,0:T(8,128)S(1)}, f32[192,128]{1,0:T(8,128)S(1)}, f32[48,128]{1,0:T(8,128)S(1)}, f32[48,128]{1,0:T(8,128)S(1)}) custom-call(f32[6,8,32,128]{3,2,1,0:T(8,128)} %refs_1_.7, f32[8,32,128]{2,1,0:T(8,128)} %density.1, f32[8,32,128]{2,1,0:T(8,128)} %refs_3_.7), custom_call_target="tpu_custom_call" | custom-call | flops 32768 | bytes 2097152 | tf_op jit(solution)/shard_map/pallas_call | solution.py:511
  1.8 3.0 %collective-permute-start = (f32[192,128]{1,0:T(8,128)S(1)}, f32[192,128]{1,0:T(8,128)S(1)}, u32[]{:S(2)}, u32[]{:S(2)}) collective-permute-start(f32[192,128]{1,0:T(8,128)S(1)} %get-tuple-element.34), channel_id=1, source_target_pairs={{0,8},{1,9},{2,10},{3,11},{4,12},{5,13},{6,14},{7,15},{8,0},{9,1},... | collective-permute-start | bytes 294920 | tf_op jit(solution)/shard_map/ppermute | solution.py:533
  4.8 0.0 collective-permute-start.1
  4.8 1.5 %collective-permute-start.2 = (f32[48,128]{1,0:T(8,128)S(1)}, f32[48,128]{1,0:T(8,128)S(1)}, u32[]{:S(2)}, u32[]{:S(2)}) collective-permute-start(f32[48,128]{1,0:T(8,128)S(1)} %get-tuple-element.36), channel_id=1, source_target_pairs={{0,16},{1,2},{2,1},{3,4},{4,3},{5,6},{6,5},{7,23},{8,24},{9,10},{1... | collective-permute-start | bytes 73736 | tf_op jit(solution)/shard_map/ppermute | solution.py:533
  6.4 0.2 collective-permute-start.3
  6.5 0.0 copy-done
  6.5 0.0 copy-done.4
  6.5 1.0 %copy-done.3 = f32[3,8,32,128]{3,2,1,0:T(8,128)S(1)} copy-done((f32[3,8,32,128]{3,2,1,0:T(8,128)S(1)}, f32[3,8,32,128]{3,2,1,0:T(8,128)}, u32[]{:S(2)}) %copy-start.3) | copy-done | bytes 393240
  7.5 0.4 %shard_map.68 = (f32[3,8,32,128]{3,2,1,0:T(8,128)S(1)}, f32[1,8,32,128]{3,2,1,0:T(8,128)S(1)}, f32[3,8,32,128]{3,2,1,0:T(8,128)S(1)}) custom-call(f32[3,8,32,128]{3,2,1,0:T(8,128)S(1)} %copy-done.3, f32[6,8,32,128]{3,2,1,0:T(8,128)S(1)} %copy-done, f32[8,32,128]{2,1,0:T(8,128)S(1)} %copy-done.4), custom_call_target="tpu_custom_call" | custom-call | flops 1966080 | bytes 2097152 | tf_op jit(solution)/shard_map/pallas_call | solution.py:511
  7.9 0.7 %collective-permute-done.2.refs_7_.refs_6_ = f32[48,128]{1,0:T(8,128)S(1)} collective-permute-done((f32[48,128]{1,0:T(8,128)S(1)}, f32[48,128]{1,0:T(8,128)S(1)}, u32[]{:S(2)}, u32[]{:S(2)}) %collective-permute-start.2) | collective-permute-done | bytes 24608 | tf_op jit(solution)/shard_map/ppermute | solution.py:533
  8.7 0.0 collective-permute-done.3.refs_8_.refs_7_
  8.7 0.0 collective-permute-done.refs_5_.refs_4_
  8.7 0.0 collective-permute-done.1.refs_6_.refs_5_
  8.7 0.0 copy-start.1
  8.7 0.0 copy-start.2
  8.7 0.2 shard_map.70
  8.9 4.1 %collective-permute-start.4 = (f32[168,128]{1,0:T(8,128)S(1)}, f32[168,128]{1,0:T(8,128)S(1)}, u32[]{:S(2)}, u32[]{:S(2)}) collective-permute-start(f32[168,128]{1,0:T(8,128)S(1)} %get-tuple-element.42), channel_id=1, source_target_pairs={{0,8},{1,9},{2,10},{3,11},{4,12},{5,13},{6,14},{7,15},{8,0},{9,1},... | collective-permute-start | bytes 258056 | tf_op jit(solution)/shard_map/ppermute | solution.py:533
  13.0 0.0 collective-permute-start.5
  13.0 1.5 %collective-permute-start.6 = (f32[40,128]{1,0:T(8,128)S(1)}, f32[40,128]{1,0:T(8,128)S(1)}, u32[]{:S(2)}, u32[]{:S(2)}) collective-permute-start(f32[40,128]{1,0:T(8,128)S(1)} %get-tuple-element.44), channel_id=1, source_target_pairs={{0,16},{1,2},{2,1},{3,4},{4,3},{5,6},{6,5},{7,23},{8,24},{9,10},{1... | collective-permute-start | bytes 61448 | tf_op jit(solution)/shard_map/ppermute | solution.py:533
  14.6 0.0 collective-permute-start.7
  14.6 0.5 %shard_map.71 = (f32[6,8,32,128]{3,2,1,0:T(8,128)S(1)}, f32[3,8,32,128]{3,2,1,0:T(8,128)S(1)}, f32[40,128]{1,0:T(8,128)S(1)}) custom-call(f32[3,8,32,128]{3,2,1,0:T(8,128)S(1)} %get-tuple-element.38.refs_0_, f32[6,8,32,128]{3,2,1,0:T(8,128)S(1)} %copy-done, f32[8,32,128]{2,1,0:T(8,128)S(1)} %copy-done.2, f32[8,32,128]{2,1,0:T(8,128)S(1)} %copy-done.1, ...), custom_call_target="tpu_custom_call" | custom-call | flops 2621440 | bytes 2097152 | tf_op jit(solution)/shard_map/pallas_call | solution.py:511
  15.1 1.7 %collective-permute-done.6.refs_9_ = f32[40,128]{1,0:T(8,128)S(1)} collective-permute-done((f32[40,128]{1,0:T(8,128)S(1)}, f32[40,128]{1,0:T(8,128)S(1)}, u32[]{:S(2)}, u32[]{:S(2)}) %collective-permute-start.6) | collective-permute-done | bytes 20512 | tf_op jit(solution)/shard_map/ppermute | solution.py:533
  16.8 0.0 collective-permute-done.7.refs_10_
  16.8 0.0 collective-permute-done.4.refs_7_
  16.8 0.0 collective-permute-done.5.refs_8_
  16.8 0.2 shard_map.72
  17.1 1.8 %collective-permute-start.8 = (f32[160,128]{1,0:T(8,128)S(1)}, f32[160,128]{1,0:T(8,128)S(1)}, u32[]{:S(2)}, u32[]{:S(2)}) collective-permute-start(f32[160,128]{1,0:T(8,128)S(1)} %get-tuple-element.48), channel_id=1, source_target_pairs={{0,8},{1,9},{2,10},{3,11},{4,12},{5,13},{6,14},{7,15},{8,0},{9,1},... | collective-permute-start | bytes 245768 | tf_op jit(solution)/shard_map/ppermute | solution.py:533
  18.8 0.0 collective-permute-start.9
  18.8 1.8 %collective-permute-start.10 = (f32[40,128]{1,0:T(8,128)S(1)}, f32[40,128]{1,0:T(8,128)S(1)}, u32[]{:S(2)}, u32[]{:S(2)}) collective-permute-start(f32[40,128]{1,0:T(8,128)S(1)} %get-tuple-element.50), channel_id=1, source_target_pairs={{0,16},{1,2},{2,1},{3,4},{4,3},{5,6},{6,5},{7,23},{8,24},{9,10},{1... | collective-permute-start | bytes 61448 | tf_op jit(solution)/shard_map/ppermute | solution.py:533
  20.6 0.0 collective-permute-start.11
  20.6 0.4 %shard_map.73.refs_4_ = f32[3,8,32,128]{3,2,1,0:T(8,128)S(1)} custom-call(f32[3,8,32,128]{3,2,1,0:T(8,128)S(1)} %get-tuple-element.38.refs_0_, f32[6,8,32,128]{3,2,1,0:T(8,128)S(1)} %get-tuple-element.46.refs_1_, f32[3,8,32,128]{3,2,1,0:T(8,128)S(1)} %get-tuple-element.32.refs_3_.refs_2_), custom_call_target="tpu_custom_call" | custom-call | flops 1966080 | bytes 2097152 | tf_op jit(solution)/shard_map/pallas_call | solution.py:511
  21.0 1.6 %collective-permute-done.10.refs_7_ = f32[40,128]{1,0:T(8,128)S(1)} collective-permute-done((f32[40,128]{1,0:T(8,128)S(1)}, f32[40,128]{1,0:T(8,128)S(1)}, u32[]{:S(2)}, u32[]{:S(2)}) %collective-permute-start.10) | collective-permute-done | bytes 20512 | tf_op jit(solution)/shard_map/ppermute | solution.py:533
  22.6 0.0 collective-permute-done.11.refs_8_
  22.6 0.0 collective-permute-done.8.refs_5_
  22.6 0.0 collective-permute-done.9.refs_6_
  22.6 0.2 shard_map.74
  22.9 2.2 %collective-permute-start.12 = (f32[160,128]{1,0:T(8,128)S(1)}, f32[160,128]{1,0:T(8,128)S(1)}, u32[]{:S(2)}, u32[]{:S(2)}) collective-permute-start(f32[160,128]{1,0:T(8,128)S(1)} %get-tuple-element.56), channel_id=1, source_target_pairs={{0,8},{1,9},{2,10},{3,11},{4,12},{5,13},{6,14},{7,15},{8,0},{9,1},... | collective-permute-start | bytes 245768 | tf_op jit(solution)/shard_map/ppermute | solution.py:533
  25.0 0.0 collective-permute-start.13
  25.1 1.5 %collective-permute-start.14 = (f32[40,128]{1,0:T(8,128)S(1)}, f32[40,128]{1,0:T(8,128)S(1)}, u32[]{:S(2)}, u32[]{:S(2)}) collective-permute-start(f32[40,128]{1,0:T(8,128)S(1)} %get-tuple-element.58), channel_id=1, source_target_pairs={{0,16},{1,2},{2,1},{3,4},{4,3},{5,6},{6,5},{7,23},{8,24},{9,10},{1... | collective-permute-start | bytes 61448 | tf_op jit(solution)/shard_map/ppermute | solution.py:533
  26.6 0.0 collective-permute-start.15
  26.6 1.1 %shard_map.75 = (f32[6,8,32,128]{3,2,1,0:T(8,128)S(1)}, f32[3,8,32,128]{3,2,1,0:T(8,128)}) custom-call(f32[3,8,32,128]{3,2,1,0:T(8,128)S(1)} %get-tuple-element.52.refs_0_, f32[6,8,32,128]{3,2,1,0:T(8,128)S(1)} %get-tuple-element.46.refs_1_, f32[8,32,128]{2,1,0:T(8,128)S(1)} %copy-done.2, f32[8,32,128]{2,1,0:T(8,128)S(1)} %copy-done.1, ...), custom_call_target="tpu_custom_call" | custom-call | flops 2621440 | bytes 2097152 | tf_op jit(solution)/shard_map/pallas_call | solution.py:511
  27.7 1.2 %collective-permute-done.14.refs_9_ = f32[40,128]{1,0:T(8,128)S(1)} collective-permute-done((f32[40,128]{1,0:T(8,128)S(1)}, f32[40,128]{1,0:T(8,128)S(1)}, u32[]{:S(2)}, u32[]{:S(2)}) %collective-permute-start.14) | collective-permute-done | bytes 20512 | tf_op jit(solution)/shard_map/ppermute | solution.py:533
  28.8 0.0 collective-permute-done.15.refs_10_
  28.8 0.0 collective-permute-done.12.refs_7_
  28.8 0.0 collective-permute-done.13.refs_8_
  28.8 1.0 %shard_map.76 = f32[6,8,32,128]{3,2,1,0:T(8,128)} custom-call(f32[3,8,32,128]{3,2,1,0:T(8,128)S(1)} %get-tuple-element.52.refs_0_, f32[6,8,32,128]{3,2,1,0:T(8,128)S(1)} %get-tuple-element.46.refs_1_, f32[8,32,128]{2,1,0:T(8,128)S(1)} %copy-done.2, f32[8,32,128]{2,1,0:T(8,128)S(1)} %copy-done.1, f32[3,8,32,128]{3,2,1,0:T(8,128)S(1)} %get-tuple-element.40.refs_5_.refs_4_, ...), custom_call_target="tpu_custom_call" | custom-call | flops 655360 | bytes 2097152 | tf_op jit(solution)/shard_map/pallas_call | solution.py:511
  (3 shorter events, 0.0 us)
Async XLA Ops:
  0.6 5.9 %copy-start = (f32[6,8,32,128]{3,2,1,0:T(8,128)S(1)}, f32[6,8,32,128]{3,2,1,0:T(8,128)}, u32[]{:S(2)}) copy-start(f32[6,8,32,128]{3,2,1,0:T(8,128)} %refs_1_.7) | copy-start | bytes 2359300
  0.6 5.9 %copy-start.4 = (f32[8,32,128]{2,1,0:T(8,128)S(1)}, f32[8,32,128]{2,1,0:T(8,128)}, u32[]{:S(2)}) copy-start(f32[8,32,128]{2,1,0:T(8,128)} %density.1) | copy-start | bytes 393220
  1.8 6.8 %collective-permute-start = (f32[192,128]{1,0:T(8,128)S(1)}, f32[192,128]{1,0:T(8,128)S(1)}, u32[]{:S(2)}, u32[]{:S(2)}) collective-permute-start(f32[192,128]{1,0:T(8,128)S(1)} %get-tuple-element.34), channel_id=1, source_target_pairs={{0,8},{1,9},{2,10},{3,11},{4,12},{5,13},{6,14},{7,15},{8,0},{9,1},... | collective-permute-start | bytes 294920 | tf_op jit(solution)/shard_map/ppermute | solution.py:533
  4.8 3.8 %collective-permute-start.1 = (f32[192,128]{1,0:T(8,128)S(1)}, f32[192,128]{1,0:T(8,128)S(1)}, u32[]{:S(2)}, u32[]{:S(2)}) collective-permute-start(f32[192,128]{1,0:T(8,128)S(1)} %get-tuple-element.35), channel_id=1, source_target_pairs={{0,1},{1,0},{2,3},{3,2},{4,5},{5,4},{6,7},{7,6},{8,16},{9,17},{10,... | collective-permute-start | bytes 294920 | tf_op jit(solution)/shard_map/ppermute | solution.py:533
  4.8 3.8 %collective-permute-start.2 = (f32[48,128]{1,0:T(8,128)S(1)}, f32[48,128]{1,0:T(8,128)S(1)}, u32[]{:S(2)}, u32[]{:S(2)}) collective-permute-start(f32[48,128]{1,0:T(8,128)S(1)} %get-tuple-element.36), channel_id=1, source_target_pairs={{0,16},{1,2},{2,1},{3,4},{4,3},{5,6},{6,5},{7,23},{8,24},{9,10},{1... | collective-permute-start | bytes 73736 | tf_op jit(solution)/shard_map/ppermute | solution.py:533
  6.4 2.3 %collective-permute-start.3 = (f32[48,128]{1,0:T(8,128)S(1)}, f32[48,128]{1,0:T(8,128)S(1)}, u32[]{:S(2)}, u32[]{:S(2)}) collective-permute-start(f32[48,128]{1,0:T(8,128)S(1)} %get-tuple-element.37), channel_id=1, source_target_pairs={{0,1},{1,0},{2,3},{3,2},{4,5},{5,4},{6,7},{7,6},{8,9},{9,8},{10,11... | collective-permute-start | bytes 73736 | tf_op jit(solution)/shard_map/ppermute | solution.py:533
  6.5 1.0 %copy-start.3 = (f32[3,8,32,128]{3,2,1,0:T(8,128)S(1)}, f32[3,8,32,128]{3,2,1,0:T(8,128)}, u32[]{:S(2)}) copy-start(f32[3,8,32,128]{3,2,1,0:T(8,128)} %refs_0_.3) | copy-start | bytes 1179652
  8.7 5.9 %copy-start.1 = (f32[8,32,128]{2,1,0:T(8,128)S(1)}, f32[8,32,128]{2,1,0:T(8,128)}, u32[]{:S(2)}) copy-start(f32[8,32,128]{2,1,0:T(8,128)} %refs_3_.7) | copy-start | bytes 393220
  8.7 5.9 %copy-start.2 = (f32[8,32,128]{2,1,0:T(8,128)S(1)}, f32[8,32,128]{2,1,0:T(8,128)}, u32[]{:S(2)}) copy-start(f32[8,32,128]{2,1,0:T(8,128)} %refs_2_.9) | copy-start | bytes 393220
  8.9 7.9 %collective-permute-start.4 = (f32[168,128]{1,0:T(8,128)S(1)}, f32[168,128]{1,0:T(8,128)S(1)}, u32[]{:S(2)}, u32[]{:S(2)}) collective-permute-start(f32[168,128]{1,0:T(8,128)S(1)} %get-tuple-element.42), channel_id=1, source_target_pairs={{0,8},{1,9},{2,10},{3,11},{4,12},{5,13},{6,14},{7,15},{8,0},{9,1},... | collective-permute-start | bytes 258056 | tf_op jit(solution)/shard_map/ppermute | solution.py:533
  13.0 3.8 %collective-permute-start.5 = (f32[168,128]{1,0:T(8,128)S(1)}, f32[168,128]{1,0:T(8,128)S(1)}, u32[]{:S(2)}, u32[]{:S(2)}) collective-permute-start(f32[168,128]{1,0:T(8,128)S(1)} %get-tuple-element.43), channel_id=1, source_target_pairs={{0,1},{1,0},{2,3},{3,2},{4,5},{5,4},{6,7},{7,6},{8,16},{9,17},{10,... | collective-permute-start | bytes 258056 | tf_op jit(solution)/shard_map/ppermute | solution.py:533
  13.0 3.8 %collective-permute-start.6 = (f32[40,128]{1,0:T(8,128)S(1)}, f32[40,128]{1,0:T(8,128)S(1)}, u32[]{:S(2)}, u32[]{:S(2)}) collective-permute-start(f32[40,128]{1,0:T(8,128)S(1)} %get-tuple-element.44), channel_id=1, source_target_pairs={{0,16},{1,2},{2,1},{3,4},{4,3},{5,6},{6,5},{7,23},{8,24},{9,10},{1... | collective-permute-start | bytes 61448 | tf_op jit(solution)/shard_map/ppermute | solution.py:533
  14.6 2.2 %collective-permute-start.7 = (f32[40,128]{1,0:T(8,128)S(1)}, f32[40,128]{1,0:T(8,128)S(1)}, u32[]{:S(2)}, u32[]{:S(2)}) collective-permute-start(f32[40,128]{1,0:T(8,128)S(1)} %get-tuple-element.45), channel_id=1, source_target_pairs={{0,1},{1,0},{2,3},{3,2},{4,5},{5,4},{6,7},{7,6},{8,9},{9,8},{10,11... | collective-permute-start | bytes 61448 | tf_op jit(solution)/shard_map/ppermute | solution.py:533
  17.1 5.5 %collective-permute-start.8 = (f32[160,128]{1,0:T(8,128)S(1)}, f32[160,128]{1,0:T(8,128)S(1)}, u32[]{:S(2)}, u32[]{:S(2)}) collective-permute-start(f32[160,128]{1,0:T(8,128)S(1)} %get-tuple-element.48), channel_id=1, source_target_pairs={{0,8},{1,9},{2,10},{3,11},{4,12},{5,13},{6,14},{7,15},{8,0},{9,1},... | collective-permute-start | bytes 245768 | tf_op jit(solution)/shard_map/ppermute | solution.py:533
  18.8 3.8 %collective-permute-start.9 = (f32[160,128]{1,0:T(8,128)S(1)}, f32[160,128]{1,0:T(8,128)S(1)}, u32[]{:S(2)}, u32[]{:S(2)}) collective-permute-start(f32[160,128]{1,0:T(8,128)S(1)} %get-tuple-element.49), channel_id=1, source_target_pairs={{0,1},{1,0},{2,3},{3,2},{4,5},{5,4},{6,7},{7,6},{8,16},{9,17},{10,... | collective-permute-start | bytes 245768 | tf_op jit(solution)/shard_map/ppermute | solution.py:533
  18.8 3.8 %collective-permute-start.10 = (f32[40,128]{1,0:T(8,128)S(1)}, f32[40,128]{1,0:T(8,128)S(1)}, u32[]{:S(2)}, u32[]{:S(2)}) collective-permute-start(f32[40,128]{1,0:T(8,128)S(1)} %get-tuple-element.50), channel_id=1, source_target_pairs={{0,16},{1,2},{2,1},{3,4},{4,3},{5,6},{6,5},{7,23},{8,24},{9,10},{1... | collective-permute-start | bytes 61448 | tf_op jit(solution)/shard_map/ppermute | solution.py:533
  20.6 2.0 %collective-permute-start.11 = (f32[40,128]{1,0:T(8,128)S(1)}, f32[40,128]{1,0:T(8,128)S(1)}, u32[]{:S(2)}, u32[]{:S(2)}) collective-permute-start(f32[40,128]{1,0:T(8,128)S(1)} %get-tuple-element.51), channel_id=1, source_target_pairs={{0,1},{1,0},{2,3},{3,2},{4,5},{5,4},{6,7},{7,6},{8,9},{9,8},{10,11... | collective-permute-start | bytes 61448 | tf_op jit(solution)/shard_map/ppermute | solution.py:533
  22.9 6.0 %collective-permute-start.12 = (f32[160,128]{1,0:T(8,128)S(1)}, f32[160,128]{1,0:T(8,128)S(1)}, u32[]{:S(2)}, u32[]{:S(2)}) collective-permute-start(f32[160,128]{1,0:T(8,128)S(1)} %get-tuple-element.56), channel_id=1, source_target_pairs={{0,8},{1,9},{2,10},{3,11},{4,12},{5,13},{6,14},{7,15},{8,0},{9,1},... | collective-permute-start | bytes 245768 | tf_op jit(solution)/shard_map/ppermute | solution.py:533
  25.0 3.8 %collective-permute-start.13 = (f32[160,128]{1,0:T(8,128)S(1)}, f32[160,128]{1,0:T(8,128)S(1)}, u32[]{:S(2)}, u32[]{:S(2)}) collective-permute-start(f32[160,128]{1,0:T(8,128)S(1)} %get-tuple-element.57), channel_id=1, source_target_pairs={{0,1},{1,0},{2,3},{3,2},{4,5},{5,4},{6,7},{7,6},{8,16},{9,17},{10,... | collective-permute-start | bytes 245768 | tf_op jit(solution)/shard_map/ppermute | solution.py:533
  25.1 3.8 %collective-permute-start.14 = (f32[40,128]{1,0:T(8,128)S(1)}, f32[40,128]{1,0:T(8,128)S(1)}, u32[]{:S(2)}, u32[]{:S(2)}) collective-permute-start(f32[40,128]{1,0:T(8,128)S(1)} %get-tuple-element.58), channel_id=1, source_target_pairs={{0,16},{1,2},{2,1},{3,4},{4,3},{5,6},{6,5},{7,23},{8,24},{9,10},{1... | collective-permute-start | bytes 61448 | tf_op jit(solution)/shard_map/ppermute | solution.py:533
  26.6 2.2 %collective-permute-start.15 = (f32[40,128]{1,0:T(8,128)S(1)}, f32[40,128]{1,0:T(8,128)S(1)}, u32[]{:S(2)}, u32[]{:S(2)}) collective-permute-start(f32[40,128]{1,0:T(8,128)S(1)} %get-tuple-element.59), channel_id=1, source_target_pairs={{0,1},{1,0},{2,3},{3,2},{4,5},{5,4},{6,7},{7,6},{8,9},{9,8},{10,11... | collective-permute-start | bytes 61448 | tf_op jit(solution)/shard_map/ppermute | solution.py:533

commit v6 on v5

--- a/solution.py
+++ b/solution.py
@@ -76,7 +76,7 @@
     def put(out):
         start = 0
         for ref, f, x in items:
-            value = ref[f, x]
+            value = ref[x] if f is None else ref[f, x]
             out[pl.ds(start, value.shape[0]), :] = value
             start += value.shape[0]
 
@@ -115,9 +115,9 @@
 
 
 class Field:
-    def __init__(self, ref, f, low_x=None, high_x=None, edge=None):
+    def __init__(self, ref, f, low_x=None, high_x=None, edge=None, last=None):
         self.ref, self.f = ref, f
-        self.low_x, self.high_x, self.edge = low_x, high_x, edge
+        self.low_x, self.high_x, self.edge, self.last = low_x, high_x, edge, last
 
     def at(self, x, t):
         nx, ny = self.ref.shape[-3], self.ref.shape[-2]
@@ -127,6 +127,8 @@
         if x >= nx:
             ref, index = self.high_x
             return ref[pl.ds(ny * (index + x - nx) + tile * t, tile), :]
+        if self.last is not None and x == nx - 1:
+            return self.last[pl.ds(tile * t, tile), :]
         return self.ref[self.f, x, pl.ds(tile * t, tile), :]
 
     def y(self, x, t, k):
@@ -156,6 +158,10 @@
 
 def inner_plane(x, base, nx):
     return x + base - 1 >= 0 and x + base + 2 < nx
+
+
+def inner_velocity_plane(step, c, x, base, nx):
+    return inner_plane(x, base, nx) and not (step == 1 and c == 2 and x == nx - 2)
 
 
 def inner_tile(t, ny):
@@ -184,30 +190,33 @@
     return even_x, even_y, last_x, last_y
 
 
-def first_pack(stress, density, shear, ax, bx, by, ay, tiles, sems):
+def first_pack(stress, density, shear, ax, bx, by, ay, ends, tiles, sems):
     i, j, even_x, even_y = position()
     nx, ny = density.shape[0], density.shape[1]
+    def up(out):
+        pairs = [
+            (stress.at[3, pl.ds(nx - 2, 2)], 0, 2), (stress.at[4, pl.ds(nx - 2, 2)], 2, 2),
+            (stress.at[0, pl.ds(nx - 1, 1)], 4, 1),
+        ]
+        return [pltpu.make_async_copy(source, out.at[pl.ds(n, count)], sems.at[1]) for source, n, count in pairs]
+
+    def down(out):
+        pairs = [
+            (stress.at[pl.ds(3, 2), 0], 0, 2), (stress.at[0, pl.ds(0, 2)], 2, 2),
+            (density.at[pl.ds(0, 1)], 4, 1),
+        ]
+        return [pltpu.make_async_copy(source, out.at[pl.ds(n, count)], sems.at[2]) for source, n, count in pairs]
+
     copies = [
-        pltpu.make_async_copy(stress.at[:, :, pl.ds(ny - tile, tile), :], tiles.at[pl.ds(0, 6)], sems.at[0]),
-        pltpu.make_async_copy(stress.at[:, :, pl.ds(0, tile), :], tiles.at[pl.ds(6, 6)], sems.at[0]),
-        pltpu.make_async_copy(density.at[:, pl.ds(0, tile), :], tiles.at[12], sems.at[0]),
-        pltpu.make_async_copy(shear.at[:, pl.ds(0, tile), :], tiles.at[13], sems.at[0]),
+        pltpu.make_async_copy(stress.at[pl.ds(1, 5), :, pl.ds(ny - tile, tile), :], tiles.at[pl.ds(0, 5)], sems.at[0]),
+        pltpu.make_async_copy(stress.at[pl.ds(1, 5), :, pl.ds(0, tile), :], tiles.at[pl.ds(5, 5)], sems.at[0]),
+        pltpu.make_async_copy(density.at[:, pl.ds(0, tile), :], tiles.at[10], sems.at[0]),
+        pltpu.make_async_copy(shear.at[:, pl.ds(0, tile), :], tiles.at[11], sems.at[0]),
+        pltpu.make_async_copy(shear.at[0], ends.at[0], sems.at[0]),
+        pltpu.make_async_copy(shear.at[nx - 1], ends.at[1], sems.at[0]),
     ]
     for copy in copies:
         copy.start()
-
-    def up(out):
-        return [
-            pltpu.make_async_copy(stress.at[f, x], out.at[pl.ds(n * ny, ny), :], sems.at[1])
-            for n, (f, x) in enumerate([(3, nx - 2), (3, nx - 1), (4, nx - 2), (4, nx - 1), (0, nx - 1)])
-        ]
-
-    def down(out):
-        sources = [stress.at[3, 0], stress.at[4, 0], stress.at[0, 0], stress.at[0, 1], density.at[0], shear.at[0]]
-        return [
-            pltpu.make_async_copy(source, out.at[pl.ds(n * ny, ny), :], sems.at[2])
-            for n, source in enumerate(sources)
-        ]
 
     @pl.when(even_x)
     def _():
@@ -222,31 +231,39 @@
     for copy in copies:
         copy.wait()
     Pack(ay, by, even_y).put(
-        put_rows([(tiles, 3, tile - 2, 2), (tiles, 5, tile - 2, 2), (tiles, 1, tile - 1, 1)], nx),
-        put_rows([(tiles, 9, 0, 1), (tiles, 11, 0, 1), (tiles, 7, 0, 2), (tiles, 12, 0, 1), (tiles, 13, 0, 1)], nx),
+        put_rows([(tiles, 2, tile - 2, 2), (tiles, 4, tile - 2, 2), (tiles, 0, tile - 1, 1)], nx),
+        put_rows([(tiles, 7, 0, 1), (tiles, 9, 0, 1), (tiles, 5, 0, 2), (tiles, 10, 0, 1), (tiles, 11, 0, 1)], nx),
     )
     for copy in up(ax) + down(bx):
         copy.wait()
 
 
-def velocity_terms(stress, low_x, high_x, edges):
+def velocity_terms(stress, low_x, high_x, edges, last_xz=None):
     xx = Field(stress, 0, (low_x, 5), (high_x, 2))
     yy = Field(stress, 1, edge=edges.at[2] if edges is not None else None)
     zz = Field(stress, 2)
     xy = Field(stress, 3, (low_x, 2), (high_x, 0), edges.at[0] if edges is not None else None)
-    xz = Field(stress, 4, (low_x, 4), (high_x, 1))
+    xz = Field(stress, 4, (low_x, 4), (high_x, 1), last=last_xz)
     yz = Field(stress, 5, edge=edges.at[1] if edges is not None else None)
     return ((xx, 0), (xy, -1), (xz, -1)), ((xy, -1), (yy, 0), (yz, -1)), ((xz, -1), (yz, -1), (zz, 0))
 
 
 def velocity_inside(step, *refs):
     if step == 0:
-        velocity, stress, density, out, buoy, buoys = refs
+        stress, density, out, buoy, buoys = refs
     else:
-        velocity, stress, buoys, out = refs
+        velocity, stress, buoys, shear, ax, bx, out, factor_low = refs
     nx, ny = stress.shape[1], stress.shape[2]
     lane = lanes()
     terms = velocity_terms(stress, None, None, None)
+    if step == 1:
+        i, j, even_x, _ = position()
+        for t in range(ny // tile):
+            rows, source = pl.ds(tile * t, tile), pl.ds(4 * ny + tile * t, tile)
+            below = 1.0 / jnp.where(i == 0, 1.0, jnp.where(even_x, bx[source, :], ax[source, :]))
+            pair = below + 1.0 / shear[0, rows, :]
+            factor = (-4.0 * time_step * far) / (pair + z_shift(pair, 1, lane))
+            factor_low[rows, :] = jnp.where(i == 0, 0.0, factor)
     if step == 0:
         for x in range(nx):
             buoy[0, x] = 1.0 / density[x]
@@ -264,31 +281,41 @@
                     buoys[1, x, rows, :] = half * (here + buoy_field.y(x, t, 1))
                 buoys[2, x, rows, :] = half * (here + z_shift(here, 1, lane))
             for c, ((fx, sx), (fy, sy), (fz, sz)) in enumerate(terms):
-                total = d.dz(fz, sz)
-                whole_x, whole_y = inner_plane(x, sx, nx), inner_tile(t, ny)
+                late = step == 1 and c == 0 and x == nx - 1
+                total = jnp.zeros((tile, 128), jnp.float32) if late else d.dz(fz, sz)
+                whole_x, whole_y = inner_velocity_plane(step, c, x, sx, nx), inner_tile(t, ny)
                 if whole_x:
                     total += d.dx(fx, sx)
                 if whole_y:
                     total += d.dy(fy, sy)
                 if whole_x and whole_y:
-                    total = velocity[c, x, rows, :] + buoys[c, x, rows, :] * total
+                    total = buoys[c, x, rows, :] * total
+                    if step == 1:
+                        total += velocity[c, x, rows, :]
                 out[c, x, rows, :] = total
 
 
 def velocity_edges(step, *refs):
     if step == 0:
-        (velocity, stress, buoy, buoys, part, ax, bx, by, ay, out, buoys_end, pax, pbx, pby, pay,
+        (velocity, stress, buoy, buoys, ends, part, ax, bx, by, ay, out, buoys_end, pax, pbx, pby, pay,
          low_x, high_x, low_y, high_y, edges, edge_b) = refs
+        last_xz = None
     else:
-        (velocity, stress, buoys, buoys_end, part, ax, bx, by, ay, out, pax, pbx, pby, pay,
-         low_x, high_x, low_y, high_y, edges) = refs
+        (velocity, stress, buoys, buoys_end, shear_end, factor_low, part, ax, bx, by, ay,
+         out, last_xz, pax, pbx, pby, pay, low_x, high_x, low_y, high_y, edges) = refs
     nx, ny = stress.shape[1], stress.shape[2]
     even_x, even_y, last_x, last_y = receive((ax, bx, by, ay), (low_x, high_x, low_y, high_y))
     fill_edges(stress, 3, edges.at[0], low_y, high_y, 0, 2, 0, 1)
     fill_edges(stress, 5, edges.at[1], low_y, high_y, 2, 2, 1, 1)
     fill_edges(stress, 1, edges.at[2], low_y, high_y, 4, 1, 2, 2)
-    terms = velocity_terms(stress, low_x, high_x, edges)
+    terms = velocity_terms(stress, low_x, high_x, edges, last_xz)
     lane = lanes()
+    if step == 1:
+        for t in range(ny // tile):
+            rows, source = pl.ds(tile * t, tile), pl.ds(4 * ny + tile * t, tile)
+            last_xz[rows, :] = stress[4, nx - 1, rows, :] - far * shear_end[1, rows, :] * high_x[source, :]
+            below = pl.ds(3 * ny + tile * t, tile)
+            low_x[below, :] = low_x[below, :] + factor_low[rows, :] * velocity[2, 1, rows, :]
     if step == 0:
         half = 0.5 * time_step
         for t in range(ny // tile):
@@ -306,16 +333,18 @@
         for t in range(ny // tile):
             rows = pl.ds(tile * t, tile)
             d = Differences(x, t, lane)
-            for c, ((fx, sx), (fy, sy), _) in enumerate(terms):
-                whole_x, whole_y = inner_plane(x, sx, nx), inner_tile(t, ny)
+            for c, ((fx, sx), (fy, sy), (fz, sz)) in enumerate(terms):
+                whole_x, whole_y = inner_velocity_plane(step, c, x, sx, nx), inner_tile(t, ny)
                 total = part[c, x, rows, :]
                 if whole_x and whole_y:
-                    out[c, x, rows, :] = total
+                    out[c, x, rows, :] = velocity[c, x, rows, :] + total if step == 0 else total
                     continue
                 if not whole_x:
                     total += d.dx(fx, sx)
                 if not whole_y:
                     total += d.dy(fy, sy)
+                if step == 1 and c == 0 and x == nx - 1:
+                    total += d.dz(fz, sz)
                 if c == 0 and x == nx - 1:
                     factor = buoys_end[rows, :]
                 elif c == 1 and t == ny // tile - 1:
@@ -324,16 +353,21 @@
                     factor = buoys[c, x, rows, :]
                 out[c, x, rows, :] = velocity[c, x, rows, :] + factor * total
 
-    planes_down = put_planes([(out, 0, 0), (out, 1, 0), (out, 1, 1), (out, 2, 0), (out, 2, 1)])
+    planes_up = [(out, 0, nx - 2), (out, 0, nx - 1), (out, 1, nx - 1), (out, 2, nx - 1)]
+    planes_down = [(out, 0, 0), (out, 1, 0), (out, 1, 1), (out, 2, 0)]
+    if step == 0:
+        planes_up.append((ends, None, 1))
+        planes_down.append((ends, None, 0))
+    else:
+        planes_down.append((out, 2, 1))
 
     def down(package):
-        planes_down(package)
+        put_planes(planes_down)(package)
         if step == 0:
             row = high_y[pl.ds(5, 1), :]
             package[pl.ds(5 * ny, 1), :] = jnp.where(last_y, 0.0, 1.0 / jnp.where(last_y, 1.0, row))
 
-    Pack(pax, pbx, even_x).put(
-        put_planes([(out, 0, nx - 2), (out, 0, nx - 1), (out, 1, nx - 1), (out, 2, nx - 1)]), down)
+    Pack(pax, pbx, even_x).put(put_planes(planes_up), down)
     Pack(pay, pby, even_y).put(
         put_rows([(out, 1, ny - 2, 2), (out, 0, ny - 1, 1), (out, 2, ny - 1, 1)], nx),
         put_rows([(out, 1, 0, 1), (out, 0, 0, 2), (out, 2, 0, 2)], nx),
@@ -356,7 +390,7 @@
 
 def stress_inside(step, *refs):
     if step == 0:
-        velocity, stress, lam, shear, ax, bx, by, ay, out, shears, halo_c, comps, edge_c = refs
+        velocity, stress, lam, shear, by, ay, out, shears, comps, edge_c = refs
     else:
         velocity, stress, lam, shear, shears, out, final_velocity, sem = refs
     nx, ny = stress.shape[1], stress.shape[2]
@@ -366,23 +400,16 @@
         copy = pltpu.make_async_copy(velocity, final_velocity, sem)
         copy.start()
     if step == 0:
-        i, j, even_x, even_y = position()
-        _, last_x, _, last_y = sides(i, j)
+        i, j, _, even_y = position()
+        _, _, _, last_y = sides(i, j)
         for x in range(nx):
             comps[x] = 1.0 / shear[x]
             edge_c[x, pl.ds(0, tile), :] = comps[x, pl.ds(ny - tile, tile), :]
             row = pl.ds(ay.shape[0] // nx * x + 5, 1)
             value = jnp.where(last_y, 1.0, jnp.where(even_y, ay[row, :], by[row, :]))
             edge_c[x, pl.ds(tile, 1), :] = jnp.where(last_y, 0.0, 1.0 / value)
-        for t in range(ny // tile):
-            rows = pl.ds(5 * ny + tile * t, tile)
-            value = jnp.where(last_x, 1.0, jnp.where(even_x, ax[rows, :], bx[rows, :]))
-            halo_c[pl.ds(tile * t, tile), :] = jnp.where(last_x, 0.0, 1.0 / value)
-        halo_c[pl.ds(ny, tile), :] = edge_c[nx - 1, pl.ds(1, tile), :]
 
         def comp(x, t, k):
-            if x == nx:
-                return halo_c[pl.ds(tile * t + k, tile), :]
             if k == 1 and t == ny // tile - 1:
                 return edge_c[x, pl.ds(1, tile), :]
             return comps[x, pl.ds(tile * t + k, tile), :]
@@ -392,15 +419,17 @@
             rows = pl.ds(tile * t, tile)
             d = Differences(x, t, lane)
             if step == 0:
-                here = comp(x, t, 0)
-                next_x, next_y = comp(x + 1, t, 0), comp(x, t, 1)
-                pair_x, pair_y = here + next_x, here + next_y
+                here, next_y = comp(x, t, 0), comp(x, t, 1)
+                pair_y = here + next_y
                 four = 4.0 * time_step
-                if x == nx - 1 and t == ny // tile - 1:
-                    shears[0, x, rows, :] = pair_x + next_y
+                if x == nx - 1:
+                    shears[0, x, rows, :] = pair_y
+                    shears[1, x, rows, :] = here + z_shift(here, 1, lane)
                 else:
+                    next_x = comp(x + 1, t, 0)
+                    pair_x = here + next_x
                     shears[0, x, rows, :] = four / (pair_x + (next_y + comp(x + 1, t, 1)))
-                shears[1, x, rows, :] = four / (pair_x + z_shift(pair_x, 1, lane))
+                    shears[1, x, rows, :] = four / (pair_x + z_shift(pair_x, 1, lane))
                 shears[2, x, rows, :] = four / (pair_y + z_shift(pair_y, 1, lane))
             whole_y = inner_tile(t, ny)
             whole_x = inner_plane(x, -1, nx)
@@ -433,23 +462,30 @@
 
 def stress_edges(step, *refs):
     if step == 0:
-        (velocity, stress, lam, shear, halo_c, shears, part, ax, bx, by, ay,
-         out, shear_end, pax, pbx, pby, pay, low_x, high_x, low_y, high_y, edges, corner) = refs
+        (velocity, stress, lam, shear, shears, part, ax, bx, by, ay,
+         out, shear_end, pax, pbx, pby, pay, low_x, high_x, low_y, high_y, edges, above) = refs
     else:
-        (velocity, stress, lam, shear, shears, shear_end, part, ax, bx, by, ay,
+        (velocity, stress, lam, shear, shears, shear_end, last_xz, part, ax, bx, by, ay,
          final_stress, low_x, high_x, low_y, high_y, edges, out, sems) = refs
     nx, ny = stress.shape[1], stress.shape[2]
-    even_x, even_y, _, _ = receive((ax, bx, by, ay), (low_x, high_x, low_y, high_y))
+    even_x, even_y, last_x, _ = receive((ax, bx, by, ay), (low_x, high_x, low_y, high_y))
     fill_edges(velocity, 1, edges.at[0], low_y, high_y, 0, 2, 0, 1)
     fill_edges(velocity, 0, edges.at[1], low_y, high_y, 2, 1, 1, 2)
     fill_edges(velocity, 2, edges.at[2], low_y, high_y, 3, 1, 3, 2)
     vx, vy, vz = stress_fields(velocity, low_x, high_x, edges)
     lane = lanes()
     if step == 0:
-        last = pl.ds(ny - tile, tile)
-        corner[pl.ds(0, tile), :] = halo_c[last, :]
-        corner[pl.ds(tile, 1), :] = high_x[pl.ds(5 * ny, 1), :]
-        shear_end[...] = (4.0 * time_step) / (shears[0, nx - 1, last, :] + corner[pl.ds(1, tile), :])
+        for t in range(ny // tile):
+            value = jnp.where(last_x, 1.0, high_x[pl.ds(4 * ny + tile * t, tile), :])
+            above[pl.ds(tile * t, tile), :] = jnp.where(last_x, 0.0, 1.0 / value)
+        above[pl.ds(ny, 1), :] = high_x[pl.ds(5 * ny, 1), :]
+        for t in range(ny // tile):
+            rows = pl.ds(tile * t, tile)
+            value = above[rows, :]
+            pair = value + above[pl.ds(tile * t + 1, tile), :]
+            shear_end[0, rows, :] = (4.0 * time_step) / (shears[0, nx - 1, rows, :] + pair)
+            pair = value + z_shift(value, 1, lane)
+            shear_end[1, rows, :] = (4.0 * time_step) / (shears[1, nx - 1, rows, :] + pair)
     copies = []
     for x in sorted(range(nx), key=lambda x: not inner_plane(x, 0, nx) or not inner_plane(x, -1, nx)):
         for t in range(ny // tile):
@@ -473,13 +509,23 @@
                     total += d.dy(vx, 0)
                 if not whole_x:
                     total += d.dx(vy, 0)
-                at_end = x == nx - 1 and t == ny // tile - 1
-                factor = shear_end[...] if at_end else shears[0, x, rows, :]
+                factor = shear_end[0, rows, :] if x == nx - 1 else shears[0, x, rows, :]
                 total = stress[3, x, rows, :] + factor * total
             out[3, x, rows, :] = total
             total = part[4, x, rows, :]
             if not whole_x:
-                total = stress[4, x, rows, :] + shears[1, x, rows, :] * (total + d.dx(vz, 0))
+                before = stress[4, x, rows, :]
+                factor = shears[1, x, rows, :]
+                change = None
+                if x == nx - 1:
+                    factor = shear_end[1, rows, :]
+                    if step == 0:
+                        change = near * (vz.at(x + 1, t) - vz.at(x, t)) + far * vz.at(x - 1, t)
+                    else:
+                        before = last_xz[rows, :]
+                if change is None:
+                    change = d.dx(vz, 0)
+                total = before + factor * (total + change)
             out[4, x, rows, :] = total
             total = part[5, x, rows, :]
             if not whole_y:
@@ -494,7 +540,7 @@
     if step == 0:
         Pack(pax, pbx, even_x).put(
             put_planes([(out, 3, nx - 2), (out, 3, nx - 1), (out, 4, nx - 2), (out, 4, nx - 1), (out, 0, nx - 1)]),
-            put_planes([(out, 3, 0), (out, 4, 0), (out, 0, 0), (out, 0, 1)]),
+            put_planes([(out, 3, 0), (out, 4, 0), (out, 0, 0), (out, 0, 1), (velocity, 2, 1)]),
         )
         Pack(pay, pby, even_y).put(
             put_rows([(out, 3, ny - 2, 2), (out, 5, ny - 2, 2), (out, 1, ny - 1, 1)], nx),
@@ -538,38 +584,41 @@
     def kernel(function, step):
         return lambda *refs: function(step, *refs)
 
-    first, second, later = (6 * ny, 6), 5 * ny + tile, 5 * ny
-    packed = call(
-        first_pack, packages(*first), [(14, nx, tile, nz), dma((4,))],
+    first, second, later = (5 * ny, 6), (5 * ny + tile, 5), (5 * ny, 5)
+    *packed, ends = call(
+        first_pack, [(5, ny, nz)] * 2 + packages(*first)[2:] + [(2, ny, nz)], [(12, nx, tile, nz), dma((3,))],
         (stress, density, lame_mu), cells, hbm_in=(0, 1, 2))
+    packed, velocity, stress, density, lame_lambda, lame_mu = lax.optimization_barrier(
+        ([package.reshape(-1, nz) for package in packed], velocity, stress, density, lame_lambda, lame_mu))
     got = exchange(packed)
     part, buoy, buoys = call(
-        kernel(velocity_inside, 0), [three, one, three], [], (velocity, stress, density), 60 * cells)
+        kernel(velocity_inside, 0), [three, one, three], [], (stress, density), 60 * cells)
     new_velocity, buoys_end, *packed = call(
-        kernel(velocity_edges, 0), [three, (ny + nx * tile, nz)] + packages(second), halos(*first) + [(2 * tile, nz)],
-        (velocity, stress, buoy, buoys, part, *got), 20 * cells)
-    materials = got
+        kernel(velocity_edges, 0), [three, (ny + nx * tile, nz)] + packages(*second), halos(*first) + [(2 * tile, nz)],
+        (velocity, stress, buoy, buoys, ends, part, *got), 20 * cells)
+    rows_y = got[2:]
     got = exchange(packed)
-    part, shears, halo_c = call(
-        kernel(stress_inside, 0), [stress.shape, three, (ny + tile, nz)], [(nx, ny, nz), (nx, 2 * tile, nz)],
-        (new_velocity, stress, lame_lambda, lame_mu, *materials), 80 * cells)
+    part, shears = call(
+        kernel(stress_inside, 0), [stress.shape, three], [(nx, ny, nz), (nx, 2 * tile, nz)],
+        (new_velocity, stress, lame_lambda, lame_mu, *rows_y), 80 * cells)
     new_stress, shear_end, *packed = call(
-        kernel(stress_edges, 0), [stress.shape, (tile, nz)] + packages(later), halos(second) + [(2 * tile, nz)],
-        (new_velocity, stress, lame_lambda, lame_mu, halo_c, shears, part, *got), 20 * cells)
+        kernel(stress_edges, 0), [stress.shape, (2, ny, nz)] + packages(*later), halos(*second) + [(ny + tile, nz)],
+        (new_velocity, stress, lame_lambda, lame_mu, shears, part, *got), 20 * cells)
     velocity, stress = new_velocity, new_stress
+    planes_x = got[:2]
     got = exchange(packed)
-    (part,) = call(
-        kernel(velocity_inside, 1), [three], [], (velocity, stress, buoys), 60 * cells)
-    velocity, *packed = call(
-        kernel(velocity_edges, 1), [three] + packages(later), halos(later),
-        (velocity, stress, buoys, buoys_end, part, *got), 20 * cells)
+    part, factor_low = call(
+        kernel(velocity_inside, 1), [three, (ny, nz)], [], (velocity, stress, buoys, lame_mu, *planes_x), 60 * cells)
+    velocity, last_xz, *packed = call(
+        kernel(velocity_edges, 1), [three, (ny, nz)] + packages(*later), halos(*later),
+        (velocity, stress, buoys, buoys_end, shear_end, factor_low, part, *got), 20 * cells)
     got = exchange(packed)
     part, final_velocity = call(
         kernel(stress_inside, 1), [stress.shape, three], [dma],
         (velocity, stress, lame_lambda, lame_mu, shears), 80 * cells, hbm_out=(1,))
     (final_stress,) = call(
-        kernel(stress_edges, 1), [stress.shape], halos(later) + [stress.shape, dma((nx,))],
-        (velocity, stress, lame_lambda, lame_mu, shears, shear_end, part, *got), 20 * cells, hbm_out=(0,))
+        kernel(stress_edges, 1), [stress.shape], halos(*later) + [stress.shape, dma((nx,))],
+        (velocity, stress, lame_lambda, lame_mu, shears, shear_end, last_xz, part, *got), 20 * cells, hbm_out=(0,))
     return (final_velocity, final_stress)
 
 

time: 30.1 us -> 29.5 us (0.980)
  waiting for transfers between devices: 5.28 us -> 6.46 us
  local copies, waits for them, and re-layouts: 1.02 us -> 0.03 us
  starting transfers between devices: 17.6 us -> 16.8 us
    ppermute x16, waiting for transfers between devices: 5.28 us -> 6.46 us  [exchange(): lax.ppermute(array, AXES, route)]
    unnamed x10, local copies, waits for them, and re-layouts: 1.02 us -> 0.03 us
    ppermute x16, starting transfers between devices: 17.6 us -> 16.8 us  [exchange(): lax.ppermute(array, AXES, route)]
where the time goes in v6:
time: 29.5 us; the launch traced here: 29.3 us
  starting transfers between devices  16.8 us (57%)
  waiting for transfers between devices  6.46 us (22%)
  Pallas kernels  5.31 us (18%)
  between operations  0.77 us (3%)
    ppermute x16, starting transfers between devices, exchange(): lax.ppermute(array, AXES, route)  16.8 us
    ppermute x16, waiting for transfers between devices, exchange(): lax.ppermute(array, AXES, route)  6.46 us
    pallas_call x9, Pallas kernels, call(): pl.pallas_call(kernel, out_shape=[(pltpu.HBM if n in hbm_out else pltpu.V...  5.31 us
  transfers between devices with their start and end apart: 16, of which 4 were waited for; matrix products, arithmetic and copies ran while one was open for 0% of the time, Pallas kernels for 8%

profile of v6, /device:TPU:0, one launch (start us, length us, event | category | flops | bytes accessed | tf_op | source)
XLA Modules:
  0.0 29.3 jit_solution(12999425041465196343)
XLA Ops:
  0.6 0.0 copy-start
  0.6 0.0 copy-start.3
  0.6 1.1 %shard_map.68 = (f32[5,32,128]{2,1,0:T(8,128)S(1)}, f32[5,32,128]{2,1,0:T(8,128)S(1)}, f32[48,128]{1,0:T(8,128)S(1)}, f32[48,128]{1,0:T(8,128)S(1)}, f32[2,32,128]{2,1,0:T(8,128)S(1)}) custom-call(f32[6,8,32,128]{3,2,1,0:T(8,128)} %refs_1_.3, f32[8,32,128]{2,1,0:T(8,128)} %refs_1_, f32[8,32,128]{2,1,0:T(8,128)} %refs_3_.4), custom_call_target="tpu_custom_call" | custom-call | flops 32768 | bytes 2097152 | tf_op jit(solution)/shard_map/pallas_call | solution.py:557
  1.8 0.0 copy-start.4
  1.8 3.0 %collective-permute-start = (f32[160,128]{1,0:T(8,128)S(1)}, f32[160,128]{1,0:T(8,128)S(1)}, u32[]{:S(2)}, u32[]{:S(2)}) collective-permute-start(f32[160,128]{1,0:T(8,128)S(1)} %bitcast.3), channel_id=1, source_target_pairs={{0,8},{1,9},{2,10},{3,11},{4,12},{5,13},{6,14},{7,15},{8,0},{9,1},... | collective-permute-start | bytes 245768 | tf_op jit(solution)/shard_map/ppermute | solution.py:579
  4.8 0.0 collective-permute-start.1
  4.8 1.5 %collective-permute-start.2 = (f32[48,128]{1,0:T(8,128)S(1)}, f32[48,128]{1,0:T(8,128)S(1)}, u32[]{:S(2)}, u32[]{:S(2)}) collective-permute-start(f32[48,128]{1,0:T(8,128)S(1)} %get-tuple-element.56), channel_id=1, source_target_pairs={{0,16},{1,2},{2,1},{3,4},{4,3},{5,6},{6,5},{7,23},{8,24},{9,10},{1... | collective-permute-start | bytes 73736 | tf_op jit(solution)/shard_map/ppermute | solution.py:579
  6.4 0.2 collective-permute-start.3
  6.5 0.0 copy-done
  6.5 0.4 %shard_map.69 = (f32[3,8,32,128]{3,2,1,0:T(8,128)S(1)}, f32[1,8,32,128]{3,2,1,0:T(8,128)S(1)}, f32[3,8,32,128]{3,2,1,0:T(8,128)S(1)}) custom-call(f32[6,8,32,128]{3,2,1,0:T(8,128)S(1)} %copy-done, f32[8,32,128]{2,1,0:T(8,128)S(1)} %copy-done.3), custom_call_target="tpu_custom_call" | custom-call | flops 1966080 | bytes 2097152 | tf_op jit(solution)/shard_map/pallas_call | solution.py:557
  6.9 1.7 %collective-permute-done.2.refs_8_.refs_4_ = f32[48,128]{1,0:T(8,128)S(1)} collective-permute-done((f32[48,128]{1,0:T(8,128)S(1)}, f32[48,128]{1,0:T(8,128)S(1)}, u32[]{:S(2)}, u32[]{:S(2)}) %collective-permute-start.2) | collective-permute-done | bytes 24608 | tf_op jit(solution)/shard_map/ppermute | solution.py:579
  8.6 0.0 collective-permute-done.3.refs_9_.refs_5_
  8.6 0.0 collective-permute-done.refs_6_
  8.7 0.0 collective-permute-done.1.refs_7_
  8.7 0.0 copy-start.1
  8.7 0.0 copy-start.2
  8.7 0.3 shard_map.70
  9.0 3.4 %collective-permute-start.4 = (f32[168,128]{1,0:T(8,128)S(1)}, f32[168,128]{1,0:T(8,128)S(1)}, u32[]{:S(2)}, u32[]{:S(2)}) collective-permute-start(f32[168,128]{1,0:T(8,128)S(1)} %get-tuple-element.63), channel_id=1, source_target_pairs={{0,8},{1,9},{2,10},{3,11},{4,12},{5,13},{6,14},{7,15},{8,0},{9,1},... | collective-permute-start | bytes 258056 | tf_op jit(solution)/shard_map/ppermute | solution.py:579
  12.4 0.0 collective-permute-start.5
  12.4 1.5 %collective-permute-start.6 = (f32[40,128]{1,0:T(8,128)S(1)}, f32[40,128]{1,0:T(8,128)S(1)}, u32[]{:S(2)}, u32[]{:S(2)}) collective-permute-start(f32[40,128]{1,0:T(8,128)S(1)} %get-tuple-element.65), channel_id=1, source_target_pairs={{0,16},{1,2},{2,1},{3,4},{4,3},{5,6},{6,5},{7,23},{8,24},{9,10},{1... | collective-permute-start | bytes 61448 | tf_op jit(solution)/shard_map/ppermute | solution.py:579
  13.9 0.0 collective-permute-start.7
  13.9 0.0 copy-done.2
  13.9 0.5 %shard_map.71 = (f32[6,8,32,128]{3,2,1,0:T(8,128)S(1)}, f32[3,8,32,128]{3,2,1,0:T(8,128)S(1)}) custom-call(f32[3,8,32,128]{3,2,1,0:T(8,128)S(1)} %get-tuple-element.58.refs_0_, f32[6,8,32,128]{3,2,1,0:T(8,128)S(1)} %copy-done, f32[8,32,128]{2,1,0:T(8,128)S(1)} %copy-done.2, f32[8,32,128]{2,1,0:T(8,128)S(1)} %copy-done.1, ...), custom_call_target="tpu_custom_call" | custom-call | flops 2621440 | bytes 2097152 | tf_op jit(solution)/shard_map/pallas_call | solution.py:557
  14.4 1.8 %collective-permute-done.6.refs_8_ = f32[40,128]{1,0:T(8,128)S(1)} collective-permute-done((f32[40,128]{1,0:T(8,128)S(1)}, f32[40,128]{1,0:T(8,128)S(1)}, u32[]{:S(2)}, u32[]{:S(2)}) %collective-permute-start.6) | collective-permute-done | bytes 20512 | tf_op jit(solution)/shard_map/ppermute | solution.py:579
  16.2 0.0 collective-permute-done.7.refs_9_
  16.2 0.0 collective-permute-done.4.refs_6_.refs_4_
  16.2 0.0 collective-permute-done.5.refs_7_.refs_5_
  16.2 0.3 %shard_map.72 = (f32[6,8,32,128]{3,2,1,0:T(8,128)S(1)}, f32[2,32,128]{2,1,0:T(8,128)S(1)}, f32[160,128]{1,0:T(8,128)S(1)}, f32[160,128]{1,0:T(8,128)S(1)}, f32[40,128]{1,0:T(8,128)S(1)}, /*index=5*/f32[40,128]{1,0:T(8,128)S(1)}) custom-call(f32[3,8,32,128]{3,2,1,0:T(8,128)S(1)} %get-tuple-element.58.refs_0_, f32[6,8,32,128]{3,2,1,0:T(8,128)S(1)} %copy-done, ...), custom_call_target="tpu_custom_call" | custom-call | flops 655360 | bytes 2097152 | tf_op jit(solution)/shard_map/pallas_call | solution.py:557
  16.5 2.0 %collective-permute-start.8 = (f32[160,128]{1,0:T(8,128)S(1)}, f32[160,128]{1,0:T(8,128)S(1)}, u32[]{:S(2)}, u32[]{:S(2)}) collective-permute-start(f32[160,128]{1,0:T(8,128)S(1)} %get-tuple-element.72), channel_id=1, source_target_pairs={{0,8},{1,9},{2,10},{3,11},{4,12},{5,13},{6,14},{7,15},{8,0},{9,1},... | collective-permute-start | bytes 245768 | tf_op jit(solution)/shard_map/ppermute | solution.py:579
  18.4 0.0 collective-permute-start.9
  18.4 1.6 %collective-permute-start.10 = (f32[40,128]{1,0:T(8,128)S(1)}, f32[40,128]{1,0:T(8,128)S(1)}, u32[]{:S(2)}, u32[]{:S(2)}) collective-permute-start(f32[40,128]{1,0:T(8,128)S(1)} %get-tuple-element.74), channel_id=1, source_target_pairs={{0,16},{1,2},{2,1},{3,4},{4,3},{5,6},{6,5},{7,23},{8,24},{9,10},{1... | collective-permute-start | bytes 61448 | tf_op jit(solution)/shard_map/ppermute | solution.py:579
  20.0 0.0 collective-permute-start.11
  20.0 0.4 %shard_map.73 = (f32[3,8,32,128]{3,2,1,0:T(8,128)S(1)}, f32[32,128]{1,0:T(8,128)S(1)}) custom-call(f32[3,8,32,128]{3,2,1,0:T(8,128)S(1)} %get-tuple-element.58.refs_0_, f32[6,8,32,128]{3,2,1,0:T(8,128)S(1)} %get-tuple-element.67.refs_1_, f32[3,8,32,128]{3,2,1,0:T(8,128)S(1)} %get-tuple-element.51.refs_3_.refs_2_, f32[8,32,128]{2,1,0:T(8,128)S(1)} %copy-done.1, ...), custom_call_target="tpu_custom_call" | custom-call | flops 1966080 | bytes 2097152 | tf_op jit(solution)/shard_map/pallas_call | solution.py:557
  20.4 1.8 %collective-permute-done.10.refs_9_ = f32[40,128]{1,0:T(8,128)S(1)} collective-permute-done((f32[40,128]{1,0:T(8,128)S(1)}, f32[40,128]{1,0:T(8,128)S(1)}, u32[]{:S(2)}, u32[]{:S(2)}) %collective-permute-start.10) | collective-permute-done | bytes 20512 | tf_op jit(solution)/shard_map/ppermute | solution.py:579
  22.2 0.0 collective-permute-done.11.refs_10_
  22.2 0.0 collective-permute-done.8.refs_7_
  22.2 0.0 collective-permute-done.9.refs_8_
  22.2 0.3 shard_map.74
  22.5 2.0 %collective-permute-start.12 = (f32[160,128]{1,0:T(8,128)S(1)}, f32[160,128]{1,0:T(8,128)S(1)}, u32[]{:S(2)}, u32[]{:S(2)}) collective-permute-start(f32[160,128]{1,0:T(8,128)S(1)} %get-tuple-element.80), channel_id=1, source_target_pairs={{0,8},{1,9},{2,10},{3,11},{4,12},{5,13},{6,14},{7,15},{8,0},{9,1},... | collective-permute-start | bytes 245768 | tf_op jit(solution)/shard_map/ppermute | solution.py:579
  24.5 0.0 collective-permute-start.13
  24.5 1.6 %collective-permute-start.14 = (f32[40,128]{1,0:T(8,128)S(1)}, f32[40,128]{1,0:T(8,128)S(1)}, u32[]{:S(2)}, u32[]{:S(2)}) collective-permute-start(f32[40,128]{1,0:T(8,128)S(1)} %get-tuple-element.82), channel_id=1, source_target_pairs={{0,16},{1,2},{2,1},{3,4},{4,3},{5,6},{6,5},{7,23},{8,24},{9,10},{1... | collective-permute-start | bytes 61448 | tf_op jit(solution)/shard_map/ppermute | solution.py:579
  26.1 0.0 collective-permute-start.15
  26.1 1.1 %shard_map.75 = (f32[6,8,32,128]{3,2,1,0:T(8,128)S(1)}, f32[3,8,32,128]{3,2,1,0:T(8,128)}) custom-call(f32[3,8,32,128]{3,2,1,0:T(8,128)S(1)} %get-tuple-element.76.refs_0_, f32[6,8,32,128]{3,2,1,0:T(8,128)S(1)} %get-tuple-element.67.refs_1_, f32[8,32,128]{2,1,0:T(8,128)S(1)} %copy-done.2, f32[8,32,128]{2,1,0:T(8,128)S(1)} %copy-done.1, ...), custom_call_target="tpu_custom_call" | custom-call | flops 2621440 | bytes 2097152 | tf_op jit(solution)/shard_map/pallas_call | solution.py:557
  27.1 1.2 %collective-permute-done.14.refs_10_ = f32[40,128]{1,0:T(8,128)S(1)} collective-permute-done((f32[40,128]{1,0:T(8,128)S(1)}, f32[40,128]{1,0:T(8,128)S(1)}, u32[]{:S(2)}, u32[]{:S(2)}) %collective-permute-start.14) | collective-permute-done | bytes 20512 | tf_op jit(solution)/shard_map/ppermute | solution.py:579
  28.3 0.0 collective-permute-done.15.refs_11_
  28.3 0.0 collective-permute-done.12.refs_8_
  28.3 0.0 collective-permute-done.13.refs_9_
  28.3 1.0 %shard_map.76 = f32[6,8,32,128]{3,2,1,0:T(8,128)} custom-call(f32[3,8,32,128]{3,2,1,0:T(8,128)S(1)} %get-tuple-element.76.refs_0_, f32[6,8,32,128]{3,2,1,0:T(8,128)S(1)} %get-tuple-element.67.refs_1_, f32[8,32,128]{2,1,0:T(8,128)S(1)} %copy-done.2, f32[8,32,128]{2,1,0:T(8,128)S(1)} %copy-done.1, f32[3,8,32,128]{3,2,1,0:T(8,128)S(1)} %get-tuple-element.61.refs_4_, ...), custom_call_target="tpu_custom_call" | custom-call | flops 655360 | bytes 2097152 | tf_op jit(solution)/shard_map/pallas_call | solution.py:557
  (3 shorter events, 0.0 us)
Async XLA Ops:
  0.6 5.9 %copy-start = (f32[6,8,32,128]{3,2,1,0:T(8,128)S(1)}, f32[6,8,32,128]{3,2,1,0:T(8,128)}, u32[]{:S(2)}) copy-start(f32[6,8,32,128]{3,2,1,0:T(8,128)} %refs_1_.3) | copy-start | bytes 2359300
  0.6 5.9 %copy-start.3 = (f32[8,32,128]{2,1,0:T(8,128)S(1)}, f32[8,32,128]{2,1,0:T(8,128)}, u32[]{:S(2)}) copy-start(f32[8,32,128]{2,1,0:T(8,128)} %refs_1_) | copy-start | bytes 393220
  1.8 6.9 %copy-start.4 = (f32[3,8,32,128]{3,2,1,0:T(8,128)S(1)}, f32[3,8,32,128]{3,2,1,0:T(8,128)}, u32[]{:S(2)}) copy-start(f32[3,8,32,128]{3,2,1,0:T(8,128)} %refs_0_.1) | copy-start | bytes 1179652
  1.8 6.8 %collective-permute-start = (f32[160,128]{1,0:T(8,128)S(1)}, f32[160,128]{1,0:T(8,128)S(1)}, u32[]{:S(2)}, u32[]{:S(2)}) collective-permute-start(f32[160,128]{1,0:T(8,128)S(1)} %bitcast.3), channel_id=1, source_target_pairs={{0,8},{1,9},{2,10},{3,11},{4,12},{5,13},{6,14},{7,15},{8,0},{9,1},... | collective-permute-start | bytes 245768 | tf_op jit(solution)/shard_map/ppermute | solution.py:579
  4.8 3.8 %collective-permute-start.1 = (f32[160,128]{1,0:T(8,128)S(1)}, f32[160,128]{1,0:T(8,128)S(1)}, u32[]{:S(2)}, u32[]{:S(2)}) collective-permute-start(f32[160,128]{1,0:T(8,128)S(1)} %bitcast.2), channel_id=1, source_target_pairs={{0,1},{1,0},{2,3},{3,2},{4,5},{5,4},{6,7},{7,6},{8,16},{9,17},{10,... | collective-permute-start | bytes 245768 | tf_op jit(solution)/shard_map/ppermute | solution.py:579
  4.8 3.8 %collective-permute-start.2 = (f32[48,128]{1,0:T(8,128)S(1)}, f32[48,128]{1,0:T(8,128)S(1)}, u32[]{:S(2)}, u32[]{:S(2)}) collective-permute-start(f32[48,128]{1,0:T(8,128)S(1)} %get-tuple-element.56), channel_id=1, source_target_pairs={{0,16},{1,2},{2,1},{3,4},{4,3},{5,6},{6,5},{7,23},{8,24},{9,10},{1... | collective-permute-start | bytes 73736 | tf_op jit(solution)/shard_map/ppermute | solution.py:579
  6.4 2.3 %collective-permute-start.3 = (f32[48,128]{1,0:T(8,128)S(1)}, f32[48,128]{1,0:T(8,128)S(1)}, u32[]{:S(2)}, u32[]{:S(2)}) collective-permute-start(f32[48,128]{1,0:T(8,128)S(1)} %get-tuple-element.57), channel_id=1, source_target_pairs={{0,1},{1,0},{2,3},{3,2},{4,5},{5,4},{6,7},{7,6},{8,9},{9,8},{10,11... | collective-permute-start | bytes 73736 | tf_op jit(solution)/shard_map/ppermute | solution.py:579
  8.7 5.3 %copy-start.1 = (f32[8,32,128]{2,1,0:T(8,128)S(1)}, f32[8,32,128]{2,1,0:T(8,128)}, u32[]{:S(2)}) copy-start(f32[8,32,128]{2,1,0:T(8,128)} %refs_3_.4) | copy-start | bytes 393220
  8.7 5.2 %copy-start.2 = (f32[8,32,128]{2,1,0:T(8,128)S(1)}, f32[8,32,128]{2,1,0:T(8,128)}, u32[]{:S(2)}) copy-start(f32[8,32,128]{2,1,0:T(8,128)} %refs_2_.3) | copy-start | bytes 393220
  9.0 7.2 %collective-permute-start.4 = (f32[168,128]{1,0:T(8,128)S(1)}, f32[168,128]{1,0:T(8,128)S(1)}, u32[]{:S(2)}, u32[]{:S(2)}) collective-permute-start(f32[168,128]{1,0:T(8,128)S(1)} %get-tuple-element.63), channel_id=1, source_target_pairs={{0,8},{1,9},{2,10},{3,11},{4,12},{5,13},{6,14},{7,15},{8,0},{9,1},... | collective-permute-start | bytes 258056 | tf_op jit(solution)/shard_map/ppermute | solution.py:579
  12.4 3.8 %collective-permute-start.5 = (f32[168,128]{1,0:T(8,128)S(1)}, f32[168,128]{1,0:T(8,128)S(1)}, u32[]{:S(2)}, u32[]{:S(2)}) collective-permute-start(f32[168,128]{1,0:T(8,128)S(1)} %get-tuple-element.64), channel_id=1, source_target_pairs={{0,1},{1,0},{2,3},{3,2},{4,5},{5,4},{6,7},{7,6},{8,16},{9,17},{10,... | collective-permute-start | bytes 258056 | tf_op jit(solution)/shard_map/ppermute | solution.py:579
  12.4 3.8 %collective-permute-start.6 = (f32[40,128]{1,0:T(8,128)S(1)}, f32[40,128]{1,0:T(8,128)S(1)}, u32[]{:S(2)}, u32[]{:S(2)}) collective-permute-start(f32[40,128]{1,0:T(8,128)S(1)} %get-tuple-element.65), channel_id=1, source_target_pairs={{0,16},{1,2},{2,1},{3,4},{4,3},{5,6},{6,5},{7,23},{8,24},{9,10},{1... | collective-permute-start | bytes 61448 | tf_op jit(solution)/shard_map/ppermute | solution.py:579
  13.9 2.2 %collective-permute-start.7 = (f32[40,128]{1,0:T(8,128)S(1)}, f32[40,128]{1,0:T(8,128)S(1)}, u32[]{:S(2)}, u32[]{:S(2)}) collective-permute-start(f32[40,128]{1,0:T(8,128)S(1)} %get-tuple-element.66), channel_id=1, source_target_pairs={{0,1},{1,0},{2,3},{3,2},{4,5},{5,4},{6,7},{7,6},{8,9},{9,8},{10,11... | collective-permute-start | bytes 61448 | tf_op jit(solution)/shard_map/ppermute | solution.py:579
  16.5 5.8 %collective-permute-start.8 = (f32[160,128]{1,0:T(8,128)S(1)}, f32[160,128]{1,0:T(8,128)S(1)}, u32[]{:S(2)}, u32[]{:S(2)}) collective-permute-start(f32[160,128]{1,0:T(8,128)S(1)} %get-tuple-element.72), channel_id=1, source_target_pairs={{0,8},{1,9},{2,10},{3,11},{4,12},{5,13},{6,14},{7,15},{8,0},{9,1},... | collective-permute-start | bytes 245768 | tf_op jit(solution)/shard_map/ppermute | solution.py:579
  18.4 3.8 %collective-permute-start.9 = (f32[160,128]{1,0:T(8,128)S(1)}, f32[160,128]{1,0:T(8,128)S(1)}, u32[]{:S(2)}, u32[]{:S(2)}) collective-permute-start(f32[160,128]{1,0:T(8,128)S(1)} %get-tuple-element.73), channel_id=1, source_target_pairs={{0,1},{1,0},{2,3},{3,2},{4,5},{5,4},{6,7},{7,6},{8,16},{9,17},{10,... | collective-permute-start | bytes 245768 | tf_op jit(solution)/shard_map/ppermute | solution.py:579
  18.4 3.8 %collective-permute-start.10 = (f32[40,128]{1,0:T(8,128)S(1)}, f32[40,128]{1,0:T(8,128)S(1)}, u32[]{:S(2)}, u32[]{:S(2)}) collective-permute-start(f32[40,128]{1,0:T(8,128)S(1)} %get-tuple-element.74), channel_id=1, source_target_pairs={{0,16},{1,2},{2,1},{3,4},{4,3},{5,6},{6,5},{7,23},{8,24},{9,10},{1... | collective-permute-start | bytes 61448 | tf_op jit(solution)/shard_map/ppermute | solution.py:579
  20.0 2.2 %collective-permute-start.11 = (f32[40,128]{1,0:T(8,128)S(1)}, f32[40,128]{1,0:T(8,128)S(1)}, u32[]{:S(2)}, u32[]{:S(2)}) collective-permute-start(f32[40,128]{1,0:T(8,128)S(1)} %get-tuple-element.75), channel_id=1, source_target_pairs={{0,1},{1,0},{2,3},{3,2},{4,5},{5,4},{6,7},{7,6},{8,9},{9,8},{10,11... | collective-permute-start | bytes 61448 | tf_op jit(solution)/shard_map/ppermute | solution.py:579
  22.5 5.8 %collective-permute-start.12 = (f32[160,128]{1,0:T(8,128)S(1)}, f32[160,128]{1,0:T(8,128)S(1)}, u32[]{:S(2)}, u32[]{:S(2)}) collective-permute-start(f32[160,128]{1,0:T(8,128)S(1)} %get-tuple-element.80), channel_id=1, source_target_pairs={{0,8},{1,9},{2,10},{3,11},{4,12},{5,13},{6,14},{7,15},{8,0},{9,1},... | collective-permute-start | bytes 245768 | tf_op jit(solution)/shard_map/ppermute | solution.py:579
  24.5 3.8 %collective-permute-start.13 = (f32[160,128]{1,0:T(8,128)S(1)}, f32[160,128]{1,0:T(8,128)S(1)}, u32[]{:S(2)}, u32[]{:S(2)}) collective-permute-start(f32[160,128]{1,0:T(8,128)S(1)} %get-tuple-element.81), channel_id=1, source_target_pairs={{0,1},{1,0},{2,3},{3,2},{4,5},{5,4},{6,7},{7,6},{8,16},{9,17},{10,... | collective-permute-start | bytes 245768 | tf_op jit(solution)/shard_map/ppermute | solution.py:579
  24.5 3.8 %collective-permute-start.14 = (f32[40,128]{1,0:T(8,128)S(1)}, f32[40,128]{1,0:T(8,128)S(1)}, u32[]{:S(2)}, u32[]{:S(2)}) collective-permute-start(f32[40,128]{1,0:T(8,128)S(1)} %get-tuple-element.82), channel_id=1, source_target_pairs={{0,16},{1,2},{2,1},{3,4},{4,3},{5,6},{6,5},{7,23},{8,24},{9,10},{1... | collective-permute-start | bytes 61448 | tf_op jit(solution)/shard_map/ppermute | solution.py:579
  26.1 2.2 %collective-permute-start.15 = (f32[40,128]{1,0:T(8,128)S(1)}, f32[40,128]{1,0:T(8,128)S(1)}, u32[]{:S(2)}, u32[]{:S(2)}) collective-permute-start(f32[40,128]{1,0:T(8,128)S(1)} %get-tuple-element.83), channel_id=1, source_target_pairs={{0,1},{1,0},{2,3},{3,2},{4,5},{5,4},{6,7},{7,6},{8,9},{9,8},{10,11... | collective-permute-start | bytes 61448 | tf_op jit(solution)/shard_map/ppermute | solution.py:579

commit v7 on v6

--- a/solution.py
+++ b/solution.py
@@ -46,12 +46,15 @@
     return i, j, lax.rem(i, 2) == 0, lax.rem(j, 2) == 0
 
 
-def unpack(inner, outer, low, high, even, first, last):
-    for start in range(0, inner.shape[0], tile):
-        rows = pl.ds(start, tile)
-        a, b = inner[rows, :], outer[rows, :]
-        low[rows, :] = jnp.where(first, 0.0, jnp.where(even, b, a))
-        high[rows, :] = jnp.where(last, 0.0, jnp.where(even, a, b))
+class Halo:
+    def __init__(self, inner, outer, by_inner, outside):
+        self.inner, self.outer, self.by_inner, self.outside = inner, outer, by_inner, outside
+        self.rows = inner.shape[0]
+
+    def load(self, start, count):
+        rows = pl.ds(start, count)
+        value = jnp.where(self.by_inner, self.inner[rows, :], self.outer[rows, :])
+        return jnp.where(self.outside, 0.0, value)
 
 
 class Pack:
@@ -115,30 +118,36 @@
 
 
 class Field:
-    def __init__(self, ref, f, low_x=None, high_x=None, edge=None, last=None):
+    def __init__(self, ref, f, low_x=None, high_x=None, low_y=None, high_y=None, last=None, below=None):
         self.ref, self.f = ref, f
-        self.low_x, self.high_x, self.edge, self.last = low_x, high_x, edge, last
+        self.low_x, self.high_x, self.low_y, self.high_y = low_x, high_x, low_y, high_y
+        self.last, self.below = last, below
 
     def at(self, x, t):
         nx, ny = self.ref.shape[-3], self.ref.shape[-2]
         if x < 0:
-            ref, index = self.low_x
-            return ref[pl.ds(ny * (index + x) + tile * t, tile), :]
+            halo, index = self.low_x
+            value = halo.load(ny * (index + x) + tile * t, tile)
+            return value + self.below(t) if self.below is not None and x == -1 else value
         if x >= nx:
-            ref, index = self.high_x
-            return ref[pl.ds(ny * (index + x - nx) + tile * t, tile), :]
+            halo, index = self.high_x
+            return halo.load(ny * (index + x - nx) + tile * t, tile)
         if self.last is not None and x == nx - 1:
             return self.last[pl.ds(tile * t, tile), :]
         return self.ref[self.f, x, pl.ds(tile * t, tile), :]
 
     def y(self, x, t, k):
-        ny = self.ref.shape[-2]
+        nx, ny = self.ref.shape[-3], self.ref.shape[-2]
         start = tile * t + k
-        if start < 0:
-            return self.edge[0, x, pl.ds(tile + k, tile), :]
-        if start + tile > ny:
-            return self.edge[1, x, pl.ds(k, tile), :]
-        return self.ref[self.f, x, pl.ds(start, tile), :]
+        if 0 <= start <= ny - tile:
+            return self.ref[self.f, x, pl.ds(start, tile), :]
+        halo, first = self.low_y if k < 0 else self.high_y
+        moved = pltpu.roll(self.ref[self.f, x, pl.ds(tile * t, tile), :], (-k) % tile, 0)
+        place = lax.broadcasted_iota(jnp.int32, moved.shape, 0)
+        for n in range(abs(k)):
+            row = halo.load(halo.rows // nx * x + first + (n + k + 1 if k < 0 else n), 1)
+            moved = jnp.where(place == (n if k < 0 else tile - k + n), row, moved)
+        return moved
 
 
 class Differences:
@@ -168,26 +177,17 @@
     return 0 < t < ny // tile - 1
 
 
-def fill_edges(ref, f, edge, lows, highs, low_row, low_count, high_row, high_count):
-    nx, ny = ref.shape[-3], ref.shape[-2]
-    each = lows.shape[0] // nx
-    for x in range(nx):
-        if low_count:
-            edge[0, x, pl.ds(tile - low_count, low_count), :] = lows[pl.ds(each * x + low_row, low_count), :]
-            edge[0, x, pl.ds(tile, tile), :] = ref[f, x, pl.ds(0, tile), :]
-        if high_count:
-            edge[1, x, pl.ds(0, tile), :] = ref[f, x, pl.ds(ny - tile, tile), :]
-            edge[1, x, pl.ds(tile, high_count), :] = highs[pl.ds(each * x + high_row, high_count), :]
-
-
-def receive(got, halos):
+def receive(ax, bx, by, ay):
     i, j, even_x, even_y = position()
-    ax, bx, by, ay = got
-    low_x, high_x, low_y, high_y = halos
     first_x, last_x, first_y, last_y = sides(i, j)
-    unpack(ax, bx, low_x, high_x, even_x, first_x, last_x)
-    unpack(ay, by, low_y, high_y, even_y, first_y, last_y)
-    return even_x, even_y, last_x, last_y
+    odd_x, odd_y = jnp.logical_not(even_x), jnp.logical_not(even_y)
+    low_x, high_x = Halo(ax, bx, odd_x, first_x), Halo(ax, bx, even_x, last_x)
+    low_y, high_y = Halo(ay, by, odd_y, first_y), Halo(ay, by, even_y, last_y)
+    return low_x, high_x, low_y, high_y
+
+
+def inverse(value, outside):
+    return jnp.where(outside, 0.0, 1.0 / jnp.where(outside, 1.0, value))
 
 
 def first_pack(stress, density, shear, ax, bx, by, ay, ends, tiles, sems):
@@ -238,13 +238,14 @@
         copy.wait()
 
 
-def velocity_terms(stress, low_x, high_x, edges, last_xz=None):
+def velocity_terms(stress, halos=(None,) * 4, last_xz=None, below_xz=None):
+    low_x, high_x, low_y, high_y = halos
     xx = Field(stress, 0, (low_x, 5), (high_x, 2))
-    yy = Field(stress, 1, edge=edges.at[2] if edges is not None else None)
+    yy = Field(stress, 1, low_y=(low_y, 4), high_y=(high_y, 2))
     zz = Field(stress, 2)
-    xy = Field(stress, 3, (low_x, 2), (high_x, 0), edges.at[0] if edges is not None else None)
-    xz = Field(stress, 4, (low_x, 4), (high_x, 1), last=last_xz)
-    yz = Field(stress, 5, edge=edges.at[1] if edges is not None else None)
+    xy = Field(stress, 3, (low_x, 2), (high_x, 0), (low_y, 1), (high_y, 0))
+    xz = Field(stress, 4, (low_x, 4), (high_x, 1), last=last_xz, below=below_xz)
+    yz = Field(stress, 5, low_y=(low_y, 3), high_y=(high_y, 1))
     return ((xx, 0), (xy, -1), (xz, -1)), ((xy, -1), (yy, 0), (yz, -1)), ((xz, -1), (yz, -1), (zz, 0))
 
 
@@ -255,7 +256,7 @@
         velocity, stress, buoys, shear, ax, bx, out, factor_low = refs
     nx, ny = stress.shape[1], stress.shape[2]
     lane = lanes()
-    terms = velocity_terms(stress, None, None, None)
+    terms = velocity_terms(stress)
     if step == 1:
         i, j, even_x, _ = position()
         for t in range(ny // tile):
@@ -297,38 +298,41 @@
 
 def velocity_edges(step, *refs):
     if step == 0:
-        (velocity, stress, buoy, buoys, ends, part, ax, bx, by, ay, out, buoys_end, pax, pbx, pby, pay,
-         low_x, high_x, low_y, high_y, edges, edge_b) = refs
-        last_xz = None
+        (velocity, stress, buoy, buoys, ends, part, ax, bx, by, ay, out, buoys_end, pax, pbx, pby, pay) = refs
+        last_xz = below_xz = None
     else:
         (velocity, stress, buoys, buoys_end, shear_end, factor_low, part, ax, bx, by, ay,
-         out, last_xz, pax, pbx, pby, pay, low_x, high_x, low_y, high_y, edges) = refs
+         out, last_xz, pax, pbx, pby, pay) = refs
+
+        def below_xz(t):
+            rows = pl.ds(tile * t, tile)
+            return factor_low[rows, :] * velocity[2, 1, rows, :]
+
     nx, ny = stress.shape[1], stress.shape[2]
-    even_x, even_y, last_x, last_y = receive((ax, bx, by, ay), (low_x, high_x, low_y, high_y))
-    fill_edges(stress, 3, edges.at[0], low_y, high_y, 0, 2, 0, 1)
-    fill_edges(stress, 5, edges.at[1], low_y, high_y, 2, 2, 1, 1)
-    fill_edges(stress, 1, edges.at[2], low_y, high_y, 4, 1, 2, 2)
-    terms = velocity_terms(stress, low_x, high_x, edges, last_xz)
+    i, j, even_x, even_y = position()
+    _, last_x, _, last_y = sides(i, j)
+    halos = receive(ax, bx, by, ay)
+    _, high_x, _, high_y = halos
+    terms = velocity_terms(stress, halos, last_xz, below_xz)
     lane = lanes()
     if step == 1:
         for t in range(ny // tile):
-            rows, source = pl.ds(tile * t, tile), pl.ds(4 * ny + tile * t, tile)
-            last_xz[rows, :] = stress[4, nx - 1, rows, :] - far * shear_end[1, rows, :] * high_x[source, :]
-            below = pl.ds(3 * ny + tile * t, tile)
-            low_x[below, :] = low_x[below, :] + factor_low[rows, :] * velocity[2, 1, rows, :]
+            rows = pl.ds(tile * t, tile)
+            further = high_x.load(4 * ny + tile * t, tile)
+            last_xz[rows, :] = stress[4, nx - 1, rows, :] - far * shear_end[1, rows, :] * further
     if step == 0:
         half = 0.5 * time_step
         for t in range(ny // tile):
             rows = pl.ds(tile * t, tile)
-            above = jnp.where(last_x, 0.0, 1.0 / jnp.where(last_x, 1.0, high_x[pl.ds(4 * ny + tile * t, tile), :]))
+            above = inverse(high_x.load(4 * ny + tile * t, tile), last_x)
             buoys_end[rows, :] = half * (buoy[0, nx - 1, rows, :] + above)
         rows = pl.ds(ny - tile, tile)
+        place = lax.broadcasted_iota(jnp.int32, (tile, 128), 0)
         for x in range(nx):
             here = buoy[0, x, rows, :]
-            row = high_y[pl.ds(high_y.shape[0] // nx * x + 4, 1), :]
-            edge_b[pl.ds(0, tile), :] = here
-            edge_b[pl.ds(tile, 1), :] = jnp.where(last_y, 0.0, 1.0 / jnp.where(last_y, 1.0, row))
-            buoys_end[pl.ds(ny + tile * x, tile), :] = half * (here + edge_b[pl.ds(1, tile), :])
+            row = inverse(high_y.load(high_y.rows // nx * x + 4, 1), last_y)
+            next_y = jnp.where(place == tile - 1, row, pltpu.roll(here, tile - 1, 0))
+            buoys_end[pl.ds(ny + tile * x, tile), :] = half * (here + next_y)
     for x in range(nx):
         for t in range(ny // tile):
             rows = pl.ds(tile * t, tile)
@@ -364,8 +368,7 @@
     def down(package):
         put_planes(planes_down)(package)
         if step == 0:
-            row = high_y[pl.ds(5, 1), :]
-            package[pl.ds(5 * ny, 1), :] = jnp.where(last_y, 0.0, 1.0 / jnp.where(last_y, 1.0, row))
+            package[pl.ds(5 * ny, 1), :] = inverse(high_y.load(5, 1), last_y)
 
     Pack(pax, pbx, even_x).put(put_planes(planes_up), down)
     Pack(pay, pby, even_y).put(
@@ -374,10 +377,11 @@
     )
 
 
-def stress_fields(velocity, low_x, high_x, edges):
-    vx = Field(velocity, 0, (low_x, 2), (high_x, 0), edges.at[1] if edges is not None else None)
-    vy = Field(velocity, 1, (low_x, 3), (high_x, 1), edges.at[0] if edges is not None else None)
-    vz = Field(velocity, 2, (low_x, 4), (high_x, 3), edges.at[2] if edges is not None else None)
+def stress_fields(velocity, halos=(None,) * 4):
+    low_x, high_x, low_y, high_y = halos
+    vx = Field(velocity, 0, (low_x, 2), (high_x, 0), (low_y, 2), (high_y, 1))
+    vy = Field(velocity, 1, (low_x, 3), (high_x, 1), (low_y, 1), (high_y, 0))
+    vz = Field(velocity, 2, (low_x, 4), (high_x, 3), (low_y, 3), (high_y, 3))
     return vx, vy, vz
 
 
@@ -395,7 +399,7 @@
         velocity, stress, lam, shear, shears, out, final_velocity, sem = refs
     nx, ny = stress.shape[1], stress.shape[2]
     lane = lanes()
-    vx, vy, vz = stress_fields(velocity, None, None, None)
+    vx, vy, vz = stress_fields(velocity)
     if step == 1:
         copy = pltpu.make_async_copy(velocity, final_velocity, sem)
         copy.start()
@@ -463,22 +467,21 @@
 def stress_edges(step, *refs):
     if step == 0:
         (velocity, stress, lam, shear, shears, part, ax, bx, by, ay,
-         out, shear_end, pax, pbx, pby, pay, low_x, high_x, low_y, high_y, edges, above) = refs
+         out, shear_end, pax, pbx, pby, pay, above) = refs
     else:
         (velocity, stress, lam, shear, shears, shear_end, last_xz, part, ax, bx, by, ay,
-         final_stress, low_x, high_x, low_y, high_y, edges, out, sems) = refs
+         final_stress, out, sems) = refs
     nx, ny = stress.shape[1], stress.shape[2]
-    even_x, even_y, last_x, _ = receive((ax, bx, by, ay), (low_x, high_x, low_y, high_y))
-    fill_edges(velocity, 1, edges.at[0], low_y, high_y, 0, 2, 0, 1)
-    fill_edges(velocity, 0, edges.at[1], low_y, high_y, 2, 1, 1, 2)
-    fill_edges(velocity, 2, edges.at[2], low_y, high_y, 3, 1, 3, 2)
-    vx, vy, vz = stress_fields(velocity, low_x, high_x, edges)
+    i, j, even_x, even_y = position()
+    _, last_x, _, _ = sides(i, j)
+    halos = receive(ax, bx, by, ay)
+    high_x = halos[1]
+    vx, vy, vz = stress_fields(velocity, halos)
     lane = lanes()
     if step == 0:
         for t in range(ny // tile):
-            value = jnp.where(last_x, 1.0, high_x[pl.ds(4 * ny + tile * t, tile), :])
-            above[pl.ds(tile * t, tile), :] = jnp.where(last_x, 0.0, 1.0 / value)
-        above[pl.ds(ny, 1), :] = high_x[pl.ds(5 * ny, 1), :]
+            above[pl.ds(tile * t, tile), :] = inverse(high_x.load(4 * ny + tile * t, tile), last_x)
+        above[pl.ds(ny, 1), :] = high_x.load(5 * ny, 1)
         for t in range(ny // tile):
             rows = pl.ds(tile * t, tile)
             value = above[rows, :]
@@ -578,9 +581,6 @@
     def exchange(arrays):
         return [lax.ppermute(array, AXES, route) for array, route in zip(arrays, routes)]
 
-    def halos(*rows):
-        return packages(*rows) + [(3, 2, nx, 2 * tile, nz)]
-
     def kernel(function, step):
         return lambda *refs: function(step, *refs)
 
@@ -594,7 +594,7 @@
     part, buoy, buoys = call(
         kernel(velocity_inside, 0), [three, one, three], [], (stress, density), 60 * cells)
     new_velocity, buoys_end, *packed = call(
-        kernel(velocity_edges, 0), [three, (ny + nx * tile, nz)] + packages(*second), halos(*first) + [(2 * tile, nz)],
+        kernel(velocity_edges, 0), [three, (ny + nx * tile, nz)] + packages(*second), [],
         (velocity, stress, buoy, buoys, ends, part, *got), 20 * cells)
     rows_y = got[2:]
     got = exchange(packed)
@@ -602,7 +602,7 @@
         kernel(stress_inside, 0), [stress.shape, three], [(nx, ny, nz), (nx, 2 * tile, nz)],
         (new_velocity, stress, lame_lambda, lame_mu, *rows_y), 80 * cells)
     new_stress, shear_end, *packed = call(
-        kernel(stress_edges, 0), [stress.shape, (2, ny, nz)] + packages(*later), halos(*second) + [(ny + tile, nz)],
+        kernel(stress_edges, 0), [stress.shape, (2, ny, nz)] + packages(*later), [(ny + tile, nz)],
         (new_velocity, stress, lame_lambda, lame_mu, shears, part, *got), 20 * cells)
     velocity, stress = new_velocity, new_stress
     planes_x = got[:2]
@@ -610,14 +610,14 @@
     part, factor_low = call(
         kernel(velocity_inside, 1), [three, (ny, nz)], [], (velocity, stress, buoys, lame_mu, *planes_x), 60 * cells)
     velocity, last_xz, *packed = call(
-        kernel(velocity_edges, 1), [three, (ny, nz)] + packages(*later), halos(*later),
+        kernel(velocity_edges, 1), [three, (ny, nz)] + packages(*later), [],
         (velocity, stress, buoys, buoys_end, shear_end, factor_low, part, *got), 20 * cells)
     got = exchange(packed)
     part, final_velocity = call(
         kernel(stress_inside, 1), [stress.shape, three], [dma],
         (velocity, stress, lame_lambda, lame_mu, shears), 80 * cells, hbm_out=(1,))
     (final_stress,) = call(
-        kernel(stress_edges, 1), [stress.shape], halos(*later) + [stress.shape, dma((nx,))],
+        kernel(stress_edges, 1), [stress.shape], [stress.shape, dma((nx,))],
         (velocity, stress, lame_lambda, lame_mu, shears, shear_end, last_xz, part, *got), 20 * cells, hbm_out=(0,))
     return (final_velocity, final_stress)
 

time: 29.5 us -> 29.5 us (level)
  no operation moved by 1% of the time
where the time goes in v7:
time: 29.5 us; the launch traced here: 29.3 us
  starting transfers between devices  16.8 us (57%)
  waiting for transfers between devices  6.46 us (22%)
  Pallas kernels  5.24 us (18%)
  between operations  0.77 us (3%)
    ppermute x16, starting transfers between devices, exchange(): lax.ppermute(array, AXES, route)  16.8 us
    ppermute x16, waiting for transfers between devices, exchange(): lax.ppermute(array, AXES, route)  6.46 us
    pallas_call x9, Pallas kernels, call(): pl.pallas_call(kernel, out_shape=[(pltpu.HBM if n in hbm_out else pltpu.V...  5.24 us
  transfers between devices with their start and end apart: 16, of which 4 were waited for; matrix products, arithmetic and copies ran while one was open for 0% of the time, Pallas kernels for 8%

profile of v7, /device:TPU:0, one launch (start us, length us, event | category | flops | bytes accessed | tf_op | source)
XLA Modules:
  0.0 29.3 jit_solution(9707412210996634403)
XLA Ops:
  0.6 0.0 copy-start
  0.6 0.0 copy-start.3
  0.6 1.1 %shard_map.68 = (f32[5,32,128]{2,1,0:T(8,128)S(1)}, f32[5,32,128]{2,1,0:T(8,128)S(1)}, f32[48,128]{1,0:T(8,128)S(1)}, f32[48,128]{1,0:T(8,128)S(1)}, f32[2,32,128]{2,1,0:T(8,128)S(1)}) custom-call(f32[6,8,32,128]{3,2,1,0:T(8,128)} %refs_1_.3, f32[8,32,128]{2,1,0:T(8,128)} %refs_1_, f32[8,32,128]{2,1,0:T(8,128)} %refs_3_.4), custom_call_target="tpu_custom_call" | custom-call | flops 32768 | bytes 2097152 | tf_op jit(solution)/shard_map/pallas_call | solution.py:560
  1.8 0.0 copy-start.4
  1.8 3.0 %collective-permute-start = (f32[160,128]{1,0:T(8,128)S(1)}, f32[160,128]{1,0:T(8,128)S(1)}, u32[]{:S(2)}, u32[]{:S(2)}) collective-permute-start(f32[160,128]{1,0:T(8,128)S(1)} %bitcast.3), channel_id=1, source_target_pairs={{0,8},{1,9},{2,10},{3,11},{4,12},{5,13},{6,14},{7,15},{8,0},{9,1},... | collective-permute-start | bytes 245768 | tf_op jit(solution)/shard_map/ppermute | solution.py:582
  4.8 0.0 collective-permute-start.1
  4.8 1.5 %collective-permute-start.2 = (f32[48,128]{1,0:T(8,128)S(1)}, f32[48,128]{1,0:T(8,128)S(1)}, u32[]{:S(2)}, u32[]{:S(2)}) collective-permute-start(f32[48,128]{1,0:T(8,128)S(1)} %get-tuple-element.56), channel_id=1, source_target_pairs={{0,16},{1,2},{2,1},{3,4},{4,3},{5,6},{6,5},{7,23},{8,24},{9,10},{1... | collective-permute-start | bytes 73736 | tf_op jit(solution)/shard_map/ppermute | solution.py:582
  6.4 0.2 collective-permute-start.3
  6.5 0.0 copy-done.3
  6.5 0.4 %shard_map.69 = (f32[3,8,32,128]{3,2,1,0:T(8,128)S(1)}, f32[1,8,32,128]{3,2,1,0:T(8,128)S(1)}, f32[3,8,32,128]{3,2,1,0:T(8,128)S(1)}) custom-call(f32[6,8,32,128]{3,2,1,0:T(8,128)S(1)} %copy-done, f32[8,32,128]{2,1,0:T(8,128)S(1)} %copy-done.3), custom_call_target="tpu_custom_call" | custom-call | flops 1966080 | bytes 2097152 | tf_op jit(solution)/shard_map/pallas_call | solution.py:560
  6.9 1.7 %collective-permute-done.2.refs_8_.refs_4_ = f32[48,128]{1,0:T(8,128)S(1)} collective-permute-done((f32[48,128]{1,0:T(8,128)S(1)}, f32[48,128]{1,0:T(8,128)S(1)}, u32[]{:S(2)}, u32[]{:S(2)}) %collective-permute-start.2) | collective-permute-done | bytes 24608 | tf_op jit(solution)/shard_map/ppermute | solution.py:582
  8.6 0.0 collective-permute-done.3.refs_9_.refs_5_
  8.6 0.0 collective-permute-done.refs_6_
  8.7 0.0 collective-permute-done.1.refs_7_
  8.7 0.0 copy-start.1
  8.7 0.0 copy-start.2
  8.7 0.3 shard_map.70
  9.0 3.4 %collective-permute-start.4 = (f32[168,128]{1,0:T(8,128)S(1)}, f32[168,128]{1,0:T(8,128)S(1)}, u32[]{:S(2)}, u32[]{:S(2)}) collective-permute-start(f32[168,128]{1,0:T(8,128)S(1)} %get-tuple-element.63), channel_id=1, source_target_pairs={{0,8},{1,9},{2,10},{3,11},{4,12},{5,13},{6,14},{7,15},{8,0},{9,1},... | collective-permute-start | bytes 258056 | tf_op jit(solution)/shard_map/ppermute | solution.py:582
  12.4 0.0 collective-permute-start.5
  12.4 1.5 %collective-permute-start.6 = (f32[40,128]{1,0:T(8,128)S(1)}, f32[40,128]{1,0:T(8,128)S(1)}, u32[]{:S(2)}, u32[]{:S(2)}) collective-permute-start(f32[40,128]{1,0:T(8,128)S(1)} %get-tuple-element.65), channel_id=1, source_target_pairs={{0,16},{1,2},{2,1},{3,4},{4,3},{5,6},{6,5},{7,23},{8,24},{9,10},{1... | collective-permute-start | bytes 61448 | tf_op jit(solution)/shard_map/ppermute | solution.py:582
  13.9 0.0 collective-permute-start.7
  13.9 0.0 copy-done.2
  13.9 0.5 %shard_map.71 = (f32[6,8,32,128]{3,2,1,0:T(8,128)S(1)}, f32[3,8,32,128]{3,2,1,0:T(8,128)S(1)}) custom-call(f32[3,8,32,128]{3,2,1,0:T(8,128)S(1)} %get-tuple-element.58.refs_0_, f32[6,8,32,128]{3,2,1,0:T(8,128)S(1)} %copy-done, f32[8,32,128]{2,1,0:T(8,128)S(1)} %copy-done.2, f32[8,32,128]{2,1,0:T(8,128)S(1)} %copy-done.1, ...), custom_call_target="tpu_custom_call" | custom-call | flops 2621440 | bytes 2097152 | tf_op jit(solution)/shard_map/pallas_call | solution.py:560
  14.4 1.8 %collective-permute-done.6.refs_8_ = f32[40,128]{1,0:T(8,128)S(1)} collective-permute-done((f32[40,128]{1,0:T(8,128)S(1)}, f32[40,128]{1,0:T(8,128)S(1)}, u32[]{:S(2)}, u32[]{:S(2)}) %collective-permute-start.6) | collective-permute-done | bytes 20512 | tf_op jit(solution)/shard_map/ppermute | solution.py:582
  16.1 0.0 collective-permute-done.7.refs_9_
  16.1 0.0 collective-permute-done.4.refs_6_.refs_4_
  16.1 0.0 collective-permute-done.5.refs_7_.refs_5_
  16.2 0.3 %shard_map.72 = (f32[6,8,32,128]{3,2,1,0:T(8,128)S(1)}, f32[2,32,128]{2,1,0:T(8,128)S(1)}, f32[160,128]{1,0:T(8,128)S(1)}, f32[160,128]{1,0:T(8,128)S(1)}, f32[40,128]{1,0:T(8,128)S(1)}, /*index=5*/f32[40,128]{1,0:T(8,128)S(1)}) custom-call(f32[3,8,32,128]{3,2,1,0:T(8,128)S(1)} %get-tuple-element.58.refs_0_, f32[6,8,32,128]{3,2,1,0:T(8,128)S(1)} %copy-done, ...), custom_call_target="tpu_custom_call" | custom-call | flops 655360 | bytes 2097152 | tf_op jit(solution)/shard_map/pallas_call | solution.py:560
  16.5 2.0 %collective-permute-start.8 = (f32[160,128]{1,0:T(8,128)S(1)}, f32[160,128]{1,0:T(8,128)S(1)}, u32[]{:S(2)}, u32[]{:S(2)}) collective-permute-start(f32[160,128]{1,0:T(8,128)S(1)} %get-tuple-element.72), channel_id=1, source_target_pairs={{0,8},{1,9},{2,10},{3,11},{4,12},{5,13},{6,14},{7,15},{8,0},{9,1},... | collective-permute-start | bytes 245768 | tf_op jit(solution)/shard_map/ppermute | solution.py:582
  18.4 0.0 collective-permute-start.9
  18.4 1.6 %collective-permute-start.10 = (f32[40,128]{1,0:T(8,128)S(1)}, f32[40,128]{1,0:T(8,128)S(1)}, u32[]{:S(2)}, u32[]{:S(2)}) collective-permute-start(f32[40,128]{1,0:T(8,128)S(1)} %get-tuple-element.74), channel_id=1, source_target_pairs={{0,16},{1,2},{2,1},{3,4},{4,3},{5,6},{6,5},{7,23},{8,24},{9,10},{1... | collective-permute-start | bytes 61448 | tf_op jit(solution)/shard_map/ppermute | solution.py:582
  20.0 0.0 collective-permute-start.11
  20.0 0.4 %shard_map.73 = (f32[3,8,32,128]{3,2,1,0:T(8,128)S(1)}, f32[32,128]{1,0:T(8,128)S(1)}) custom-call(f32[3,8,32,128]{3,2,1,0:T(8,128)S(1)} %get-tuple-element.58.refs_0_, f32[6,8,32,128]{3,2,1,0:T(8,128)S(1)} %get-tuple-element.67.refs_1_, f32[3,8,32,128]{3,2,1,0:T(8,128)S(1)} %get-tuple-element.51.refs_3_.refs_2_, f32[8,32,128]{2,1,0:T(8,128)S(1)} %copy-done.1, ...), custom_call_target="tpu_custom_call" | custom-call | flops 1966080 | bytes 2097152 | tf_op jit(solution)/shard_map/pallas_call | solution.py:560
  20.4 1.8 %collective-permute-done.10.refs_9_ = f32[40,128]{1,0:T(8,128)S(1)} collective-permute-done((f32[40,128]{1,0:T(8,128)S(1)}, f32[40,128]{1,0:T(8,128)S(1)}, u32[]{:S(2)}, u32[]{:S(2)}) %collective-permute-start.10) | collective-permute-done | bytes 20512 | tf_op jit(solution)/shard_map/ppermute | solution.py:582
  22.2 0.0 collective-permute-done.11.refs_10_
  22.2 0.0 collective-permute-done.8.refs_7_
  22.2 0.0 collective-permute-done.9.refs_8_
  22.2 0.3 shard_map.74
  22.5 2.0 %collective-permute-start.12 = (f32[160,128]{1,0:T(8,128)S(1)}, f32[160,128]{1,0:T(8,128)S(1)}, u32[]{:S(2)}, u32[]{:S(2)}) collective-permute-start(f32[160,128]{1,0:T(8,128)S(1)} %get-tuple-element.80), channel_id=1, source_target_pairs={{0,8},{1,9},{2,10},{3,11},{4,12},{5,13},{6,14},{7,15},{8,0},{9,1},... | collective-permute-start | bytes 245768 | tf_op jit(solution)/shard_map/ppermute | solution.py:582
  24.5 0.0 collective-permute-start.13
  24.5 1.6 %collective-permute-start.14 = (f32[40,128]{1,0:T(8,128)S(1)}, f32[40,128]{1,0:T(8,128)S(1)}, u32[]{:S(2)}, u32[]{:S(2)}) collective-permute-start(f32[40,128]{1,0:T(8,128)S(1)} %get-tuple-element.82), channel_id=1, source_target_pairs={{0,16},{1,2},{2,1},{3,4},{4,3},{5,6},{6,5},{7,23},{8,24},{9,10},{1... | collective-permute-start | bytes 61448 | tf_op jit(solution)/shard_map/ppermute | solution.py:582
  26.0 0.0 collective-permute-start.15
  26.0 1.1 %shard_map.75 = (f32[6,8,32,128]{3,2,1,0:T(8,128)S(1)}, f32[3,8,32,128]{3,2,1,0:T(8,128)}) custom-call(f32[3,8,32,128]{3,2,1,0:T(8,128)S(1)} %get-tuple-element.76.refs_0_, f32[6,8,32,128]{3,2,1,0:T(8,128)S(1)} %get-tuple-element.67.refs_1_, f32[8,32,128]{2,1,0:T(8,128)S(1)} %copy-done.2, f32[8,32,128]{2,1,0:T(8,128)S(1)} %copy-done.1, ...), custom_call_target="tpu_custom_call" | custom-call | flops 2621440 | bytes 2097152 | tf_op jit(solution)/shard_map/pallas_call | solution.py:560
  27.1 1.2 %collective-permute-done.14.refs_10_ = f32[40,128]{1,0:T(8,128)S(1)} collective-permute-done((f32[40,128]{1,0:T(8,128)S(1)}, f32[40,128]{1,0:T(8,128)S(1)}, u32[]{:S(2)}, u32[]{:S(2)}) %collective-permute-start.14) | collective-permute-done | bytes 20512 | tf_op jit(solution)/shard_map/ppermute | solution.py:582
  28.3 0.0 collective-permute-done.15.refs_11_
  28.3 0.0 collective-permute-done.12.refs_8_
  28.3 0.0 collective-permute-done.13.refs_9_
  28.3 1.0 %shard_map.76 = f32[6,8,32,128]{3,2,1,0:T(8,128)} custom-call(f32[3,8,32,128]{3,2,1,0:T(8,128)S(1)} %get-tuple-element.76.refs_0_, f32[6,8,32,128]{3,2,1,0:T(8,128)S(1)} %get-tuple-element.67.refs_1_, f32[8,32,128]{2,1,0:T(8,128)S(1)} %copy-done.2, f32[8,32,128]{2,1,0:T(8,128)S(1)} %copy-done.1, f32[3,8,32,128]{3,2,1,0:T(8,128)S(1)} %get-tuple-element.61.refs_4_, ...), custom_call_target="tpu_custom_call" | custom-call | flops 655360 | bytes 2097152 | tf_op jit(solution)/shard_map/pallas_call | solution.py:560
  (3 shorter events, 0.0 us)
Async XLA Ops:
  0.6 5.9 %copy-start = (f32[6,8,32,128]{3,2,1,0:T(8,128)S(1)}, f32[6,8,32,128]{3,2,1,0:T(8,128)}, u32[]{:S(2)}) copy-start(f32[6,8,32,128]{3,2,1,0:T(8,128)} %refs_1_.3) | copy-start | bytes 2359300
  0.6 5.9 %copy-start.3 = (f32[8,32,128]{2,1,0:T(8,128)S(1)}, f32[8,32,128]{2,1,0:T(8,128)}, u32[]{:S(2)}) copy-start(f32[8,32,128]{2,1,0:T(8,128)} %refs_1_) | copy-start | bytes 393220
  1.8 6.9 %copy-start.4 = (f32[3,8,32,128]{3,2,1,0:T(8,128)S(1)}, f32[3,8,32,128]{3,2,1,0:T(8,128)}, u32[]{:S(2)}) copy-start(f32[3,8,32,128]{3,2,1,0:T(8,128)} %refs_0_.1) | copy-start | bytes 1179652
  1.8 6.8 %collective-permute-start = (f32[160,128]{1,0:T(8,128)S(1)}, f32[160,128]{1,0:T(8,128)S(1)}, u32[]{:S(2)}, u32[]{:S(2)}) collective-permute-start(f32[160,128]{1,0:T(8,128)S(1)} %bitcast.3), channel_id=1, source_target_pairs={{0,8},{1,9},{2,10},{3,11},{4,12},{5,13},{6,14},{7,15},{8,0},{9,1},... | collective-permute-start | bytes 245768 | tf_op jit(solution)/shard_map/ppermute | solution.py:582
  4.8 3.8 %collective-permute-start.1 = (f32[160,128]{1,0:T(8,128)S(1)}, f32[160,128]{1,0:T(8,128)S(1)}, u32[]{:S(2)}, u32[]{:S(2)}) collective-permute-start(f32[160,128]{1,0:T(8,128)S(1)} %bitcast.2), channel_id=1, source_target_pairs={{0,1},{1,0},{2,3},{3,2},{4,5},{5,4},{6,7},{7,6},{8,16},{9,17},{10,... | collective-permute-start | bytes 245768 | tf_op jit(solution)/shard_map/ppermute | solution.py:582
  4.8 3.8 %collective-permute-start.2 = (f32[48,128]{1,0:T(8,128)S(1)}, f32[48,128]{1,0:T(8,128)S(1)}, u32[]{:S(2)}, u32[]{:S(2)}) collective-permute-start(f32[48,128]{1,0:T(8,128)S(1)} %get-tuple-element.56), channel_id=1, source_target_pairs={{0,16},{1,2},{2,1},{3,4},{4,3},{5,6},{6,5},{7,23},{8,24},{9,10},{1... | collective-permute-start | bytes 73736 | tf_op jit(solution)/shard_map/ppermute | solution.py:582
  6.4 2.3 %collective-permute-start.3 = (f32[48,128]{1,0:T(8,128)S(1)}, f32[48,128]{1,0:T(8,128)S(1)}, u32[]{:S(2)}, u32[]{:S(2)}) collective-permute-start(f32[48,128]{1,0:T(8,128)S(1)} %get-tuple-element.57), channel_id=1, source_target_pairs={{0,1},{1,0},{2,3},{3,2},{4,5},{5,4},{6,7},{7,6},{8,9},{9,8},{10,11... | collective-permute-start | bytes 73736 | tf_op jit(solution)/shard_map/ppermute | solution.py:582
  8.7 5.2 %copy-start.1 = (f32[8,32,128]{2,1,0:T(8,128)S(1)}, f32[8,32,128]{2,1,0:T(8,128)}, u32[]{:S(2)}) copy-start(f32[8,32,128]{2,1,0:T(8,128)} %refs_3_.4) | copy-start | bytes 393220
  8.7 5.2 %copy-start.2 = (f32[8,32,128]{2,1,0:T(8,128)S(1)}, f32[8,32,128]{2,1,0:T(8,128)}, u32[]{:S(2)}) copy-start(f32[8,32,128]{2,1,0:T(8,128)} %refs_2_.3) | copy-start | bytes 393220
  9.0 7.2 %collective-permute-start.4 = (f32[168,128]{1,0:T(8,128)S(1)}, f32[168,128]{1,0:T(8,128)S(1)}, u32[]{:S(2)}, u32[]{:S(2)}) collective-permute-start(f32[168,128]{1,0:T(8,128)S(1)} %get-tuple-element.63), channel_id=1, source_target_pairs={{0,8},{1,9},{2,10},{3,11},{4,12},{5,13},{6,14},{7,15},{8,0},{9,1},... | collective-permute-start | bytes 258056 | tf_op jit(solution)/shard_map/ppermute | solution.py:582
  12.4 3.8 %collective-permute-start.5 = (f32[168,128]{1,0:T(8,128)S(1)}, f32[168,128]{1,0:T(8,128)S(1)}, u32[]{:S(2)}, u32[]{:S(2)}) collective-permute-start(f32[168,128]{1,0:T(8,128)S(1)} %get-tuple-element.64), channel_id=1, source_target_pairs={{0,1},{1,0},{2,3},{3,2},{4,5},{5,4},{6,7},{7,6},{8,16},{9,17},{10,... | collective-permute-start | bytes 258056 | tf_op jit(solution)/shard_map/ppermute | solution.py:582
  12.4 3.8 %collective-permute-start.6 = (f32[40,128]{1,0:T(8,128)S(1)}, f32[40,128]{1,0:T(8,128)S(1)}, u32[]{:S(2)}, u32[]{:S(2)}) collective-permute-start(f32[40,128]{1,0:T(8,128)S(1)} %get-tuple-element.65), channel_id=1, source_target_pairs={{0,16},{1,2},{2,1},{3,4},{4,3},{5,6},{6,5},{7,23},{8,24},{9,10},{1... | collective-permute-start | bytes 61448 | tf_op jit(solution)/shard_map/ppermute | solution.py:582
  13.9 2.2 %collective-permute-start.7 = (f32[40,128]{1,0:T(8,128)S(1)}, f32[40,128]{1,0:T(8,128)S(1)}, u32[]{:S(2)}, u32[]{:S(2)}) collective-permute-start(f32[40,128]{1,0:T(8,128)S(1)} %get-tuple-element.66), channel_id=1, source_target_pairs={{0,1},{1,0},{2,3},{3,2},{4,5},{5,4},{6,7},{7,6},{8,9},{9,8},{10,11... | collective-permute-start | bytes 61448 | tf_op jit(solution)/shard_map/ppermute | solution.py:582
  16.5 5.8 %collective-permute-start.8 = (f32[160,128]{1,0:T(8,128)S(1)}, f32[160,128]{1,0:T(8,128)S(1)}, u32[]{:S(2)}, u32[]{:S(2)}) collective-permute-start(f32[160,128]{1,0:T(8,128)S(1)} %get-tuple-element.72), channel_id=1, source_target_pairs={{0,8},{1,9},{2,10},{3,11},{4,12},{5,13},{6,14},{7,15},{8,0},{9,1},... | collective-permute-start | bytes 245768 | tf_op jit(solution)/shard_map/ppermute | solution.py:582
  18.4 3.8 %collective-permute-start.9 = (f32[160,128]{1,0:T(8,128)S(1)}, f32[160,128]{1,0:T(8,128)S(1)}, u32[]{:S(2)}, u32[]{:S(2)}) collective-permute-start(f32[160,128]{1,0:T(8,128)S(1)} %get-tuple-element.73), channel_id=1, source_target_pairs={{0,1},{1,0},{2,3},{3,2},{4,5},{5,4},{6,7},{7,6},{8,16},{9,17},{10,... | collective-permute-start | bytes 245768 | tf_op jit(solution)/shard_map/ppermute | solution.py:582
  18.4 3.8 %collective-permute-start.10 = (f32[40,128]{1,0:T(8,128)S(1)}, f32[40,128]{1,0:T(8,128)S(1)}, u32[]{:S(2)}, u32[]{:S(2)}) collective-permute-start(f32[40,128]{1,0:T(8,128)S(1)} %get-tuple-element.74), channel_id=1, source_target_pairs={{0,16},{1,2},{2,1},{3,4},{4,3},{5,6},{6,5},{7,23},{8,24},{9,10},{1... | collective-permute-start | bytes 61448 | tf_op jit(solution)/shard_map/ppermute | solution.py:582
  20.0 2.2 %collective-permute-start.11 = (f32[40,128]{1,0:T(8,128)S(1)}, f32[40,128]{1,0:T(8,128)S(1)}, u32[]{:S(2)}, u32[]{:S(2)}) collective-permute-start(f32[40,128]{1,0:T(8,128)S(1)} %get-tuple-element.75), channel_id=1, source_target_pairs={{0,1},{1,0},{2,3},{3,2},{4,5},{5,4},{6,7},{7,6},{8,9},{9,8},{10,11... | collective-permute-start | bytes 61448 | tf_op jit(solution)/shard_map/ppermute | solution.py:582
  22.5 5.8 %collective-permute-start.12 = (f32[160,128]{1,0:T(8,128)S(1)}, f32[160,128]{1,0:T(8,128)S(1)}, u32[]{:S(2)}, u32[]{:S(2)}) collective-permute-start(f32[160,128]{1,0:T(8,128)S(1)} %get-tuple-element.80), channel_id=1, source_target_pairs={{0,8},{1,9},{2,10},{3,11},{4,12},{5,13},{6,14},{7,15},{8,0},{9,1},... | collective-permute-start | bytes 245768 | tf_op jit(solution)/shard_map/ppermute | solution.py:582
  24.5 3.8 %collective-permute-start.13 = (f32[160,128]{1,0:T(8,128)S(1)}, f32[160,128]{1,0:T(8,128)S(1)}, u32[]{:S(2)}, u32[]{:S(2)}) collective-permute-start(f32[160,128]{1,0:T(8,128)S(1)} %get-tuple-element.81), channel_id=1, source_target_pairs={{0,1},{1,0},{2,3},{3,2},{4,5},{5,4},{6,7},{7,6},{8,16},{9,17},{10,... | collective-permute-start | bytes 245768 | tf_op jit(solution)/shard_map/ppermute | solution.py:582
  24.5 3.8 %collective-permute-start.14 = (f32[40,128]{1,0:T(8,128)S(1)}, f32[40,128]{1,0:T(8,128)S(1)}, u32[]{:S(2)}, u32[]{:S(2)}) collective-permute-start(f32[40,128]{1,0:T(8,128)S(1)} %get-tuple-element.82), channel_id=1, source_target_pairs={{0,16},{1,2},{2,1},{3,4},{4,3},{5,6},{6,5},{7,23},{8,24},{9,10},{1... | collective-permute-start | bytes 61448 | tf_op jit(solution)/shard_map/ppermute | solution.py:582
  26.0 2.2 %collective-permute-start.15 = (f32[40,128]{1,0:T(8,128)S(1)}, f32[40,128]{1,0:T(8,128)S(1)}, u32[]{:S(2)}, u32[]{:S(2)}) collective-permute-start(f32[40,128]{1,0:T(8,128)S(1)} %get-tuple-element.83), channel_id=1, source_target_pairs={{0,1},{1,0},{2,3},{3,2},{4,5},{5,4},{6,7},{7,6},{8,9},{9,8},{10,11... | collective-permute-start | bytes 61448 | tf_op jit(solution)/shard_map/ppermute | solution.py:582

commit v8 on v7

--- a/solution.py
+++ b/solution.py
@@ -298,7 +298,7 @@
 
 def velocity_edges(step, *refs):
     if step == 0:
-        (velocity, stress, buoy, buoys, ends, part, ax, bx, by, ay, out, buoys_end, pax, pbx, pby, pay) = refs
+        (velocity, stress, buoy, buoys, ends, part, ax, bx, by, ay, out, buoys_end, pby, pay, pax, pbx) = refs
         last_xz = below_xz = None
     else:
         (velocity, stress, buoys, buoys_end, shear_end, factor_low, part, ax, bx, by, ay,
@@ -594,8 +594,10 @@
     part, buoy, buoys = call(
         kernel(velocity_inside, 0), [three, one, three], [], (stress, density), 60 * cells)
     new_velocity, buoys_end, *packed = call(
-        kernel(velocity_edges, 0), [three, (ny + nx * tile, nz)] + packages(*second), [],
+        kernel(velocity_edges, 0),
+        [three, (ny + nx * tile, nz)] + packages(*second)[2:] + packages(*second)[:2], [],
         (velocity, stress, buoy, buoys, ends, part, *got), 20 * cells)
+    packed = packed[2:] + packed[:2]
     rows_y = got[2:]
     got = exchange(packed)
     part, shears = call(

time: 29.5 us -> 29.5 us (level)
  no operation moved by 1% of the time
where the time goes in v8:
time: 29.5 us; the launch traced here: 29.3 us
  starting transfers between devices  16.8 us (57%)
  waiting for transfers between devices  6.46 us (22%)
  Pallas kernels  5.24 us (18%)
  between operations  0.77 us (3%)
    ppermute x16, starting transfers between devices, exchange(): lax.ppermute(array, AXES, route)  16.8 us
    ppermute x16, waiting for transfers between devices, exchange(): lax.ppermute(array, AXES, route)  6.46 us
    pallas_call x9, Pallas kernels, call(): pl.pallas_call(kernel, out_shape=[(pltpu.HBM if n in hbm_out else pltpu.V...  5.24 us
  transfers between devices with their start and end apart: 16, of which 4 were waited for; matrix products, arithmetic and copies ran while one was open for 0% of the time, Pallas kernels for 8%

profile of v8, /device:TPU:0, one launch (start us, length us, event | category | flops | bytes accessed | tf_op | source)
XLA Modules:
  0.0 29.3 jit_solution(16399503170880328853)
XLA Ops:
  0.6 0.0 copy-start
  0.6 0.0 copy-start.3
  0.6 1.1 %shard_map.68 = (f32[5,32,128]{2,1,0:T(8,128)S(1)}, f32[5,32,128]{2,1,0:T(8,128)S(1)}, f32[48,128]{1,0:T(8,128)S(1)}, f32[48,128]{1,0:T(8,128)S(1)}, f32[2,32,128]{2,1,0:T(8,128)S(1)}) custom-call(f32[6,8,32,128]{3,2,1,0:T(8,128)} %refs_1_.3, f32[8,32,128]{2,1,0:T(8,128)} %refs_1_, f32[8,32,128]{2,1,0:T(8,128)} %refs_3_.4), custom_call_target="tpu_custom_call" | custom-call | flops 32768 | bytes 2097152 | tf_op jit(solution)/shard_map/pallas_call | solution.py:560
  1.8 0.0 copy-start.4
  1.8 3.0 %collective-permute-start = (f32[160,128]{1,0:T(8,128)S(1)}, f32[160,128]{1,0:T(8,128)S(1)}, u32[]{:S(2)}, u32[]{:S(2)}) collective-permute-start(f32[160,128]{1,0:T(8,128)S(1)} %bitcast.3), channel_id=1, source_target_pairs={{0,8},{1,9},{2,10},{3,11},{4,12},{5,13},{6,14},{7,15},{8,0},{9,1},... | collective-permute-start | bytes 245768 | tf_op jit(solution)/shard_map/ppermute | solution.py:582
  4.8 0.0 collective-permute-start.1
  4.8 1.5 %collective-permute-start.2 = (f32[48,128]{1,0:T(8,128)S(1)}, f32[48,128]{1,0:T(8,128)S(1)}, u32[]{:S(2)}, u32[]{:S(2)}) collective-permute-start(f32[48,128]{1,0:T(8,128)S(1)} %get-tuple-element.56), channel_id=1, source_target_pairs={{0,16},{1,2},{2,1},{3,4},{4,3},{5,6},{6,5},{7,23},{8,24},{9,10},{1... | collective-permute-start | bytes 73736 | tf_op jit(solution)/shard_map/ppermute | solution.py:582
  6.4 0.2 collective-permute-start.3
  6.5 0.0 copy-done.3
  6.5 0.4 %shard_map.69 = (f32[3,8,32,128]{3,2,1,0:T(8,128)S(1)}, f32[1,8,32,128]{3,2,1,0:T(8,128)S(1)}, f32[3,8,32,128]{3,2,1,0:T(8,128)S(1)}) custom-call(f32[6,8,32,128]{3,2,1,0:T(8,128)S(1)} %copy-done, f32[8,32,128]{2,1,0:T(8,128)S(1)} %copy-done.3), custom_call_target="tpu_custom_call" | custom-call | flops 1966080 | bytes 2097152 | tf_op jit(solution)/shard_map/pallas_call | solution.py:560
  6.9 1.7 %collective-permute-done.2.refs_8_.refs_4_ = f32[48,128]{1,0:T(8,128)S(1)} collective-permute-done((f32[48,128]{1,0:T(8,128)S(1)}, f32[48,128]{1,0:T(8,128)S(1)}, u32[]{:S(2)}, u32[]{:S(2)}) %collective-permute-start.2) | collective-permute-done | bytes 24608 | tf_op jit(solution)/shard_map/ppermute | solution.py:582
  8.6 0.0 collective-permute-done.3.refs_9_.refs_5_
  8.6 0.0 collective-permute-done.refs_6_
  8.7 0.0 collective-permute-done.1.refs_7_
  8.7 0.0 copy-start.1
  8.7 0.0 copy-start.2
  8.7 0.3 shard_map.70
  9.0 3.4 %collective-permute-start.4 = (f32[168,128]{1,0:T(8,128)S(1)}, f32[168,128]{1,0:T(8,128)S(1)}, u32[]{:S(2)}, u32[]{:S(2)}) collective-permute-start(f32[168,128]{1,0:T(8,128)S(1)} %get-tuple-element.63), channel_id=1, source_target_pairs={{0,8},{1,9},{2,10},{3,11},{4,12},{5,13},{6,14},{7,15},{8,0},{9,1},... | collective-permute-start | bytes 258056 | tf_op jit(solution)/shard_map/ppermute | solution.py:582
  12.4 0.0 collective-permute-start.5
  12.4 1.5 %collective-permute-start.6 = (f32[40,128]{1,0:T(8,128)S(1)}, f32[40,128]{1,0:T(8,128)S(1)}, u32[]{:S(2)}, u32[]{:S(2)}) collective-permute-start(f32[40,128]{1,0:T(8,128)S(1)} %get-tuple-element.65), channel_id=1, source_target_pairs={{0,16},{1,2},{2,1},{3,4},{4,3},{5,6},{6,5},{7,23},{8,24},{9,10},{1... | collective-permute-start | bytes 61448 | tf_op jit(solution)/shard_map/ppermute | solution.py:582
  13.9 0.0 collective-permute-start.7
  13.9 0.0 copy-done.2
  13.9 0.5 %shard_map.71 = (f32[6,8,32,128]{3,2,1,0:T(8,128)S(1)}, f32[3,8,32,128]{3,2,1,0:T(8,128)S(1)}) custom-call(f32[3,8,32,128]{3,2,1,0:T(8,128)S(1)} %get-tuple-element.58.refs_0_, f32[6,8,32,128]{3,2,1,0:T(8,128)S(1)} %copy-done, f32[8,32,128]{2,1,0:T(8,128)S(1)} %copy-done.2, f32[8,32,128]{2,1,0:T(8,128)S(1)} %copy-done.1, ...), custom_call_target="tpu_custom_call" | custom-call | flops 2621440 | bytes 2097152 | tf_op jit(solution)/shard_map/pallas_call | solution.py:560
  14.4 1.8 %collective-permute-done.6.refs_8_ = f32[40,128]{1,0:T(8,128)S(1)} collective-permute-done((f32[40,128]{1,0:T(8,128)S(1)}, f32[40,128]{1,0:T(8,128)S(1)}, u32[]{:S(2)}, u32[]{:S(2)}) %collective-permute-start.6) | collective-permute-done | bytes 20512 | tf_op jit(solution)/shard_map/ppermute | solution.py:582
  16.1 0.0 collective-permute-done.7.refs_9_
  16.1 0.0 collective-permute-done.4.refs_6_.refs_4_
  16.1 0.0 collective-permute-done.5.refs_7_.refs_5_
  16.2 0.3 %shard_map.72 = (f32[6,8,32,128]{3,2,1,0:T(8,128)S(1)}, f32[2,32,128]{2,1,0:T(8,128)S(1)}, f32[160,128]{1,0:T(8,128)S(1)}, f32[160,128]{1,0:T(8,128)S(1)}, f32[40,128]{1,0:T(8,128)S(1)}, /*index=5*/f32[40,128]{1,0:T(8,128)S(1)}) custom-call(f32[3,8,32,128]{3,2,1,0:T(8,128)S(1)} %get-tuple-element.58.refs_0_, f32[6,8,32,128]{3,2,1,0:T(8,128)S(1)} %copy-done, ...), custom_call_target="tpu_custom_call" | custom-call | flops 655360 | bytes 2097152 | tf_op jit(solution)/shard_map/pallas_call | solution.py:560
  16.5 2.0 %collective-permute-start.8 = (f32[160,128]{1,0:T(8,128)S(1)}, f32[160,128]{1,0:T(8,128)S(1)}, u32[]{:S(2)}, u32[]{:S(2)}) collective-permute-start(f32[160,128]{1,0:T(8,128)S(1)} %get-tuple-element.72), channel_id=1, source_target_pairs={{0,8},{1,9},{2,10},{3,11},{4,12},{5,13},{6,14},{7,15},{8,0},{9,1},... | collective-permute-start | bytes 245768 | tf_op jit(solution)/shard_map/ppermute | solution.py:582
  18.4 0.0 collective-permute-start.9
  18.4 1.6 %collective-permute-start.10 = (f32[40,128]{1,0:T(8,128)S(1)}, f32[40,128]{1,0:T(8,128)S(1)}, u32[]{:S(2)}, u32[]{:S(2)}) collective-permute-start(f32[40,128]{1,0:T(8,128)S(1)} %get-tuple-element.74), channel_id=1, source_target_pairs={{0,16},{1,2},{2,1},{3,4},{4,3},{5,6},{6,5},{7,23},{8,24},{9,10},{1... | collective-permute-start | bytes 61448 | tf_op jit(solution)/shard_map/ppermute | solution.py:582
  20.0 0.0 collective-permute-start.11
  20.0 0.4 %shard_map.73 = (f32[3,8,32,128]{3,2,1,0:T(8,128)S(1)}, f32[32,128]{1,0:T(8,128)S(1)}) custom-call(f32[3,8,32,128]{3,2,1,0:T(8,128)S(1)} %get-tuple-element.58.refs_0_, f32[6,8,32,128]{3,2,1,0:T(8,128)S(1)} %get-tuple-element.67.refs_1_, f32[3,8,32,128]{3,2,1,0:T(8,128)S(1)} %get-tuple-element.51.refs_3_.refs_2_, f32[8,32,128]{2,1,0:T(8,128)S(1)} %copy-done.1, ...), custom_call_target="tpu_custom_call" | custom-call | flops 1966080 | bytes 2097152 | tf_op jit(solution)/shard_map/pallas_call | solution.py:560
  20.4 1.8 %collective-permute-done.10.refs_9_ = f32[40,128]{1,0:T(8,128)S(1)} collective-permute-done((f32[40,128]{1,0:T(8,128)S(1)}, f32[40,128]{1,0:T(8,128)S(1)}, u32[]{:S(2)}, u32[]{:S(2)}) %collective-permute-start.10) | collective-permute-done | bytes 20512 | tf_op jit(solution)/shard_map/ppermute | solution.py:582
  22.2 0.0 collective-permute-done.11.refs_10_
  22.2 0.0 collective-permute-done.8.refs_7_
  22.2 0.0 collective-permute-done.9.refs_8_
  22.2 0.3 shard_map.74
  22.5 2.0 %collective-permute-start.12 = (f32[160,128]{1,0:T(8,128)S(1)}, f32[160,128]{1,0:T(8,128)S(1)}, u32[]{:S(2)}, u32[]{:S(2)}) collective-permute-start(f32[160,128]{1,0:T(8,128)S(1)} %get-tuple-element.80), channel_id=1, source_target_pairs={{0,8},{1,9},{2,10},{3,11},{4,12},{5,13},{6,14},{7,15},{8,0},{9,1},... | collective-permute-start | bytes 245768 | tf_op jit(solution)/shard_map/ppermute | solution.py:582
  24.5 0.0 collective-permute-start.13
  24.5 1.6 %collective-permute-start.14 = (f32[40,128]{1,0:T(8,128)S(1)}, f32[40,128]{1,0:T(8,128)S(1)}, u32[]{:S(2)}, u32[]{:S(2)}) collective-permute-start(f32[40,128]{1,0:T(8,128)S(1)} %get-tuple-element.82), channel_id=1, source_target_pairs={{0,16},{1,2},{2,1},{3,4},{4,3},{5,6},{6,5},{7,23},{8,24},{9,10},{1... | collective-permute-start | bytes 61448 | tf_op jit(solution)/shard_map/ppermute | solution.py:582
  26.0 0.0 collective-permute-start.15
  26.0 1.1 %shard_map.75 = (f32[6,8,32,128]{3,2,1,0:T(8,128)S(1)}, f32[3,8,32,128]{3,2,1,0:T(8,128)}) custom-call(f32[3,8,32,128]{3,2,1,0:T(8,128)S(1)} %get-tuple-element.76.refs_0_, f32[6,8,32,128]{3,2,1,0:T(8,128)S(1)} %get-tuple-element.67.refs_1_, f32[8,32,128]{2,1,0:T(8,128)S(1)} %copy-done.2, f32[8,32,128]{2,1,0:T(8,128)S(1)} %copy-done.1, ...), custom_call_target="tpu_custom_call" | custom-call | flops 2621440 | bytes 2097152 | tf_op jit(solution)/shard_map/pallas_call | solution.py:560
  27.1 1.2 %collective-permute-done.14.refs_10_ = f32[40,128]{1,0:T(8,128)S(1)} collective-permute-done((f32[40,128]{1,0:T(8,128)S(1)}, f32[40,128]{1,0:T(8,128)S(1)}, u32[]{:S(2)}, u32[]{:S(2)}) %collective-permute-start.14) | collective-permute-done | bytes 20512 | tf_op jit(solution)/shard_map/ppermute | solution.py:582
  28.3 0.0 collective-permute-done.15.refs_11_
  28.3 0.0 collective-permute-done.12.refs_8_
  28.3 0.0 collective-permute-done.13.refs_9_
  28.3 1.0 %shard_map.76 = f32[6,8,32,128]{3,2,1,0:T(8,128)} custom-call(f32[3,8,32,128]{3,2,1,0:T(8,128)S(1)} %get-tuple-element.76.refs_0_, f32[6,8,32,128]{3,2,1,0:T(8,128)S(1)} %get-tuple-element.67.refs_1_, f32[8,32,128]{2,1,0:T(8,128)S(1)} %copy-done.2, f32[8,32,128]{2,1,0:T(8,128)S(1)} %copy-done.1, f32[3,8,32,128]{3,2,1,0:T(8,128)S(1)} %get-tuple-element.61.refs_4_, ...), custom_call_target="tpu_custom_call" | custom-call | flops 655360 | bytes 2097152 | tf_op jit(solution)/shard_map/pallas_call | solution.py:560
  (3 shorter events, 0.0 us)
Async XLA Ops:
  0.6 5.9 %copy-start = (f32[6,8,32,128]{3,2,1,0:T(8,128)S(1)}, f32[6,8,32,128]{3,2,1,0:T(8,128)}, u32[]{:S(2)}) copy-start(f32[6,8,32,128]{3,2,1,0:T(8,128)} %refs_1_.3) | copy-start | bytes 2359300
  0.6 5.9 %copy-start.3 = (f32[8,32,128]{2,1,0:T(8,128)S(1)}, f32[8,32,128]{2,1,0:T(8,128)}, u32[]{:S(2)}) copy-start(f32[8,32,128]{2,1,0:T(8,128)} %refs_1_) | copy-start | bytes 393220
  1.8 6.9 %copy-start.4 = (f32[3,8,32,128]{3,2,1,0:T(8,128)S(1)}, f32[3,8,32,128]{3,2,1,0:T(8,128)}, u32[]{:S(2)}) copy-start(f32[3,8,32,128]{3,2,1,0:T(8,128)} %refs_0_.1) | copy-start | bytes 1179652
  1.8 6.8 %collective-permute-start = (f32[160,128]{1,0:T(8,128)S(1)}, f32[160,128]{1,0:T(8,128)S(1)}, u32[]{:S(2)}, u32[]{:S(2)}) collective-permute-start(f32[160,128]{1,0:T(8,128)S(1)} %bitcast.3), channel_id=1, source_target_pairs={{0,8},{1,9},{2,10},{3,11},{4,12},{5,13},{6,14},{7,15},{8,0},{9,1},... | collective-permute-start | bytes 245768 | tf_op jit(solution)/shard_map/ppermute | solution.py:582
  4.8 3.8 %collective-permute-start.1 = (f32[160,128]{1,0:T(8,128)S(1)}, f32[160,128]{1,0:T(8,128)S(1)}, u32[]{:S(2)}, u32[]{:S(2)}) collective-permute-start(f32[160,128]{1,0:T(8,128)S(1)} %bitcast.2), channel_id=1, source_target_pairs={{0,1},{1,0},{2,3},{3,2},{4,5},{5,4},{6,7},{7,6},{8,16},{9,17},{10,... | collective-permute-start | bytes 245768 | tf_op jit(solution)/shard_map/ppermute | solution.py:582
  4.8 3.8 %collective-permute-start.2 = (f32[48,128]{1,0:T(8,128)S(1)}, f32[48,128]{1,0:T(8,128)S(1)}, u32[]{:S(2)}, u32[]{:S(2)}) collective-permute-start(f32[48,128]{1,0:T(8,128)S(1)} %get-tuple-element.56), channel_id=1, source_target_pairs={{0,16},{1,2},{2,1},{3,4},{4,3},{5,6},{6,5},{7,23},{8,24},{9,10},{1... | collective-permute-start | bytes 73736 | tf_op jit(solution)/shard_map/ppermute | solution.py:582
  6.4 2.3 %collective-permute-start.3 = (f32[48,128]{1,0:T(8,128)S(1)}, f32[48,128]{1,0:T(8,128)S(1)}, u32[]{:S(2)}, u32[]{:S(2)}) collective-permute-start(f32[48,128]{1,0:T(8,128)S(1)} %get-tuple-element.57), channel_id=1, source_target_pairs={{0,1},{1,0},{2,3},{3,2},{4,5},{5,4},{6,7},{7,6},{8,9},{9,8},{10,11... | collective-permute-start | bytes 73736 | tf_op jit(solution)/shard_map/ppermute | solution.py:582
  8.7 5.2 %copy-start.1 = (f32[8,32,128]{2,1,0:T(8,128)S(1)}, f32[8,32,128]{2,1,0:T(8,128)}, u32[]{:S(2)}) copy-start(f32[8,32,128]{2,1,0:T(8,128)} %refs_3_.4) | copy-start | bytes 393220
  8.7 5.2 %copy-start.2 = (f32[8,32,128]{2,1,0:T(8,128)S(1)}, f32[8,32,128]{2,1,0:T(8,128)}, u32[]{:S(2)}) copy-start(f32[8,32,128]{2,1,0:T(8,128)} %refs_2_.3) | copy-start | bytes 393220
  9.0 7.2 %collective-permute-start.4 = (f32[168,128]{1,0:T(8,128)S(1)}, f32[168,128]{1,0:T(8,128)S(1)}, u32[]{:S(2)}, u32[]{:S(2)}) collective-permute-start(f32[168,128]{1,0:T(8,128)S(1)} %get-tuple-element.63), channel_id=1, source_target_pairs={{0,8},{1,9},{2,10},{3,11},{4,12},{5,13},{6,14},{7,15},{8,0},{9,1},... | collective-permute-start | bytes 258056 | tf_op jit(solution)/shard_map/ppermute | solution.py:582
  12.4 3.8 %collective-permute-start.5 = (f32[168,128]{1,0:T(8,128)S(1)}, f32[168,128]{1,0:T(8,128)S(1)}, u32[]{:S(2)}, u32[]{:S(2)}) collective-permute-start(f32[168,128]{1,0:T(8,128)S(1)} %get-tuple-element.64), channel_id=1, source_target_pairs={{0,1},{1,0},{2,3},{3,2},{4,5},{5,4},{6,7},{7,6},{8,16},{9,17},{10,... | collective-permute-start | bytes 258056 | tf_op jit(solution)/shard_map/ppermute | solution.py:582
  12.4 3.8 %collective-permute-start.6 = (f32[40,128]{1,0:T(8,128)S(1)}, f32[40,128]{1,0:T(8,128)S(1)}, u32[]{:S(2)}, u32[]{:S(2)}) collective-permute-start(f32[40,128]{1,0:T(8,128)S(1)} %get-tuple-element.65), channel_id=1, source_target_pairs={{0,16},{1,2},{2,1},{3,4},{4,3},{5,6},{6,5},{7,23},{8,24},{9,10},{1... | collective-permute-start | bytes 61448 | tf_op jit(solution)/shard_map/ppermute | solution.py:582
  13.9 2.2 %collective-permute-start.7 = (f32[40,128]{1,0:T(8,128)S(1)}, f32[40,128]{1,0:T(8,128)S(1)}, u32[]{:S(2)}, u32[]{:S(2)}) collective-permute-start(f32[40,128]{1,0:T(8,128)S(1)} %get-tuple-element.66), channel_id=1, source_target_pairs={{0,1},{1,0},{2,3},{3,2},{4,5},{5,4},{6,7},{7,6},{8,9},{9,8},{10,11... | collective-permute-start | bytes 61448 | tf_op jit(solution)/shard_map/ppermute | solution.py:582
  16.5 5.8 %collective-permute-start.8 = (f32[160,128]{1,0:T(8,128)S(1)}, f32[160,128]{1,0:T(8,128)S(1)}, u32[]{:S(2)}, u32[]{:S(2)}) collective-permute-start(f32[160,128]{1,0:T(8,128)S(1)} %get-tuple-element.72), channel_id=1, source_target_pairs={{0,8},{1,9},{2,10},{3,11},{4,12},{5,13},{6,14},{7,15},{8,0},{9,1},... | collective-permute-start | bytes 245768 | tf_op jit(solution)/shard_map/ppermute | solution.py:582
  18.4 3.8 %collective-permute-start.9 = (f32[160,128]{1,0:T(8,128)S(1)}, f32[160,128]{1,0:T(8,128)S(1)}, u32[]{:S(2)}, u32[]{:S(2)}) collective-permute-start(f32[160,128]{1,0:T(8,128)S(1)} %get-tuple-element.73), channel_id=1, source_target_pairs={{0,1},{1,0},{2,3},{3,2},{4,5},{5,4},{6,7},{7,6},{8,16},{9,17},{10,... | collective-permute-start | bytes 245768 | tf_op jit(solution)/shard_map/ppermute | solution.py:582
  18.4 3.8 %collective-permute-start.10 = (f32[40,128]{1,0:T(8,128)S(1)}, f32[40,128]{1,0:T(8,128)S(1)}, u32[]{:S(2)}, u32[]{:S(2)}) collective-permute-start(f32[40,128]{1,0:T(8,128)S(1)} %get-tuple-element.74), channel_id=1, source_target_pairs={{0,16},{1,2},{2,1},{3,4},{4,3},{5,6},{6,5},{7,23},{8,24},{9,10},{1... | collective-permute-start | bytes 61448 | tf_op jit(solution)/shard_map/ppermute | solution.py:582
  20.0 2.2 %collective-permute-start.11 = (f32[40,128]{1,0:T(8,128)S(1)}, f32[40,128]{1,0:T(8,128)S(1)}, u32[]{:S(2)}, u32[]{:S(2)}) collective-permute-start(f32[40,128]{1,0:T(8,128)S(1)} %get-tuple-element.75), channel_id=1, source_target_pairs={{0,1},{1,0},{2,3},{3,2},{4,5},{5,4},{6,7},{7,6},{8,9},{9,8},{10,11... | collective-permute-start | bytes 61448 | tf_op jit(solution)/shard_map/ppermute | solution.py:582
  22.5 5.8 %collective-permute-start.12 = (f32[160,128]{1,0:T(8,128)S(1)}, f32[160,128]{1,0:T(8,128)S(1)}, u32[]{:S(2)}, u32[]{:S(2)}) collective-permute-start(f32[160,128]{1,0:T(8,128)S(1)} %get-tuple-element.80), channel_id=1, source_target_pairs={{0,8},{1,9},{2,10},{3,11},{4,12},{5,13},{6,14},{7,15},{8,0},{9,1},... | collective-permute-start | bytes 245768 | tf_op jit(solution)/shard_map/ppermute | solution.py:582
  24.5 3.8 %collective-permute-start.13 = (f32[160,128]{1,0:T(8,128)S(1)}, f32[160,128]{1,0:T(8,128)S(1)}, u32[]{:S(2)}, u32[]{:S(2)}) collective-permute-start(f32[160,128]{1,0:T(8,128)S(1)} %get-tuple-element.81), channel_id=1, source_target_pairs={{0,1},{1,0},{2,3},{3,2},{4,5},{5,4},{6,7},{7,6},{8,16},{9,17},{10,... | collective-permute-start | bytes 245768 | tf_op jit(solution)/shard_map/ppermute | solution.py:582
  24.5 3.8 %collective-permute-start.14 = (f32[40,128]{1,0:T(8,128)S(1)}, f32[40,128]{1,0:T(8,128)S(1)}, u32[]{:S(2)}, u32[]{:S(2)}) collective-permute-start(f32[40,128]{1,0:T(8,128)S(1)} %get-tuple-element.82), channel_id=1, source_target_pairs={{0,16},{1,2},{2,1},{3,4},{4,3},{5,6},{6,5},{7,23},{8,24},{9,10},{1... | collective-permute-start | bytes 61448 | tf_op jit(solution)/shard_map/ppermute | solution.py:582
  26.0 2.2 %collective-permute-start.15 = (f32[40,128]{1,0:T(8,128)S(1)}, f32[40,128]{1,0:T(8,128)S(1)}, u32[]{:S(2)}, u32[]{:S(2)}) collective-permute-start(f32[40,128]{1,0:T(8,128)S(1)} %get-tuple-element.83), channel_id=1, source_target_pairs={{0,1},{1,0},{2,3},{3,2},{4,5},{5,4},{6,7},{7,6},{8,9},{9,8},{10,11... | collective-permute-start | bytes 61448 | tf_op jit(solution)/shard_map/ppermute | solution.py:582

commit v9 on v8

--- a/solution.py
+++ b/solution.py
@@ -302,7 +302,7 @@
         last_xz = below_xz = None
     else:
         (velocity, stress, buoys, buoys_end, shear_end, factor_low, part, ax, bx, by, ay,
-         out, last_xz, pax, pbx, pby, pay) = refs
+         out, last_xz, pby, pay, pax, pbx) = refs
 
         def below_xz(t):
             rows = pl.ds(tile * t, tile)
@@ -612,8 +612,9 @@
     part, factor_low = call(
         kernel(velocity_inside, 1), [three, (ny, nz)], [], (velocity, stress, buoys, lame_mu, *planes_x), 60 * cells)
     velocity, last_xz, *packed = call(
-        kernel(velocity_edges, 1), [three, (ny, nz)] + packages(*later), [],
+        kernel(velocity_edges, 1), [three, (ny, nz)] + packages(*later)[2:] + packages(*later)[:2], [],
         (velocity, stress, buoys, buoys_end, shear_end, factor_low, part, *got), 20 * cells)
+    packed = packed[2:] + packed[:2]
     got = exchange(packed)
     part, final_velocity = call(
         kernel(stress_inside, 1), [stress.shape, three], [dma],

time: 29.5 us -> 29.5 us (level)
  no operation moved by 1% of the time
where the time goes in v9:
time: 29.5 us; the launch traced here: 29.3 us
  starting transfers between devices  16.8 us (57%)
  waiting for transfers between devices  6.46 us (22%)
  Pallas kernels  5.24 us (18%)
  between operations  0.77 us (3%)
    ppermute x16, starting transfers between devices, exchange(): lax.ppermute(array, AXES, route)  16.8 us
    ppermute x16, waiting for transfers between devices, exchange(): lax.ppermute(array, AXES, route)  6.46 us
    pallas_call x9, Pallas kernels, call(): pl.pallas_call(kernel, out_shape=[(pltpu.HBM if n in hbm_out else pltpu.V...  5.24 us
  transfers between devices with their start and end apart: 16, of which 4 were waited for; matrix products, arithmetic and copies ran while one was open for 0% of the time, Pallas kernels for 8%

profile of v9, /device:TPU:0, one launch (start us, length us, event | category | flops | bytes accessed | tf_op | source)
XLA Modules:
  0.0 29.3 jit_solution(13667323361273907602)
XLA Ops:
  0.6 0.0 copy-start
  0.6 0.0 copy-start.3
  0.6 1.1 %shard_map.68 = (f32[5,32,128]{2,1,0:T(8,128)S(1)}, f32[5,32,128]{2,1,0:T(8,128)S(1)}, f32[48,128]{1,0:T(8,128)S(1)}, f32[48,128]{1,0:T(8,128)S(1)}, f32[2,32,128]{2,1,0:T(8,128)S(1)}) custom-call(f32[6,8,32,128]{3,2,1,0:T(8,128)} %refs_1_.3, f32[8,32,128]{2,1,0:T(8,128)} %refs_1_, f32[8,32,128]{2,1,0:T(8,128)} %refs_3_.4), custom_call_target="tpu_custom_call" | custom-call | flops 32768 | bytes 2097152 | tf_op jit(solution)/shard_map/pallas_call | solution.py:560
  1.8 0.0 copy-start.4
  1.8 3.0 %collective-permute-start = (f32[160,128]{1,0:T(8,128)S(1)}, f32[160,128]{1,0:T(8,128)S(1)}, u32[]{:S(2)}, u32[]{:S(2)}) collective-permute-start(f32[160,128]{1,0:T(8,128)S(1)} %bitcast.3), channel_id=1, source_target_pairs={{0,8},{1,9},{2,10},{3,11},{4,12},{5,13},{6,14},{7,15},{8,0},{9,1},... | collective-permute-start | bytes 245768 | tf_op jit(solution)/shard_map/ppermute | solution.py:582
  4.8 0.0 collective-permute-start.1
  4.8 1.5 %collective-permute-start.2 = (f32[48,128]{1,0:T(8,128)S(1)}, f32[48,128]{1,0:T(8,128)S(1)}, u32[]{:S(2)}, u32[]{:S(2)}) collective-permute-start(f32[48,128]{1,0:T(8,128)S(1)} %get-tuple-element.56), channel_id=1, source_target_pairs={{0,16},{1,2},{2,1},{3,4},{4,3},{5,6},{6,5},{7,23},{8,24},{9,10},{1... | collective-permute-start | bytes 73736 | tf_op jit(solution)/shard_map/ppermute | solution.py:582
  6.4 0.2 collective-permute-start.3
  6.5 0.0 copy-done.3
  6.5 0.4 %shard_map.69 = (f32[3,8,32,128]{3,2,1,0:T(8,128)S(1)}, f32[1,8,32,128]{3,2,1,0:T(8,128)S(1)}, f32[3,8,32,128]{3,2,1,0:T(8,128)S(1)}) custom-call(f32[6,8,32,128]{3,2,1,0:T(8,128)S(1)} %copy-done, f32[8,32,128]{2,1,0:T(8,128)S(1)} %copy-done.3), custom_call_target="tpu_custom_call" | custom-call | flops 1966080 | bytes 2097152 | tf_op jit(solution)/shard_map/pallas_call | solution.py:560
  6.9 1.7 %collective-permute-done.2.refs_8_.refs_4_ = f32[48,128]{1,0:T(8,128)S(1)} collective-permute-done((f32[48,128]{1,0:T(8,128)S(1)}, f32[48,128]{1,0:T(8,128)S(1)}, u32[]{:S(2)}, u32[]{:S(2)}) %collective-permute-start.2) | collective-permute-done | bytes 24608 | tf_op jit(solution)/shard_map/ppermute | solution.py:582
  8.6 0.0 collective-permute-done.3.refs_9_.refs_5_
  8.6 0.0 collective-permute-done.refs_6_
  8.7 0.0 collective-permute-done.1.refs_7_
  8.7 0.0 copy-start.1
  8.7 0.0 copy-start.2
  8.7 0.3 shard_map.70
  9.0 3.4 %collective-permute-start.4 = (f32[168,128]{1,0:T(8,128)S(1)}, f32[168,128]{1,0:T(8,128)S(1)}, u32[]{:S(2)}, u32[]{:S(2)}) collective-permute-start(f32[168,128]{1,0:T(8,128)S(1)} %get-tuple-element.63), channel_id=1, source_target_pairs={{0,8},{1,9},{2,10},{3,11},{4,12},{5,13},{6,14},{7,15},{8,0},{9,1},... | collective-permute-start | bytes 258056 | tf_op jit(solution)/shard_map/ppermute | solution.py:582
  12.4 0.0 collective-permute-start.5
  12.4 1.5 %collective-permute-start.6 = (f32[40,128]{1,0:T(8,128)S(1)}, f32[40,128]{1,0:T(8,128)S(1)}, u32[]{:S(2)}, u32[]{:S(2)}) collective-permute-start(f32[40,128]{1,0:T(8,128)S(1)} %get-tuple-element.65), channel_id=1, source_target_pairs={{0,16},{1,2},{2,1},{3,4},{4,3},{5,6},{6,5},{7,23},{8,24},{9,10},{1... | collective-permute-start | bytes 61448 | tf_op jit(solution)/shard_map/ppermute | solution.py:582
  13.9 0.0 collective-permute-start.7
  13.9 0.0 copy-done.2
  13.9 0.5 %shard_map.71 = (f32[6,8,32,128]{3,2,1,0:T(8,128)S(1)}, f32[3,8,32,128]{3,2,1,0:T(8,128)S(1)}) custom-call(f32[3,8,32,128]{3,2,1,0:T(8,128)S(1)} %get-tuple-element.58.refs_0_, f32[6,8,32,128]{3,2,1,0:T(8,128)S(1)} %copy-done, f32[8,32,128]{2,1,0:T(8,128)S(1)} %copy-done.2, f32[8,32,128]{2,1,0:T(8,128)S(1)} %copy-done.1, ...), custom_call_target="tpu_custom_call" | custom-call | flops 2621440 | bytes 2097152 | tf_op jit(solution)/shard_map/pallas_call | solution.py:560
  14.4 1.8 %collective-permute-done.6.refs_8_ = f32[40,128]{1,0:T(8,128)S(1)} collective-permute-done((f32[40,128]{1,0:T(8,128)S(1)}, f32[40,128]{1,0:T(8,128)S(1)}, u32[]{:S(2)}, u32[]{:S(2)}) %collective-permute-start.6) | collective-permute-done | bytes 20512 | tf_op jit(solution)/shard_map/ppermute | solution.py:582
  16.1 0.0 collective-permute-done.7.refs_9_
  16.1 0.0 collective-permute-done.4.refs_6_.refs_4_
  16.1 0.0 collective-permute-done.5.refs_7_.refs_5_
  16.2 0.3 %shard_map.72 = (f32[6,8,32,128]{3,2,1,0:T(8,128)S(1)}, f32[2,32,128]{2,1,0:T(8,128)S(1)}, f32[160,128]{1,0:T(8,128)S(1)}, f32[160,128]{1,0:T(8,128)S(1)}, f32[40,128]{1,0:T(8,128)S(1)}, /*index=5*/f32[40,128]{1,0:T(8,128)S(1)}) custom-call(f32[3,8,32,128]{3,2,1,0:T(8,128)S(1)} %get-tuple-element.58.refs_0_, f32[6,8,32,128]{3,2,1,0:T(8,128)S(1)} %copy-done, ...), custom_call_target="tpu_custom_call" | custom-call | flops 655360 | bytes 2097152 | tf_op jit(solution)/shard_map/pallas_call | solution.py:560
  16.5 2.0 %collective-permute-start.8 = (f32[160,128]{1,0:T(8,128)S(1)}, f32[160,128]{1,0:T(8,128)S(1)}, u32[]{:S(2)}, u32[]{:S(2)}) collective-permute-start(f32[160,128]{1,0:T(8,128)S(1)} %get-tuple-element.72), channel_id=1, source_target_pairs={{0,8},{1,9},{2,10},{3,11},{4,12},{5,13},{6,14},{7,15},{8,0},{9,1},... | collective-permute-start | bytes 245768 | tf_op jit(solution)/shard_map/ppermute | solution.py:582
  18.4 0.0 collective-permute-start.9
  18.4 1.6 %collective-permute-start.10 = (f32[40,128]{1,0:T(8,128)S(1)}, f32[40,128]{1,0:T(8,128)S(1)}, u32[]{:S(2)}, u32[]{:S(2)}) collective-permute-start(f32[40,128]{1,0:T(8,128)S(1)} %get-tuple-element.74), channel_id=1, source_target_pairs={{0,16},{1,2},{2,1},{3,4},{4,3},{5,6},{6,5},{7,23},{8,24},{9,10},{1... | collective-permute-start | bytes 61448 | tf_op jit(solution)/shard_map/ppermute | solution.py:582
  20.0 0.0 collective-permute-start.11
  20.0 0.4 %shard_map.73 = (f32[3,8,32,128]{3,2,1,0:T(8,128)S(1)}, f32[32,128]{1,0:T(8,128)S(1)}) custom-call(f32[3,8,32,128]{3,2,1,0:T(8,128)S(1)} %get-tuple-element.58.refs_0_, f32[6,8,32,128]{3,2,1,0:T(8,128)S(1)} %get-tuple-element.67.refs_1_, f32[3,8,32,128]{3,2,1,0:T(8,128)S(1)} %get-tuple-element.51.refs_3_.refs_2_, f32[8,32,128]{2,1,0:T(8,128)S(1)} %copy-done.1, ...), custom_call_target="tpu_custom_call" | custom-call | flops 1966080 | bytes 2097152 | tf_op jit(solution)/shard_map/pallas_call | solution.py:560
  20.4 1.8 %collective-permute-done.10.refs_9_ = f32[40,128]{1,0:T(8,128)S(1)} collective-permute-done((f32[40,128]{1,0:T(8,128)S(1)}, f32[40,128]{1,0:T(8,128)S(1)}, u32[]{:S(2)}, u32[]{:S(2)}) %collective-permute-start.10) | collective-permute-done | bytes 20512 | tf_op jit(solution)/shard_map/ppermute | solution.py:582
  22.2 0.0 collective-permute-done.11.refs_10_
  22.2 0.0 collective-permute-done.8.refs_7_
  22.2 0.0 collective-permute-done.9.refs_8_
  22.2 0.3 shard_map.74
  22.5 2.0 %collective-permute-start.12 = (f32[160,128]{1,0:T(8,128)S(1)}, f32[160,128]{1,0:T(8,128)S(1)}, u32[]{:S(2)}, u32[]{:S(2)}) collective-permute-start(f32[160,128]{1,0:T(8,128)S(1)} %get-tuple-element.80), channel_id=1, source_target_pairs={{0,8},{1,9},{2,10},{3,11},{4,12},{5,13},{6,14},{7,15},{8,0},{9,1},... | collective-permute-start | bytes 245768 | tf_op jit(solution)/shard_map/ppermute | solution.py:582
  24.5 0.0 collective-permute-start.13
  24.5 1.6 %collective-permute-start.14 = (f32[40,128]{1,0:T(8,128)S(1)}, f32[40,128]{1,0:T(8,128)S(1)}, u32[]{:S(2)}, u32[]{:S(2)}) collective-permute-start(f32[40,128]{1,0:T(8,128)S(1)} %get-tuple-element.82), channel_id=1, source_target_pairs={{0,16},{1,2},{2,1},{3,4},{4,3},{5,6},{6,5},{7,23},{8,24},{9,10},{1... | collective-permute-start | bytes 61448 | tf_op jit(solution)/shard_map/ppermute | solution.py:582
  26.0 0.0 collective-permute-start.15
  26.0 1.1 %shard_map.75 = (f32[6,8,32,128]{3,2,1,0:T(8,128)S(1)}, f32[3,8,32,128]{3,2,1,0:T(8,128)}) custom-call(f32[3,8,32,128]{3,2,1,0:T(8,128)S(1)} %get-tuple-element.76.refs_0_, f32[6,8,32,128]{3,2,1,0:T(8,128)S(1)} %get-tuple-element.67.refs_1_, f32[8,32,128]{2,1,0:T(8,128)S(1)} %copy-done.2, f32[8,32,128]{2,1,0:T(8,128)S(1)} %copy-done.1, ...), custom_call_target="tpu_custom_call" | custom-call | flops 2621440 | bytes 2097152 | tf_op jit(solution)/shard_map/pallas_call | solution.py:560
  27.1 1.2 %collective-permute-done.14.refs_10_ = f32[40,128]{1,0:T(8,128)S(1)} collective-permute-done((f32[40,128]{1,0:T(8,128)S(1)}, f32[40,128]{1,0:T(8,128)S(1)}, u32[]{:S(2)}, u32[]{:S(2)}) %collective-permute-start.14) | collective-permute-done | bytes 20512 | tf_op jit(solution)/shard_map/ppermute | solution.py:582
  28.3 0.0 collective-permute-done.15.refs_11_
  28.3 0.0 collective-permute-done.12.refs_8_
  28.3 0.0 collective-permute-done.13.refs_9_
  28.3 1.0 %shard_map.76 = f32[6,8,32,128]{3,2,1,0:T(8,128)} custom-call(f32[3,8,32,128]{3,2,1,0:T(8,128)S(1)} %get-tuple-element.76.refs_0_, f32[6,8,32,128]{3,2,1,0:T(8,128)S(1)} %get-tuple-element.67.refs_1_, f32[8,32,128]{2,1,0:T(8,128)S(1)} %copy-done.2, f32[8,32,128]{2,1,0:T(8,128)S(1)} %copy-done.1, f32[3,8,32,128]{3,2,1,0:T(8,128)S(1)} %get-tuple-element.61.refs_4_, ...), custom_call_target="tpu_custom_call" | custom-call | flops 655360 | bytes 2097152 | tf_op jit(solution)/shard_map/pallas_call | solution.py:560
  (3 shorter events, 0.0 us)
Async XLA Ops:
  0.6 5.9 %copy-start = (f32[6,8,32,128]{3,2,1,0:T(8,128)S(1)}, f32[6,8,32,128]{3,2,1,0:T(8,128)}, u32[]{:S(2)}) copy-start(f32[6,8,32,128]{3,2,1,0:T(8,128)} %refs_1_.3) | copy-start | bytes 2359300
  0.6 5.9 %copy-start.3 = (f32[8,32,128]{2,1,0:T(8,128)S(1)}, f32[8,32,128]{2,1,0:T(8,128)}, u32[]{:S(2)}) copy-start(f32[8,32,128]{2,1,0:T(8,128)} %refs_1_) | copy-start | bytes 393220
  1.8 6.9 %copy-start.4 = (f32[3,8,32,128]{3,2,1,0:T(8,128)S(1)}, f32[3,8,32,128]{3,2,1,0:T(8,128)}, u32[]{:S(2)}) copy-start(f32[3,8,32,128]{3,2,1,0:T(8,128)} %refs_0_.1) | copy-start | bytes 1179652
  1.8 6.8 %collective-permute-start = (f32[160,128]{1,0:T(8,128)S(1)}, f32[160,128]{1,0:T(8,128)S(1)}, u32[]{:S(2)}, u32[]{:S(2)}) collective-permute-start(f32[160,128]{1,0:T(8,128)S(1)} %bitcast.3), channel_id=1, source_target_pairs={{0,8},{1,9},{2,10},{3,11},{4,12},{5,13},{6,14},{7,15},{8,0},{9,1},... | collective-permute-start | bytes 245768 | tf_op jit(solution)/shard_map/ppermute | solution.py:582
  4.8 3.8 %collective-permute-start.1 = (f32[160,128]{1,0:T(8,128)S(1)}, f32[160,128]{1,0:T(8,128)S(1)}, u32[]{:S(2)}, u32[]{:S(2)}) collective-permute-start(f32[160,128]{1,0:T(8,128)S(1)} %bitcast.2), channel_id=1, source_target_pairs={{0,1},{1,0},{2,3},{3,2},{4,5},{5,4},{6,7},{7,6},{8,16},{9,17},{10,... | collective-permute-start | bytes 245768 | tf_op jit(solution)/shard_map/ppermute | solution.py:582
  4.8 3.8 %collective-permute-start.2 = (f32[48,128]{1,0:T(8,128)S(1)}, f32[48,128]{1,0:T(8,128)S(1)}, u32[]{:S(2)}, u32[]{:S(2)}) collective-permute-start(f32[48,128]{1,0:T(8,128)S(1)} %get-tuple-element.56), channel_id=1, source_target_pairs={{0,16},{1,2},{2,1},{3,4},{4,3},{5,6},{6,5},{7,23},{8,24},{9,10},{1... | collective-permute-start | bytes 73736 | tf_op jit(solution)/shard_map/ppermute | solution.py:582
  6.4 2.3 %collective-permute-start.3 = (f32[48,128]{1,0:T(8,128)S(1)}, f32[48,128]{1,0:T(8,128)S(1)}, u32[]{:S(2)}, u32[]{:S(2)}) collective-permute-start(f32[48,128]{1,0:T(8,128)S(1)} %get-tuple-element.57), channel_id=1, source_target_pairs={{0,1},{1,0},{2,3},{3,2},{4,5},{5,4},{6,7},{7,6},{8,9},{9,8},{10,11... | collective-permute-start | bytes 73736 | tf_op jit(solution)/shard_map/ppermute | solution.py:582
  8.7 5.2 %copy-start.1 = (f32[8,32,128]{2,1,0:T(8,128)S(1)}, f32[8,32,128]{2,1,0:T(8,128)}, u32[]{:S(2)}) copy-start(f32[8,32,128]{2,1,0:T(8,128)} %refs_3_.4) | copy-start | bytes 393220
  8.7 5.2 %copy-start.2 = (f32[8,32,128]{2,1,0:T(8,128)S(1)}, f32[8,32,128]{2,1,0:T(8,128)}, u32[]{:S(2)}) copy-start(f32[8,32,128]{2,1,0:T(8,128)} %refs_2_.3) | copy-start | bytes 393220
  9.0 7.2 %collective-permute-start.4 = (f32[168,128]{1,0:T(8,128)S(1)}, f32[168,128]{1,0:T(8,128)S(1)}, u32[]{:S(2)}, u32[]{:S(2)}) collective-permute-start(f32[168,128]{1,0:T(8,128)S(1)} %get-tuple-element.63), channel_id=1, source_target_pairs={{0,8},{1,9},{2,10},{3,11},{4,12},{5,13},{6,14},{7,15},{8,0},{9,1},... | collective-permute-start | bytes 258056 | tf_op jit(solution)/shard_map/ppermute | solution.py:582
  12.4 3.8 %collective-permute-start.5 = (f32[168,128]{1,0:T(8,128)S(1)}, f32[168,128]{1,0:T(8,128)S(1)}, u32[]{:S(2)}, u32[]{:S(2)}) collective-permute-start(f32[168,128]{1,0:T(8,128)S(1)} %get-tuple-element.64), channel_id=1, source_target_pairs={{0,1},{1,0},{2,3},{3,2},{4,5},{5,4},{6,7},{7,6},{8,16},{9,17},{10,... | collective-permute-start | bytes 258056 | tf_op jit(solution)/shard_map/ppermute | solution.py:582
  12.4 3.8 %collective-permute-start.6 = (f32[40,128]{1,0:T(8,128)S(1)}, f32[40,128]{1,0:T(8,128)S(1)}, u32[]{:S(2)}, u32[]{:S(2)}) collective-permute-start(f32[40,128]{1,0:T(8,128)S(1)} %get-tuple-element.65), channel_id=1, source_target_pairs={{0,16},{1,2},{2,1},{3,4},{4,3},{5,6},{6,5},{7,23},{8,24},{9,10},{1... | collective-permute-start | bytes 61448 | tf_op jit(solution)/shard_map/ppermute | solution.py:582
  13.9 2.2 %collective-permute-start.7 = (f32[40,128]{1,0:T(8,128)S(1)}, f32[40,128]{1,0:T(8,128)S(1)}, u32[]{:S(2)}, u32[]{:S(2)}) collective-permute-start(f32[40,128]{1,0:T(8,128)S(1)} %get-tuple-element.66), channel_id=1, source_target_pairs={{0,1},{1,0},{2,3},{3,2},{4,5},{5,4},{6,7},{7,6},{8,9},{9,8},{10,11... | collective-permute-start | bytes 61448 | tf_op jit(solution)/shard_map/ppermute | solution.py:582
  16.5 5.8 %collective-permute-start.8 = (f32[160,128]{1,0:T(8,128)S(1)}, f32[160,128]{1,0:T(8,128)S(1)}, u32[]{:S(2)}, u32[]{:S(2)}) collective-permute-start(f32[160,128]{1,0:T(8,128)S(1)} %get-tuple-element.72), channel_id=1, source_target_pairs={{0,8},{1,9},{2,10},{3,11},{4,12},{5,13},{6,14},{7,15},{8,0},{9,1},... | collective-permute-start | bytes 245768 | tf_op jit(solution)/shard_map/ppermute | solution.py:582
  18.4 3.8 %collective-permute-start.9 = (f32[160,128]{1,0:T(8,128)S(1)}, f32[160,128]{1,0:T(8,128)S(1)}, u32[]{:S(2)}, u32[]{:S(2)}) collective-permute-start(f32[160,128]{1,0:T(8,128)S(1)} %get-tuple-element.73), channel_id=1, source_target_pairs={{0,1},{1,0},{2,3},{3,2},{4,5},{5,4},{6,7},{7,6},{8,16},{9,17},{10,... | collective-permute-start | bytes 245768 | tf_op jit(solution)/shard_map/ppermute | solution.py:582
  18.4 3.8 %collective-permute-start.10 = (f32[40,128]{1,0:T(8,128)S(1)}, f32[40,128]{1,0:T(8,128)S(1)}, u32[]{:S(2)}, u32[]{:S(2)}) collective-permute-start(f32[40,128]{1,0:T(8,128)S(1)} %get-tuple-element.74), channel_id=1, source_target_pairs={{0,16},{1,2},{2,1},{3,4},{4,3},{5,6},{6,5},{7,23},{8,24},{9,10},{1... | collective-permute-start | bytes 61448 | tf_op jit(solution)/shard_map/ppermute | solution.py:582
  20.0 2.2 %collective-permute-start.11 = (f32[40,128]{1,0:T(8,128)S(1)}, f32[40,128]{1,0:T(8,128)S(1)}, u32[]{:S(2)}, u32[]{:S(2)}) collective-permute-start(f32[40,128]{1,0:T(8,128)S(1)} %get-tuple-element.75), channel_id=1, source_target_pairs={{0,1},{1,0},{2,3},{3,2},{4,5},{5,4},{6,7},{7,6},{8,9},{9,8},{10,11... | collective-permute-start | bytes 61448 | tf_op jit(solution)/shard_map/ppermute | solution.py:582
  22.5 5.8 %collective-permute-start.12 = (f32[160,128]{1,0:T(8,128)S(1)}, f32[160,128]{1,0:T(8,128)S(1)}, u32[]{:S(2)}, u32[]{:S(2)}) collective-permute-start(f32[160,128]{1,0:T(8,128)S(1)} %get-tuple-element.80), channel_id=1, source_target_pairs={{0,8},{1,9},{2,10},{3,11},{4,12},{5,13},{6,14},{7,15},{8,0},{9,1},... | collective-permute-start | bytes 245768 | tf_op jit(solution)/shard_map/ppermute | solution.py:582
  24.5 3.8 %collective-permute-start.13 = (f32[160,128]{1,0:T(8,128)S(1)}, f32[160,128]{1,0:T(8,128)S(1)}, u32[]{:S(2)}, u32[]{:S(2)}) collective-permute-start(f32[160,128]{1,0:T(8,128)S(1)} %get-tuple-element.81), channel_id=1, source_target_pairs={{0,1},{1,0},{2,3},{3,2},{4,5},{5,4},{6,7},{7,6},{8,16},{9,17},{10,... | collective-permute-start | bytes 245768 | tf_op jit(solution)/shard_map/ppermute | solution.py:582
  24.5 3.8 %collective-permute-start.14 = (f32[40,128]{1,0:T(8,128)S(1)}, f32[40,128]{1,0:T(8,128)S(1)}, u32[]{:S(2)}, u32[]{:S(2)}) collective-permute-start(f32[40,128]{1,0:T(8,128)S(1)} %get-tuple-element.82), channel_id=1, source_target_pairs={{0,16},{1,2},{2,1},{3,4},{4,3},{5,6},{6,5},{7,23},{8,24},{9,10},{1... | collective-permute-start | bytes 61448 | tf_op jit(solution)/shard_map/ppermute | solution.py:582
  26.0 2.2 %collective-permute-start.15 = (f32[40,128]{1,0:T(8,128)S(1)}, f32[40,128]{1,0:T(8,128)S(1)}, u32[]{:S(2)}, u32[]{:S(2)}) collective-permute-start(f32[40,128]{1,0:T(8,128)S(1)} %get-tuple-element.83), channel_id=1, source_target_pairs={{0,1},{1,0},{2,3},{3,2},{4,5},{5,4},{6,7},{7,6},{8,9},{9,8},{10,11... | collective-permute-start | bytes 61448 | tf_op jit(solution)/shard_map/ppermute | solution.py:582
